TPU v7x, 256 devices: a whole 4x4x8 slice. The times are simulated.
256 devices in a mesh: nest: 64 (over z, y_hi, x), parent: 4 (over y_lo, core).
Axes of the slice: x: 4, y: 4 (y_hi: 2, y_lo: 2; y = y_hi * 2 + y_lo), z: 8, core: 2. Of those that a mesh axis runs over, the one named last changes fastest.
Arguments:
- nest_state: float32 [4, 64, 64, 8192], P(None, None, 'parent', 'nest'), may hold values from -6 to 6
- mixing: float32 [64, 8192], P('parent', 'nest'), may hold values from 0.02 to 0.2
- land_mask: int32 [64, 8192], P('parent', 'nest'), may hold values 0 or 1
- face_off: int32 [64, 128], P('parent', 'nest'), may hold values from 0 to 3, as said below
- parent_state: float32 [4, 64, 4, 8192], P(None, None, 'parent', 'nest'), may hold values from -6 to 6
- parent_block: int32 [4, 64], P('parent', 'nest'), may hold values from 0 to 63, as said below
- interp_idx: int32 [64, 128, 4], P('parent', 'nest'), may hold values from 0 to 127
- interp_w: float32 [64, 128, 4], P('parent', 'nest'), may hold values from 0.1 to 1
Outputs:
- nest_new: float32 [4, 64, 64, 8192], P(None, None, 'parent', 'nest')
- parent_new: float32 [4, 64, 4, 8192], P(None, None, 'parent', 'nest')
Inputs may be any that keep to these rules, and one draw needn't show every extreme that they name: `face_off`: entry 2n of a row is tile n's west face, 2n+1 its east face; d > 0 names the tile d places west (east) in the same row block, never beyond the ends; the value 3 occurs in every draw. `parent_block`: each row is a permutation of 0 to 63 that keeps every aligned group of 4 tiles, so the block lies at most 3 tiles from its nest tile; that distance is reached in every draw.
All inputs are finite; a program needn't handle non-finite values. No bound on the sum of `land_mask` on one device may be relied on, other than what follows from the above.
Results may differ from a plain program's by a relative error of at most 0.00002.
Values sent between devices are 32-bit elements; how exact they have to be, the bound alone decides.
No kernel may reach another device: no remote copies, remote signals or barrier semaphores. Data moves between devices by JAX's collectives and lax.ppermute only.
A program may use at most 128 MiB of HBM per device.

v0:
```python
import jax
import jax.numpy as jnp
from jax import lax
from jax.sharding import PartitionSpec as P

ITERS = 4
RADIUS = 3
RATIO = 4


TIME_STEP = 0.1
DIFFUSION = 1.0
CORIOLIS = 0.5
FEEDBACK = 0.5


def passed_along(value, axis, steps):
    count = lax.axis_size(axis)
    leading, last = (max(0, -steps), min(count, count - steps))
    return lax.ppermute(value, axis, [(source, source + steps) for source in range(leading, last)])


def extended(block, sides, width):
    for axis, dim in sides:
        count = lax.axis_size(axis)
        forward = [(i, i + 1) for i in range(count - 1)]
        backward = [(target, source) for source, target in forward]
        low = lax.ppermute(
            lax.slice_in_dim(block, block.shape[dim] - width, None, axis=dim), axis, forward
        )
        high = lax.ppermute(lax.slice_in_dim(block, 0, width, axis=dim), axis, backward)
        block = jnp.concatenate([low, block, high], axis=dim)
    return block


def advance(current, padded_x, padded_y, mixing, wet_mask):
    slope_x = (padded_x[..., 2:] - padded_x[..., :-2]) * 0.5
    pair_x = padded_x[..., 2:] + padded_x[..., :-2]
    slope_y = (padded_y[:, :, 2:] - padded_y[:, :, :-2]) * 0.5
    pair_y = padded_y[:, :, 2:] + padded_y[:, :, :-2]
    level_above = jnp.concatenate([current[:, :1], current[:, :-1]], axis=1)
    level_below = jnp.concatenate([current[:, 1:], current[:, -1:]], axis=1)
    zonal_flow = current[2]
    merid_flow = current[3]
    tendency = -(zonal_flow * slope_x + merid_flow * slope_y) + DIFFUSION * (
        pair_x + pair_y - 4.0 * current
    )
    updated = current + TIME_STEP * tendency + mixing * (level_above + level_below - 2.0 * current)
    blank = jnp.zeros_like(zonal_flow)
    rotation = jnp.stack(
        [blank, blank, TIME_STEP * CORIOLIS * merid_flow, -TIME_STEP * CORIOLIS * zonal_flow]
    )
    return (updated + rotation) * wet_mask


def stencil_sum(block, cells_idx, cells_w):
    return jnp.sum(block[:, :, cells_idx] * cells_w, axis=-1)


def per_device(
    nest_state, mixing, land_mask, face_off, parent_state, parent_block, interp_idx, interp_w
):
    field_count, level_count, row_count, col_count = nest_state.shape
    coarse = parent_state[:, :, 0, :]
    own_index = lax.axis_index("nest")
    offset = parent_block[0, 0] - own_index
    distances = [step for step in range(-RADIUS, RADIUS + 1) if step != 0]
    weights_total = jnp.sum(interp_w, axis=-1)
    chosen = jnp.where(offset == 0, coarse, 0.0)
    for distance in distances:
        arrived = passed_along(coarse, "nest", -distance)
        chosen = chosen + jnp.where(offset == distance, arrived, 0.0)
    weighted = stencil_sum(chosen, interp_idx, interp_w)
    open_vals = weighted / weights_total
    wet_mask = land_mask.astype(jnp.float32)
    west_off = face_off[:, 0]
    east_off = face_off[:, 1]
    edge_shape = (field_count, level_count, row_count)
    current = nest_state
    for substep in range(ITERS):
        east_edge = current[:, :, :, col_count - 1].reshape(field_count, level_count * row_count)
        west_edge = current[:, :, :, 0].reshape(field_count, level_count * row_count)
        west_ghost = jnp.where(west_off == 0, open_vals[..., 0], 0.0)
        east_ghost = jnp.where(east_off == 0, open_vals[..., 1], 0.0)
        for distance in range(1, RADIUS + 1):
            from_west = passed_along(east_edge, "nest", distance)
            from_east = passed_along(west_edge, "nest", -distance)
            west_ghost = west_ghost + jnp.where(
                west_off == distance, from_west.reshape(edge_shape), 0.0
            )
            east_ghost = east_ghost + jnp.where(
                east_off == distance, from_east.reshape(edge_shape), 0.0
            )
        padded_y = extended(current, (("parent", 2),), 1)
        padded_x = jnp.concatenate([west_ghost[..., None], current, east_ghost[..., None]], axis=-1)
        current = advance(current, padded_x, padded_y, mixing, wet_mask)
    coarse_rows = row_count // RATIO
    coarse_cols = col_count // RATIO
    block_means = jnp.mean(
        current.reshape(field_count, level_count, coarse_rows, RATIO, coarse_cols, RATIO),
        axis=(3, 5),
    )
    block_means = block_means.reshape(field_count, level_count, coarse_rows * coarse_cols)
    received = jnp.where(offset == 0, block_means, 0.0)
    for distance in distances:
        arrived = passed_along(jnp.where(offset == distance, block_means, 0.0), "nest", distance)
        received = received + arrived
    parent_new = coarse + FEEDBACK * (received - coarse)
    return (current, parent_new[:, :, None, :])


def solution(mesh):
    return jax.shard_map(
        per_device,
        mesh=mesh,
        in_specs=(
            P(None, None, "parent", "nest"),
            P("parent", "nest"),
            P("parent", "nest"),
            P("parent", "nest"),
            P(None, None, "parent", "nest"),
            P("parent", "nest"),
            P("parent", "nest", None),
            P("parent", "nest", None),
        ),
        out_specs=(P(None, None, "parent", "nest"), P(None, None, "parent", "nest")),
        check_vma=False,
    )
```

profile of v0, /device:TPU:122, one launch (start us, length us, event | category | flops | bytes accessed | tf_op | source)
XLA Modules:
  0.0 420.5 jit_solution(9604313226204099126)
XLA Ops:
  12.5 5.3 %collective-permute-start.6 = (f32[4,1024]{1,0:T(4,128)}, f32[4,1024]{1,0:T(4,128)S(1)}, u32[]{:S(2)}, u32[]{:S(2)}) collective-permute-start(f32[4,1024]{1,0:T(4,128)} %reshape_squeeze.24), channel_id=1, source_target_pairs={{4,0},{8,4},{12,8},{16,12},{20,16},{24,20},{28,24},{32,28},{36,32}... | collective-permute-start | bytes 49160 | tf_op jit(solution)/shard_map/ppermute | solution.py:20
  18.6 6.6 %collective-permute-start.11 = (f32[4,1024]{1,0:T(4,128)}, f32[4,1024]{1,0:T(4,128)S(1)}, u32[]{:S(2)}, u32[]{:S(2)}) collective-permute-start(f32[4,1024]{1,0:T(4,128)} %reshape_squeeze.25), channel_id=1, source_target_pairs={{0,12},{4,16},{8,20},{12,24},{16,28},{20,32},{24,36},{28,40},{32,4... | collective-permute-start | bytes 49160 | tf_op jit(solution)/shard_map/ppermute | solution.py:20
  35.3 4.9 %fusion.66 = (f32[4,63,16,128]{1,3,2,0:T(8,128)}, f32[4,63,16,128]{1,3,2,0:T(8,128)}) fusion(f32[4,64,16,128]{1,3,2,0:T(8,128)S(1)} %copy-done.6), kind=kLoop, calls=%fused_computation.152 | loop fusion | bytes 8257536 | tf_op jit(solution)/shard_map/slice | solution.py:42
  44.7 7.6 %collective-permute-start.4 = (f32[4,64,128]{1,0,2:T(4,128)S(1)}, f32[4,64,128]{1,0,2:T(4,128)S(1)}, u32[]{:S(2)}, u32[]{:S(2)}) collective-permute-start(f32[4,64,128]{1,0,2:T(4,128)S(1)} %bitcast.75), channel_id=1, source_target_pairs={{8,0},{12,4},{16,8},{20,12},{24,16},{28,20},{32,24},{36,28},{40,32... | collective-permute-start | bytes 393224 | tf_op jit(solution)/shard_map/ppermute | solution.py:20
  58.8 7.2 %collective-permute-start.1 = (f32[4,64,128]{1,0,2:T(4,128)S(1)}, f32[4,64,128]{1,0,2:T(4,128)S(1)}, u32[]{:S(2)}, u32[]{:S(2)}) collective-permute-start(f32[4,64,128]{1,0,2:T(4,128)S(1)} %bitcast.78), channel_id=1, source_target_pairs={{0,8},{4,12},{8,16},{12,20},{16,24},{20,28},{24,32},{28,36},{32,40... | collective-permute-start | bytes 393224 | tf_op jit(solution)/shard_map/ppermute | solution.py:20
  68.6 5.7 %collective-permute-start.5 = (f32[4,64,128]{1,0,2:T(4,128)S(1)}, f32[4,64,128]{1,0,2:T(4,128)S(1)}, u32[]{:S(2)}, u32[]{:S(2)}) collective-permute-start(f32[4,64,128]{1,0,2:T(4,128)S(1)} %bitcast.80), channel_id=1, source_target_pairs={{12,0},{16,4},{20,8},{24,12},{28,16},{32,20},{36,24},{40,28},{44,3... | collective-permute-start | bytes 393224 | tf_op jit(solution)/shard_map/ppermute | solution.py:20
  101.4 17.9 %fusion.4 = f32[4,64,16,128]{1,3,2,0:T(8,128)S(1)} fusion(f32[4,63,16,128]{1,3,2,0:T(8,128)} %get-tuple-element.53, f32[4,1,16,128]{1,3,2,0:T(8,128)} %copy.134, f32[4,1,16,128]{1,3,2,0:T(8,128)} %copy.136, f32[4,63,16,128]{1,3,2,0:T(8,128)} %get-tuple-element.52, f32[1,64,16,128]{1,3,2,0:T(8,128)S(1)} %copy-done.8, ...), kind=kLoop, calls=%fused_computation.22 | loop fusion | flops 15204352 | bytes 10797072 | tf_op jit(solution)/shard_map/mul | solution.py:53
  133.7 6.5 %collective-permute-start.16 = (f32[4,1024]{1,0:T(4,128)}, f32[4,1024]{1,0:T(4,128)}, u32[]{:S(2)}, u32[]{:S(2)}) collective-permute-start(f32[4,1024]{1,0:T(4,128)} %reshape_squeeze.26), channel_id=1, source_target_pairs={{12,0},{16,4},{20,8},{24,12},{28,16},{32,20},{36,24},{40,28},{44,3... | collective-permute-start | bytes 49160 | tf_op jit(solution)/shard_map/ppermute | solution.py:20
  143.6 8.1 %fusion.63 = (f32[4,63,16,128]{1,3,2,0:T(8,128)}, f32[4,63,16,128]{1,3,2,0:T(8,128)}) fusion(f32[4,64,16,128]{1,3,2,0:T(8,128)} %copy-done.2), kind=kLoop, calls=%fused_computation.149 | loop fusion | bytes 8257536 | tf_op jit(solution)/shard_map/slice | solution.py:42
  151.8 4.8 %fusion.64 = (f32[4,1,16,128]{1,3,2,0:T(8,128)}, f32[4,1,16,128]{1,3,2,0:T(8,128)}) fusion(f32[4,64,16,128]{1,3,2,0:T(8,128)S(1)} %copy-done.3), kind=kLoop, calls=%fused_computation.150 | loop fusion | bytes 131072 | tf_op jit(solution)/shard_map/slice | solution.py:42
  158.1 5.8 %collective-permute-start.14 = (f32[4,1024]{1,0:T(4,128)}, f32[4,1024]{1,0:T(4,128)}, u32[]{:S(2)}, u32[]{:S(2)}) collective-permute-start(f32[4,1024]{1,0:T(4,128)} %reshape_squeeze.26), channel_id=1, source_target_pairs={{4,0},{8,4},{12,8},{16,12},{20,16},{24,20},{28,24},{32,28},{36,32}... | collective-permute-start | bytes 49160 | tf_op jit(solution)/shard_map/ppermute | solution.py:20
  187.2 16.4 %fusion.9 = f32[4,64,16,128]{1,3,2,0:T(8,128)S(1)} fusion(f32[4,63,16,128]{1,3,2,0:T(8,128)} %get-tuple-element.43, f32[4,1,16,128]{1,3,2,0:T(8,128)} %get-tuple-element.45, f32[4,1,16,128]{1,3,2,0:T(8,128)} %get-tuple-element.44, f32[4,63,16,128]{1,3,2,0:T(8,128)} %get-tuple-element.42, f32[1,64,16,128]{1,3,2,0:T(8,128)S(1)} %get-tuple-element.35, ...), kind=kLoop, calls=%fused_computation.28 | loop fusion | flops 15204352 | bytes 10797072 | tf_op jit(solution)/shard_map/mul | solution.py:53
  206.4 5.8 %collective-permute-start.27 = (f32[4,1024]{1,0:T(4,128)}, f32[4,1024]{1,0:T(4,128)}, u32[]{:S(2)}, u32[]{:S(2)}) collective-permute-start(f32[4,1024]{1,0:T(4,128)} %reshape_squeeze.29), channel_id=1, source_target_pairs={{0,12},{4,16},{8,20},{12,24},{16,28},{20,32},{24,36},{28,40},{32,4... | collective-permute-start | bytes 49160 | tf_op jit(solution)/shard_map/ppermute | solution.py:20
  218.3 6.9 %collective-permute-start.24 = (f32[4,1024]{1,0:T(4,128)}, f32[4,1024]{1,0:T(4,128)}, u32[]{:S(2)}, u32[]{:S(2)}) collective-permute-start(f32[4,1024]{1,0:T(4,128)} %reshape_squeeze.28), channel_id=1, source_target_pairs={{12,0},{16,4},{20,8},{24,12},{28,16},{32,20},{36,24},{40,28},{44,3... | collective-permute-start | bytes 49160 | tf_op jit(solution)/shard_map/ppermute | solution.py:20
  228.6 8.2 %fusion.59 = (f32[4,63,16,128]{1,3,2,0:T(8,128)}, f32[4,63,16,128]{1,3,2,0:T(8,128)}) fusion(f32[4,64,16,128]{1,3,2,0:T(8,128)} %copy-done.4), kind=kLoop, calls=%fused_computation.145 | loop fusion | bytes 8257536 | tf_op jit(solution)/shard_map/slice | solution.py:42
  236.8 4.8 %fusion.60 = (f32[4,1,16,128]{1,3,2,0:T(8,128)}, f32[4,1,16,128]{1,3,2,0:T(8,128)}) fusion(f32[4,64,16,128]{1,3,2,0:T(8,128)S(1)} %copy-done.5), kind=kLoop, calls=%fused_computation.146 | loop fusion | bytes 131072 | tf_op jit(solution)/shard_map/slice | solution.py:42
  271.2 16.4 %fusion.14 = f32[4,64,16,128]{1,3,2,0:T(8,128)S(1)} fusion(f32[4,63,16,128]{1,3,2,0:T(8,128)} %get-tuple-element.31, f32[4,1,16,128]{1,3,2,0:T(8,128)} %get-tuple-element.33, f32[4,1,16,128]{1,3,2,0:T(8,128)} %get-tuple-element.32, f32[4,63,16,128]{1,3,2,0:T(8,128)} %get-tuple-element.30, f32[1,64,16,128]{1,3,2,0:T(8,128)S(1)} %get-tuple-element.23, ...), kind=kLoop, calls=%fused_computation.34 | loop fusion | flops 15204352 | bytes 10797072 | tf_op jit(solution)/shard_map/mul | solution.py:53
  290.4 7.0 %collective-permute-start.35 = (f32[4,1024]{1,0:T(4,128)}, f32[4,1024]{1,0:T(4,128)}, u32[]{:S(2)}, u32[]{:S(2)}) collective-permute-start(f32[4,1024]{1,0:T(4,128)} %reshape_squeeze.31), channel_id=1, source_target_pairs={{0,12},{4,16},{8,20},{12,24},{16,28},{20,32},{24,36},{28,40},{32,4... | collective-permute-start | bytes 49160 | tf_op jit(solution)/shard_map/ppermute | solution.py:20
  303.6 6.9 %collective-permute-start.32 = (f32[4,1024]{1,0:T(4,128)}, f32[4,1024]{1,0:T(4,128)}, u32[]{:S(2)}, u32[]{:S(2)}) collective-permute-start(f32[4,1024]{1,0:T(4,128)} %reshape_squeeze.30), channel_id=1, source_target_pairs={{12,0},{16,4},{20,8},{24,12},{28,16},{32,20},{36,24},{40,28},{44,3... | collective-permute-start | bytes 49160 | tf_op jit(solution)/shard_map/ppermute | solution.py:20
  313.8 8.2 %fusion.55 = (f32[4,63,16,128]{1,3,2,0:T(8,128)}, f32[4,63,16,128]{1,3,2,0:T(8,128)}) fusion(f32[4,64,16,128]{1,3,2,0:T(8,128)} %copy-done), kind=kLoop, calls=%fused_computation.141 | loop fusion | bytes 8257536 | tf_op jit(solution)/shard_map/slice | solution.py:42
  355.0 17.3 %fusion.19 = f32[4,64,16,128]{1,3,2,0:T(8,128)} fusion(f32[4,63,16,128]{1,3,2,0:T(8,128)} %get-tuple-element.19, f32[4,1,16,128]{1,3,2,0:T(8,128)} %get-tuple-element.21, f32[4,1,16,128]{1,3,2,0:T(8,128)} %get-tuple-element.20, f32[4,63,16,128]{1,3,2,0:T(8,128)} %get-tuple-element.18, f32[1,64,16,128]{1,3,2,0:T(8,128)S(1)} %get-tuple-element.11, ...), kind=kLoop, calls=%fused_computation.40 | loop fusion | flops 15204352 | bytes 10797072 | tf_op jit(solution)/shard_map/mul | solution.py:53
  376.4 8.2 %collective-permute-start.43 = (f32[4,64,128]{1,0,2:T(4,128)S(1)}, f32[4,64,128]{1,0,2:T(4,128)S(1)}, u32[]{:S(2)}, u32[]{:S(2)}) collective-permute-start(f32[4,64,128]{1,0,2:T(4,128)S(1)} %copy.168), channel_id=1, source_target_pairs={{0,12},{4,16},{8,20},{12,24},{16,28},{20,32},{24,36},{28,40},{32,4... | collective-permute-start | bytes 393224 | tf_op jit(solution)/shard_map/ppermute | solution.py:20
  394.7 6.4 %collective-permute-start.39 = (f32[4,64,128]{1,0,2:T(4,128)S(1)}, f32[4,64,128]{1,0,2:T(4,128)S(1)}, u32[]{:S(2)}, u32[]{:S(2)}) collective-permute-start(f32[4,64,128]{1,0,2:T(4,128)S(1)} %copy.164), channel_id=1, source_target_pairs={{8,0},{12,4},{16,8},{20,12},{24,16},{28,20},{32,24},{36,28},{40,32... | collective-permute-start | bytes 393224 | tf_op jit(solution)/shard_map/ppermute | solution.py:20
  408.0 11.4 %collective-permute-done.38 = f32[4,64,128]{1,0,2:T(4,128)S(1)} collective-permute-done((f32[4,64,128]{1,0,2:T(4,128)S(1)}, f32[4,64,128]{1,0,2:T(4,128)S(1)}, u32[]{:S(2)}, u32[]{:S(2)}) %collective-permute-start.38) | collective-permute-done | bytes 131104 | tf_op jit(solution)/shard_map/ppermute | solution.py:20
  (217 shorter events, 213.8 us)
Async XLA Ops:
  5.5 35.8 %collective-permute-start.8 = (f32[4,1024]{1,0:T(4,128)}, f32[4,1024]{1,0:T(4,128)S(1)}, u32[]{:S(2)}, u32[]{:S(2)}) collective-permute-start(f32[4,1024]{1,0:T(4,128)} %reshape_squeeze.24), channel_id=1, source_target_pairs={{12,0},{16,4},{20,8},{24,12},{28,16},{32,20},{36,24},{40,28},{44,3... | collective-permute-start | bytes 49160 | tf_op jit(solution)/shard_map/ppermute | solution.py:20
  9.5 35.2 %collective-permute-start.7 = (f32[4,1024]{1,0:T(4,128)}, f32[4,1024]{1,0:T(4,128)S(1)}, u32[]{:S(2)}, u32[]{:S(2)}) collective-permute-start(f32[4,1024]{1,0:T(4,128)} %reshape_squeeze.24), channel_id=1, source_target_pairs={{8,0},{12,4},{16,8},{20,12},{24,16},{28,20},{32,24},{36,28},{40,32... | collective-permute-start | bytes 49160 | tf_op jit(solution)/shard_map/ppermute | solution.py:20
  12.5 40.4 %collective-permute-start.6 = (f32[4,1024]{1,0:T(4,128)}, f32[4,1024]{1,0:T(4,128)S(1)}, u32[]{:S(2)}, u32[]{:S(2)}) collective-permute-start(f32[4,1024]{1,0:T(4,128)} %reshape_squeeze.24), channel_id=1, source_target_pairs={{4,0},{8,4},{12,8},{16,12},{20,16},{24,20},{28,24},{32,28},{36,32}... | collective-permute-start | bytes 49160 | tf_op jit(solution)/shard_map/ppermute | solution.py:20
  18.6 37.7 %collective-permute-start.11 = (f32[4,1024]{1,0:T(4,128)}, f32[4,1024]{1,0:T(4,128)S(1)}, u32[]{:S(2)}, u32[]{:S(2)}) collective-permute-start(f32[4,1024]{1,0:T(4,128)} %reshape_squeeze.25), channel_id=1, source_target_pairs={{0,12},{4,16},{8,20},{12,24},{16,28},{20,32},{24,36},{28,40},{32,4... | collective-permute-start | bytes 49160 | tf_op jit(solution)/shard_map/ppermute | solution.py:20
  25.2 33.6 %collective-permute-start.10 = (f32[4,1024]{1,0:T(4,128)}, f32[4,1024]{1,0:T(4,128)S(1)}, u32[]{:S(2)}, u32[]{:S(2)}) collective-permute-start(f32[4,1024]{1,0:T(4,128)} %reshape_squeeze.25), channel_id=1, source_target_pairs={{0,8},{4,12},{8,16},{12,20},{16,24},{20,28},{24,32},{28,36},{32,40... | collective-permute-start | bytes 49160 | tf_op jit(solution)/shard_map/ppermute | solution.py:20
  53.0 38.7 %collective-permute-start.3 = (f32[4,64,128]{1,0,2:T(4,128)S(1)}, f32[4,64,128]{1,0,2:T(4,128)S(1)}, u32[]{:S(2)}, u32[]{:S(2)}) collective-permute-start(f32[4,64,128]{1,0,2:T(4,128)S(1)} %bitcast.76), channel_id=1, source_target_pairs={{4,0},{8,4},{12,8},{16,12},{20,16},{24,20},{28,24},{32,28},{36,32}... | collective-permute-start | bytes 393224 | tf_op jit(solution)/shard_map/ppermute | solution.py:20
  56.3 37.2 %collective-permute-start.2 = (f32[4,64,128]{1,0,2:T(4,128)S(1)}, f32[4,64,128]{1,0,2:T(4,128)S(1)}, u32[]{:S(2)}, u32[]{:S(2)}) collective-permute-start(f32[4,64,128]{1,0,2:T(4,128)S(1)} %bitcast.77), channel_id=1, source_target_pairs={{0,4},{4,8},{8,12},{12,16},{16,20},{20,24},{24,28},{28,32},{32,36}... | collective-permute-start | bytes 393224 | tf_op jit(solution)/shard_map/ppermute | solution.py:20
  58.8 38.4 %collective-permute-start.1 = (f32[4,64,128]{1,0,2:T(4,128)S(1)}, f32[4,64,128]{1,0,2:T(4,128)S(1)}, u32[]{:S(2)}, u32[]{:S(2)}) collective-permute-start(f32[4,64,128]{1,0,2:T(4,128)S(1)} %bitcast.78), channel_id=1, source_target_pairs={{0,8},{4,12},{8,16},{12,20},{16,24},{20,28},{24,32},{28,36},{32,40... | collective-permute-start | bytes 393224 | tf_op jit(solution)/shard_map/ppermute | solution.py:20
  66.1 31.1 %collective-permute-start = (f32[4,64,128]{1,0,2:T(4,128)S(1)}, f32[4,64,128]{1,0,2:T(4,128)S(1)}, u32[]{:S(2)}, u32[]{:S(2)}) collective-permute-start(f32[4,64,128]{1,0,2:T(4,128)S(1)} %bitcast.79), channel_id=1, source_target_pairs={{0,12},{4,16},{8,20},{12,24},{16,28},{20,32},{24,36},{28,40},{32,4... | collective-permute-start | bytes 393224 | tf_op jit(solution)/shard_map/ppermute | solution.py:20
  68.6 28.6 %collective-permute-start.5 = (f32[4,64,128]{1,0,2:T(4,128)S(1)}, f32[4,64,128]{1,0,2:T(4,128)S(1)}, u32[]{:S(2)}, u32[]{:S(2)}) collective-permute-start(f32[4,64,128]{1,0,2:T(4,128)S(1)} %bitcast.80), channel_id=1, source_target_pairs={{12,0},{16,4},{20,8},{24,12},{28,16},{32,20},{36,24},{40,28},{44,3... | collective-permute-start | bytes 393224 | tf_op jit(solution)/shard_map/ppermute | solution.py:20
  122.2 47.9 %collective-permute-start.19 = (f32[4,1024]{1,0:T(4,128)}, f32[4,1024]{1,0:T(4,128)}, u32[]{:S(2)}, u32[]{:S(2)}) collective-permute-start(f32[4,1024]{1,0:T(4,128)} %reshape_squeeze.27), channel_id=1, source_target_pairs={{0,12},{4,16},{8,20},{12,24},{16,28},{20,32},{24,36},{28,40},{32,4... | collective-permute-start | bytes 49160 | tf_op jit(solution)/shard_map/ppermute | solution.py:20
  126.8 39.6 %collective-permute-start.18 = (f32[4,1024]{1,0:T(4,128)}, f32[4,1024]{1,0:T(4,128)S(1)}, u32[]{:S(2)}, u32[]{:S(2)}) collective-permute-start(f32[4,1024]{1,0:T(4,128)} %reshape_squeeze.27), channel_id=1, source_target_pairs={{0,8},{4,12},{8,16},{12,20},{16,24},{20,28},{24,32},{28,36},{32,40... | collective-permute-start | bytes 49160 | tf_op jit(solution)/shard_map/ppermute | solution.py:20
  133.7 49.3 %collective-permute-start.16 = (f32[4,1024]{1,0:T(4,128)}, f32[4,1024]{1,0:T(4,128)}, u32[]{:S(2)}, u32[]{:S(2)}) collective-permute-start(f32[4,1024]{1,0:T(4,128)} %reshape_squeeze.26), channel_id=1, source_target_pairs={{12,0},{16,4},{20,8},{24,12},{28,16},{32,20},{36,24},{40,28},{44,3... | collective-permute-start | bytes 49160 | tf_op jit(solution)/shard_map/ppermute | solution.py:20
  140.1 39.8 %collective-permute-start.15 = (f32[4,1024]{1,0:T(4,128)}, f32[4,1024]{1,0:T(4,128)}, u32[]{:S(2)}, u32[]{:S(2)}) collective-permute-start(f32[4,1024]{1,0:T(4,128)} %reshape_squeeze.26), channel_id=1, source_target_pairs={{8,0},{12,4},{16,8},{20,12},{24,16},{28,20},{32,24},{36,28},{40,32... | collective-permute-start | bytes 49160 | tf_op jit(solution)/shard_map/ppermute | solution.py:20
  206.4 47.6 %collective-permute-start.27 = (f32[4,1024]{1,0:T(4,128)}, f32[4,1024]{1,0:T(4,128)}, u32[]{:S(2)}, u32[]{:S(2)}) collective-permute-start(f32[4,1024]{1,0:T(4,128)} %reshape_squeeze.29), channel_id=1, source_target_pairs={{0,12},{4,16},{8,20},{12,24},{16,28},{20,32},{24,36},{28,40},{32,4... | collective-permute-start | bytes 49160 | tf_op jit(solution)/shard_map/ppermute | solution.py:20
  212.2 38.1 %collective-permute-start.26 = (f32[4,1024]{1,0:T(4,128)}, f32[4,1024]{1,0:T(4,128)S(1)}, u32[]{:S(2)}, u32[]{:S(2)}) collective-permute-start(f32[4,1024]{1,0:T(4,128)} %reshape_squeeze.29), channel_id=1, source_target_pairs={{0,8},{4,12},{8,16},{12,20},{16,24},{20,28},{24,32},{28,36},{32,40... | collective-permute-start | bytes 49160 | tf_op jit(solution)/shard_map/ppermute | solution.py:20
  214.1 29.0 %collective-permute-start.25 = (f32[4,1024]{1,0:T(4,128)}, f32[4,1024]{1,0:T(4,128)S(1)}, u32[]{:S(2)}, u32[]{:S(2)}) collective-permute-start(f32[4,1024]{1,0:T(4,128)} %reshape_squeeze.29), channel_id=1, source_target_pairs={{0,4},{4,8},{8,12},{12,16},{16,20},{20,24},{24,28},{28,32},{32,36}... | collective-permute-start | bytes 49160 | tf_op jit(solution)/shard_map/ppermute | solution.py:20
  218.3 48.7 %collective-permute-start.24 = (f32[4,1024]{1,0:T(4,128)}, f32[4,1024]{1,0:T(4,128)}, u32[]{:S(2)}, u32[]{:S(2)}) collective-permute-start(f32[4,1024]{1,0:T(4,128)} %reshape_squeeze.28), channel_id=1, source_target_pairs={{12,0},{16,4},{20,8},{24,12},{28,16},{32,20},{36,24},{40,28},{44,3... | collective-permute-start | bytes 49160 | tf_op jit(solution)/shard_map/ppermute | solution.py:20
  225.3 38.7 %collective-permute-start.23 = (f32[4,1024]{1,0:T(4,128)}, f32[4,1024]{1,0:T(4,128)}, u32[]{:S(2)}, u32[]{:S(2)}) collective-permute-start(f32[4,1024]{1,0:T(4,128)} %reshape_squeeze.28), channel_id=1, source_target_pairs={{8,0},{12,4},{16,8},{20,12},{24,16},{28,20},{32,24},{36,28},{40,32... | collective-permute-start | bytes 49160 | tf_op jit(solution)/shard_map/ppermute | solution.py:20
  290.4 47.6 %collective-permute-start.35 = (f32[4,1024]{1,0:T(4,128)}, f32[4,1024]{1,0:T(4,128)}, u32[]{:S(2)}, u32[]{:S(2)}) collective-permute-start(f32[4,1024]{1,0:T(4,128)} %reshape_squeeze.31), channel_id=1, source_target_pairs={{0,12},{4,16},{8,20},{12,24},{16,28},{20,32},{24,36},{28,40},{32,4... | collective-permute-start | bytes 49160 | tf_op jit(solution)/shard_map/ppermute | solution.py:20
  297.5 36.9 %collective-permute-start.34 = (f32[4,1024]{1,0:T(4,128)}, f32[4,1024]{1,0:T(4,128)S(1)}, u32[]{:S(2)}, u32[]{:S(2)}) collective-permute-start(f32[4,1024]{1,0:T(4,128)} %reshape_squeeze.31), channel_id=1, source_target_pairs={{0,8},{4,12},{8,16},{12,20},{16,24},{20,28},{24,32},{28,36},{32,40... | collective-permute-start | bytes 49160 | tf_op jit(solution)/shard_map/ppermute | solution.py:20
  299.4 29.0 %collective-permute-start.33 = (f32[4,1024]{1,0:T(4,128)}, f32[4,1024]{1,0:T(4,128)S(1)}, u32[]{:S(2)}, u32[]{:S(2)}) collective-permute-start(f32[4,1024]{1,0:T(4,128)} %reshape_squeeze.31), channel_id=1, source_target_pairs={{0,4},{4,8},{8,12},{12,16},{16,20},{20,24},{24,28},{28,32},{32,36}... | collective-permute-start | bytes 49160 | tf_op jit(solution)/shard_map/ppermute | solution.py:20
  303.6 47.3 %collective-permute-start.32 = (f32[4,1024]{1,0:T(4,128)}, f32[4,1024]{1,0:T(4,128)}, u32[]{:S(2)}, u32[]{:S(2)}) collective-permute-start(f32[4,1024]{1,0:T(4,128)} %reshape_squeeze.30), channel_id=1, source_target_pairs={{12,0},{16,4},{20,8},{24,12},{28,16},{32,20},{36,24},{40,28},{44,3... | collective-permute-start | bytes 49160 | tf_op jit(solution)/shard_map/ppermute | solution.py:20
  310.5 37.3 %collective-permute-start.31 = (f32[4,1024]{1,0:T(4,128)}, f32[4,1024]{1,0:T(4,128)}, u32[]{:S(2)}, u32[]{:S(2)}) collective-permute-start(f32[4,1024]{1,0:T(4,128)} %reshape_squeeze.30), channel_id=1, source_target_pairs={{8,0},{12,4},{16,8},{20,12},{24,16},{28,20},{32,24},{36,28},{40,32... | collective-permute-start | bytes 49160 | tf_op jit(solution)/shard_map/ppermute | solution.py:20
  (36 other events, 603.9 us)
where the time goes:
time: 423 us; the launch traced here: 420 us
  starting transfers between devices  180 us (43%)
  local copies, waits for them, and re-layouts  136 us (32%)
  other arithmetic  89.2 us (21%)
  waiting for transfers between devices  13.2 us (3%)
    ppermute x36, starting transfers between devices, passed_along(): lax.ppermute(value, axis, [(source, source + steps) for source in range(l...  157 us
    mul x4, other arithmetic, advance(): return (updated + rotation) * wet_mask  68 us
    slice x9, local copies, waits for them, and re-layouts, advance(): level_below = jnp.concatenate([current[:, 1:], current[:, -1:]], axis=1)  46.5 us
    reshape x24, local copies, waits for them, and re-layouts, per_device(): from_east.reshape(edge_shape)  31.4 us
    reshape x24, local copies, waits for them, and re-layouts, per_device(): from_west.reshape(edge_shape)  21.5 us
    unnamed x37, local copies, waits for them, and re-layouts  15.8 us
    ppermute x4, starting transfers between devices, extended(): lax.ppermute(lax.slice_in_dim(block, 0, width, axis=dim), axis, backward)  14.8 us
    ppermute x36, waiting for transfers between devices, passed_along(): lax.ppermute(value, axis, [(source, source + steps) for source in range(l...  12.3 us
  transfers between devices with their start and end apart: 44, of which 3 were waited for; matrix products, arithmetic and copies ran while one was open for 33% of the time, Pallas kernels for 0%

commit v1 on v0

v1 whole, which is shorter than its diff:
```python
import functools

import jax
import jax.numpy as jnp
from jax import lax
from jax.experimental import pallas as pl
from jax.experimental.pallas import tpu as pltpu
from jax.sharding import PartitionSpec as P

FIELDS = 4
LEVELS = 64
ROWS = 16
COLS = 128
HALO = 4
EXT = ROWS + 2 * HALO
HALF = LEVELS // 2
PLANES = 2 * FIELDS
PAD = 8
STATE_ROWS = FIELDS * LEVELS * EXT + 2 * PAD
PACK_ROWS = PLANES * EXT
SIDE_ROWS = PACK_ROWS + EXT
REACH = 3
SLOTS = 2 * REACH + 1
GROUP = 4
UNROLL = 4
VMEM_BYTES = 44 * 1024 * 1024

TIME_STEP = 0.1
TURN = 0.05
FEEDBACK = 0.5

S_EVEN, S_TOP, S_BOTTOM, S_PBX, S_SLOT, S_XEVEN, S_LOW, S_PB = 0, 1, 2, 3, 4, 10, 11, 12


def lanes():
    return lax.broadcasted_iota(jnp.int32, (8, COLS), 1)


def send_rows_kernel(sc, nest, pay1, pay2):
    even = sc[S_EVEN] == 1
    first = jnp.where(even, ROWS - HALO, 0)
    second = jnp.where(even, 0, ROWS - HALO)

    def body(i, carry):
        for j in range(8):
            at = (i * 8 + j) * ROWS
            to = (i * 8 + j) * HALO
            pay1[pl.ds(to, HALO), :] = nest[pl.ds(at + first, HALO), :]
            pay2[pl.ds(to, HALO), :] = nest[pl.ds(at + second, HALO), :]
        return carry

    lax.fori_loop(0, FIELDS * LEVELS // 8, body, 0)


def open_kernel(sc, own, got1, got2, got3, idx, weight, face, mask, mixing, og, off, pay1, pay2):
    pbx = sc[S_PBX]
    chosen = own[...]
    for code, got in ((1, got1), (2, got2), (3, got3)):
        chosen = jnp.where(pbx == code, got[...], chosen)
    cell = lax.broadcasted_iota(jnp.int32, (ROWS, COLS), 1)
    spread = []
    for side in range(2):
        total = jnp.zeros((ROWS, 1), jnp.float32)
        table = jnp.zeros((ROWS, COLS), jnp.float32)
        for j in range(4):
            w = weight[:, side * 4 + j : side * 4 + j + 1]
            total = total + w
            table = table + jnp.where(idx[:, side * 4 + j : side * 4 + j + 1] == cell, w, 0.0)
        spread.append(table / total)
    table = jnp.concatenate(spread, axis=0)
    values = lax.dot_general(
        table, chosen, (((1,), (1,)), ((), ())),
        precision=lax.Precision.HIGHEST, preferred_element_type=jnp.float32,
    )
    source = lax.broadcasted_iota(jnp.int32, (COLS, COLS), 0)
    target = lax.broadcasted_iota(jnp.int32, (COLS, COLS), 1)
    lane16 = lax.broadcasted_iota(jnp.int32, (ROWS, COLS), 1)
    column = lane16 % 4
    wcol = face[:, 0:1].astype(jnp.float32)
    ecol = face[:, 1:2].astype(jnp.float32)
    off_plane = jnp.where(column == 1, wcol, ecol)
    off[...] = off_plane
    planes = []
    for h in range(2):
        for f in range(FIELDS):
            quarter = (f % 2) * 2 + h
            expand = (source == quarter * HALF + target // 4).astype(jnp.float32)
            block = values[:, (f // 2) * COLS : (f // 2 + 1) * COLS]
            wide = lax.dot_general(
                block, expand, (((1,), (0,)), ((), ())),
                precision=lax.Precision.HIGHEST, preferred_element_type=jnp.float32,
            )
            plane = jnp.where(column == 1, wide[:ROWS], wide[ROWS:])
            og[pl.ds((h * FIELDS + f) * ROWS, ROWS), :] = plane
            planes.append(plane)
    planes += [mask[...].astype(jnp.float32), mixing[...], off_plane]
    even = sc[S_EVEN] == 1
    for i, plane in enumerate(planes):
        low, high = plane[:HALO], plane[ROWS - HALO :]
        pay1[pl.ds(i * HALO, HALO), :] = jnp.where(even, high, low)
        pay2[pl.ds(i * HALO, HALO), :] = jnp.where(even, low, high)


def pack_into(acc, value, k, lane):
    hit = (lane // 4) == k
    return jnp.where(hit, pltpu.roll(value, 4 * k + 2, 1), acc)


def extend_kernel(
    sc, nest, wide1, wide2, og, off, mask, mixing, edge1, edge2,
    ext, pack, og_ext, stat, msg_e, msg_o, msg_lo, msg_hi,
):
    even = sc[S_EVEN] == 1
    top_in = sc[S_TOP] == 1
    bottom_in = sc[S_BOTTOM] == 1

    def halos(one, two):
        top = jnp.where(top_in, jnp.where(even, two, one), 0.0)
        bottom = jnp.where(bottom_in, jnp.where(even, one, two), 0.0)
        return top, bottom

    zero_pad = jnp.zeros((PAD, COLS), jnp.float32)
    ext[pl.ds(0, PAD), :] = zero_pad
    ext[pl.ds(STATE_ROWS - PAD, PAD), :] = zero_pad

    def fill(i, carry):
        for j in range(4):
            fk = i * 4 + j
            base = PAD + fk * EXT
            top, bottom = halos(wide1[pl.ds(fk * HALO, HALO), :], wide2[pl.ds(fk * HALO, HALO), :])
            ext[pl.ds(base, HALO), :] = top
            ext[pl.ds(base + HALO, 8), :] = nest[pl.ds(fk * ROWS, 8), :]
            ext[pl.ds(base + HALO + 8, 8), :] = nest[pl.ds(fk * ROWS + 8, 8), :]
            ext[pl.ds(base + HALO + ROWS, HALO), :] = bottom
        return carry

    lax.fori_loop(0, FIELDS * LEVELS // 4, fill, 0)

    def put(dst, base, own, plane):
        top, bottom = halos(edge1[pl.ds(plane * HALO, HALO), :], edge2[pl.ds(plane * HALO, HALO), :])
        dst[pl.ds(base, HALO), :] = top
        dst[pl.ds(base + HALO, ROWS), :] = own
        dst[pl.ds(base + HALO + ROWS, HALO), :] = bottom

    for i in range(PLANES):
        put(og_ext, i * EXT, og[pl.ds(i * ROWS, ROWS), :], i)
    put(stat, 0, mask[...].astype(jnp.float32), PLANES)
    put(stat, EXT, mixing[...], PLANES + 1)
    put(stat, 2 * EXT, off[...], PLANES + 2)

    lane = lanes()
    column = lane % 4
    for g in range(3):
        for h in range(2):

            def gather(i, acc, g=g, h=h):
                acc = list(acc)
                for j in range(UNROLL):
                    k = i * UNROLL + j
                    for f in range(FIELDS):
                        at = PAD + (f * LEVELS + h * HALF + k) * EXT + 8 * g
                        acc[f] = pack_into(acc[f], ext[pl.ds(at, 8), :], k, lane)
                return tuple(acc)

            acc = lax.fori_loop(
                0, HALF // UNROLL, gather, tuple(jnp.zeros((8, COLS), jnp.float32) for _ in range(FIELDS))
            )
            for f in range(FIELDS):
                pack[pl.ds((h * FIELDS + f) * EXT + 8 * g, 8), :] = acc[f]

    x_even = sc[S_XEVEN] == 1
    low = sc[S_LOW] == 1
    number = sc[S_PB].astype(jnp.float32)
    for i in range(PLANES + 1):
        for g in range(3):
            rows = pl.ds(i * EXT + 8 * g, 8)
            if i < PLANES:
                own, opened = pack[rows, :], og_ext[rows, :]
                right = jnp.where(column == 3, pltpu.roll(opened, 1, 1), own)
                left = jnp.where(column == 0, pltpu.roll(opened, COLS - 1, 1), own)
            else:
                wet = stat[pl.ds(8 * g, 8), :]
                mix = stat[pl.ds(EXT + 8 * g, 8), :]
                away = stat[pl.ds(2 * EXT + 8 * g, 8), :]
                right = jnp.where(lane == 0, pltpu.roll(wet, 1, 1), jnp.where(lane == 1, pltpu.roll(mix, 2, 1), away))
                left = jnp.where(
                    lane == 0, wet, jnp.where(lane == 1, pltpu.roll(mix, 1, 1), pltpu.roll(away, 1, 1))
                )
                right = jnp.where(lane == 3, number, right)
                left = jnp.where(lane == 3, number, left)
            msg_e[rows, :] = jnp.where(x_even, right, left)
            msg_o[rows, :] = jnp.where(x_even, left, right)
            msg_lo[rows, :] = jnp.where(low, right, left)
            msg_hi[rows, :] = jnp.where(low, left, right)


def ghosts(side, out0, out1, og_ext, stat, nxt):
    lane = lanes()
    column = lane % 4
    span = SIDE_ROWS

    def rows_of(slot, plane, row):
        return side[pl.ds(PAD + slot * span + plane * EXT + row, 8), :]

    for g in range(3):
        row = 8 * g
        away = stat[pl.ds(2 * EXT + row, 8), :]
        for plane in range(PLANES):
            at = pl.ds(plane * EXT + row, 8)
            value = og_ext[at, :]
            out1[at, :] = value
            for d in range(1, REACH + 1):
                source = jnp.where(column == 1, rows_of(REACH - d, plane, row), rows_of(REACH + d, plane, row))
                value = jnp.where(away == d, source, value)
            out0[at, :] = value
        for d in range(1, REACH + 1):
            stat_l = rows_of(REACH - d, PLANES, row)
            stat_r = rows_of(REACH + d, PLANES, row)
            from_left = column < 2

            def both(i):
                return jnp.where(
                    from_left,
                    jnp.broadcast_to(stat_l[:, i : i + 1], (8, COLS)),
                    jnp.broadcast_to(stat_r[:, i : i + 1], (8, COLS)),
                )

            wet, mix = both(0), both(1)
            east_off = jnp.broadcast_to(stat_l[:, 2:3], (8, COLS))
            west_off = jnp.broadcast_to(stat_r[:, 2:3], (8, COLS))
            kmix = wet * mix
            centre = wet - 4.0 * TIME_STEP * wet - 2.0 * kmix
            base = TIME_STEP * wet

            def joined(plane, row):
                return jnp.where(from_left, rows_of(REACH - d, plane, row), rows_of(REACH + d, plane, row))

            here = [joined(plane, row) for plane in range(PLANES)]
            for h in range(2):
                cu = TURN * wet * here[h * FIELDS + 2]
                cv = TURN * wet * here[h * FIELDS + 3]
                ke, kw, kn, ks = base - cu, base + cu, base - cv, base + cv
                for f in range(FIELDS):
                    plane = h * FIELDS + f
                    q = here[plane]
                    edge_e = rows_of(REACH - d, plane, row)
                    edge_w = rows_of(REACH + d, plane, row)
                    east_ghost = jnp.zeros_like(q)
                    west_ghost = jnp.zeros_like(q)
                    for e in range(1, REACH + 1):
                        east_ghost = jnp.where(east_off == e, rows_of(REACH - d + e, plane, row), east_ghost)
                        west_ghost = jnp.where(west_off == e, rows_of(REACH + d - e, plane, row), west_ghost)
                    east_ghost = jnp.where(
                        east_off == 0, pltpu.roll(edge_e, COLS - 2, 1), pltpu.roll(east_ghost, COLS - 1, 1)
                    )
                    west_ghost = jnp.where(
                        west_off == 0, pltpu.roll(edge_w, 2, 1), pltpu.roll(west_ghost, 1, 1)
                    )
                    east = jnp.where(column == 1, east_ghost, pltpu.roll(q, COLS - 1, 1))
                    west = jnp.where(column == 2, west_ghost, pltpu.roll(q, 1, 1))
                    north, south = joined(plane, row + 1), joined(plane, row - 1)
                    other = here[(1 - h) * FIELDS + f]
                    if h == 0:
                        above = jnp.where(lane < 4, q, pltpu.roll(q, 4, 1))
                        below = pltpu.roll(jnp.where(lane < 4, other, q), COLS - 4, 1)
                    else:
                        above = pltpu.roll(jnp.where(lane >= COLS - 4, other, q), 4, 1)
                        below = jnp.where(lane >= COLS - 4, q, pltpu.roll(q, COLS - 4, 1))
                    new = centre * q + ke * east + kw * west + kn * north + ks * south + kmix * (above + below)
                    if f == 2:
                        new = new + cv
                    if f == 3:
                        new = new - cu
                    at = pl.ds(plane * EXT + row, 8)
                    out1[at, :] = jnp.where(away == d, new, out1[at, :])


def substep(src, dst_store, ghost, stat, starts, pack):
    lane = lanes()
    first_lane, last_lane = lane == 0, lane == COLS - 1
    for row in starts:
        wet = stat[pl.ds(row, 8), :]
        mix = stat[pl.ds(EXT + row, 8), :]
        kmix = wet * mix
        centre = wet - 4.0 * TIME_STEP * wet - 2.0 * kmix
        base = TIME_STEP * wet
        turn = TURN * wet

        def load(f, k, shift=0, row=row):
            return src[pl.ds(PAD + (f * LEVELS + k) * EXT + row + shift, 8), :]

        cur = tuple(load(f, 0) for f in range(FIELDS))
        carry = (cur, cur)
        for h in range(2):
            ghost_h = [ghost[pl.ds((h * FIELDS + f) * EXT + row, 8), :] for f in range(FIELDS)]

            def body(i, state, h=h, ghost_h=ghost_h, row=row):
                prev, cur, acc = state
                acc = list(acc)
                for j in range(UNROLL):
                    kk = i * UNROLL + j
                    k = h * HALF + kk
                    nxt = tuple(load(f, jnp.minimum(k + 1, LEVELS - 1)) for f in range(FIELDS))
                    cu, cv = turn * cur[2], turn * cur[3]
                    ke, kw, kn, ks = base - cu, base + cu, base - cv, base + cv
                    for f in range(FIELDS):
                        q = cur[f]
                        edge = pltpu.roll(ghost_h[f], COLS - 2 - 4 * kk, 1)
                        west = pltpu.roll(jnp.where(last_lane, edge, q), 1, 1)
                        east = pltpu.roll(jnp.where(first_lane, edge, q), COLS - 1, 1)
                        north, south = load(f, k, 1), load(f, k, -1)
                        new = (centre * q + ke * east) + (kw * west + kn * north)
                        new = new + (ks * south + kmix * (prev[f] + nxt[f]))
                        if f == 2:
                            new = new + cv
                        if f == 3:
                            new = new - cu
                        dst_store(f, k, row, new)
                        if pack is not None:
                            acc[f] = pack_into(acc[f], new, kk, lane)
                    prev, cur = cur, nxt
                return prev, cur, tuple(acc)

            zero = tuple(jnp.zeros((8, COLS), jnp.float32) for _ in range(FIELDS if pack is not None else 0))
            prev, cur, acc = lax.fori_loop(0, HALF // UNROLL, body, carry + (zero,))
            carry = (prev, cur)
            if pack is not None:
                for f in range(FIELDS):
                    pack[pl.ds((h * FIELDS + f) * EXT + row, 8), :] = acc[f]


def store_in(ref):
    def store(f, k, row, value):
        ref[pl.ds(PAD + (f * LEVELS + k) * EXT + row, 8), :] = value

    return store


def clear_pads(*refs):
    for ref in refs:
        rows = ref.shape[0]
        ref[pl.ds(0, PAD), :] = jnp.zeros((PAD, COLS), jnp.float32)
        ref[pl.ds(rows - PAD, PAD), :] = jnp.zeros((PAD, COLS), jnp.float32)


def first_kernel(sc, ext, own, og_ext, stat, r0, r1, r2, r3, r4, r5, out, pack, side, mid, gh0, gh1):
    clear_pads(side, mid, out)
    side[pl.ds(PAD + REACH * SIDE_ROWS, PACK_ROWS), :] = own[...]
    side[pl.ds(PAD + REACH * SIDE_ROWS + PACK_ROWS, EXT), :] = jnp.zeros((EXT, COLS), jnp.float32)
    for j, r in enumerate((r0, r1, r2, r3, r4, r5)):
        at = pl.multiple_of(PAD + sc[S_SLOT + j] * SIDE_ROWS, 8)
        side[pl.ds(at, SIDE_ROWS), :] = r[...]
    ghosts(side, gh0, gh1, og_ext, stat, None)
    substep(ext, store_in(mid), gh0, stat, (0, 8, 16), None)
    substep(mid, store_in(out), gh1, stat, (0, 8, 16), pack)


def second_kernel(
    sc, ext, own, og_ext, stat, r0, r1, r2, r3, r4, r5, s0, s1, s2, s3, s4, s5,
    out, means, side, mid, gh0, gh1,
):
    clear_pads(side, mid)
    side[pl.ds(PAD + REACH * SIDE_ROWS, PACK_ROWS), :] = own[...]
    side[pl.ds(PAD + REACH * SIDE_ROWS + PACK_ROWS, EXT), :] = jnp.zeros((EXT, COLS), jnp.float32)
    column = lax.broadcasted_iota(jnp.int32, (EXT, COLS), 1) % 4
    for j, (r, s) in enumerate(zip((r0, r1, r2, r3, r4, r5), (s0, s1, s2, s3, s4, s5))):
        slot = sc[S_SLOT + j]
        at = PAD + slot * SIDE_ROWS
        kept = column == jnp.where(slot > REACH, 0, 3)
        for plane in range(PLANES):
            rows = pl.ds(plane * EXT, EXT)
            side[pl.ds(pl.multiple_of(at + plane * EXT, 8), EXT), :] = jnp.where(kept, r[rows, :], s[rows, :])
        side[pl.ds(pl.multiple_of(at + PACK_ROWS, 8), EXT), :] = r[pl.ds(PACK_ROWS, EXT), :]
    ghosts(side, gh0, gh1, og_ext, stat, None)
    substep(ext, store_in(mid), gh0, stat, (0, 8, 16), None)

    def store_out(f, k, row, value):
        out[pl.ds((f * LEVELS + k) * ROWS + row - HALO, 8), :] = value

    substep(mid, store_out, gh1, stat, (HALO, HALO + 8), None)

    source = lax.broadcasted_iota(jnp.int32, (COLS, COLS), 0)
    target = lax.broadcasted_iota(jnp.int32, (COLS, COLS), 1)
    block = 64
    for b in range(FIELDS * LEVELS // block):
        total = jnp.zeros((block, COLS), jnp.float32)
        for a in range(4):
            rows = []
            for c in range(block // 8):
                at = (b * block + c * 8) * ROWS + 4 * a
                part = [out[pl.ds(at + i, 8, stride=ROWS), :] for i in range(4)]
                rows.append((part[0] + part[1]) + (part[2] + part[3]))
            gather = jnp.where(a * 32 + source // 4 == target, 1.0 / 16.0, 0.0).astype(jnp.float32)
            total = total + lax.dot_general(
                jnp.concatenate(rows, axis=0), gather, (((1,), (0,)), ((), ())),
                precision=lax.Precision.HIGHEST, preferred_element_type=jnp.float32,
            )
        means[pl.ds(b * block, block), :] = total


def call(kernel, outs, scratch, *args):
    return pl.pallas_call(
        kernel,
        out_shape=[jax.ShapeDtypeStruct(s, jnp.float32) for s in outs],
        in_specs=[pl.BlockSpec(memory_space=pltpu.SMEM)] + [pl.BlockSpec(memory_space=pltpu.VMEM)] * (len(args) - 1),
        out_specs=[pl.BlockSpec(memory_space=pltpu.VMEM)] * len(outs),
        scratch_shapes=[pltpu.VMEM(s, jnp.float32) for s in scratch],
        compiler_params=pltpu.CompilerParams(vmem_limit_bytes=VMEM_BYTES),
    )(*args)


def per_device(nest_state, mixing, land_mask, face_off, parent_state, parent_block, interp_idx, interp_w):
    tiles = lax.axis_size("nest")
    blocks = lax.axis_size("parent")
    n = lax.axis_index("nest")
    p = lax.axis_index("parent")
    x = n % GROUP
    own_block = parent_block[0, 0]

    def inside(code):
        return [(s, s ^ code) for s in range(tiles)]

    def across(pairs):
        links = []
        for g in range(tiles // GROUP):
            for a, b in pairs:
                i, j = GROUP * g + a, (GROUP * (g + 1) + b) % tiles
                links += [(i, j), (j, i)]
        return links

    rows_1 = [(s, s ^ 1) for s in range(blocks)]
    rows_2 = [(s, ((s + 1) ^ 1) - 1) if 0 < s < blocks - 1 else (s, blocks - 1 - s) for s in range(blocks)]
    links = [
        inside(1), inside(2), inside(3),
        across([(3, 0), (2, 1)]), across([(3, 1), (2, 0)]), across([(3, 2), (1, 0)]),
    ]
    x_even, low = x % 2 == 0, x < 2
    rel = [
        jnp.where(x_even, 1, -1),
        jnp.where(low, 2, -2),
        3 - 2 * x,
        jnp.where(low, -1 - 2 * x, 7 - 2 * x),
        jnp.where(low, -2, 2),
        jnp.where(x_even, -3, 3),
    ]
    sc = jnp.stack(
        [
            (p % 2 == 0).astype(jnp.int32),
            (p > 0).astype(jnp.int32),
            (p < blocks - 1).astype(jnp.int32),
            own_block ^ n,
        ]
        + [REACH + r for r in rel]
        + [x_even.astype(jnp.int32), low.astype(jnp.int32), own_block]
    ).astype(jnp.int32)

    nest2 = nest_state.reshape(FIELDS * LEVELS * ROWS, COLS)
    coarse = parent_state.reshape(FIELDS * LEVELS, COLS)
    halo_rows = (FIELDS * LEVELS * HALO, COLS)
    pay1, pay2 = call(send_rows_kernel, [halo_rows] * 2, [], sc, nest2)
    wide1 = lax.ppermute(pay1, "parent", rows_1)
    wide2 = lax.ppermute(pay2, "parent", rows_2)
    got = [lax.ppermute(coarse, "nest", links[i]) for i in range(3)]
    edge_rows = ((PLANES + 3) * HALO, COLS)
    og, off, epay1, epay2 = call(
        open_kernel, [(PLANES * ROWS, COLS), (ROWS, COLS), edge_rows, edge_rows], [],
        sc, coarse, *got, interp_idx.reshape(ROWS, 8), interp_w.reshape(ROWS, 8), face_off, land_mask, mixing,
    )
    edge1 = lax.ppermute(epay1, "parent", rows_1)
    edge2 = lax.ppermute(epay2, "parent", rows_2)
    side = (SIDE_ROWS, COLS)
    ext, pack, og_ext, stat, msg_e, msg_o, msg_lo, msg_hi = call(
        extend_kernel,
        [(STATE_ROWS, COLS), (PACK_ROWS, COLS), (PACK_ROWS, COLS), (3 * EXT, COLS)] + [side] * 4, [],
        sc, nest2, wide1, wide2, og, off, land_mask, mixing, edge1, edge2,
    )
    msgs = [msg_e, msg_lo, msg_lo, msg_hi, msg_hi, msg_o]
    first = [lax.ppermute(m, "nest", link) for m, link in zip(msgs, links)]
    work = [(SLOTS * SIDE_ROWS + 2 * PAD, COLS), (STATE_ROWS, COLS), (PACK_ROWS, COLS), (PACK_ROWS, COLS)]
    ext, pack = call(
        first_kernel, [(STATE_ROWS, COLS), (PACK_ROWS, COLS)], work, sc, ext, pack, og_ext, stat, *first
    )
    second = [lax.ppermute(pack, "nest", link) for link in links]
    new2, means = call(
        second_kernel, [(FIELDS * LEVELS * ROWS, COLS), (FIELDS * LEVELS, COLS)], work,
        sc, ext, pack, og_ext, stat, *first, *second,
    )
    received = means
    me = n.astype(jnp.float32)
    for i in range(3):
        arrived = lax.ppermute(means, "nest", links[i])
        received = jnp.where(first[i][PACK_ROWS, 3] == me, arrived, received)
    parent_new = coarse + FEEDBACK * (received - coarse)
    return new2.reshape(nest_state.shape), parent_new.reshape(parent_state.shape)


def solution(mesh):
    return jax.shard_map(
        per_device,
        mesh=mesh,
        in_specs=(
            P(None, None, "parent", "nest"),
            P("parent", "nest"),
            P("parent", "nest"),
            P("parent", "nest"),
            P(None, None, "parent", "nest"),
            P("parent", "nest"),
            P("parent", "nest", None),
            P("parent", "nest", None),
        ),
        out_specs=(P(None, None, "parent", "nest"), P(None, None, "parent", "nest")),
        check_vma=False,
    )
```

time: 423 us -> 127 us (0.30)
  the two profiles are of different devices: /device:TPU:122 before, /device:TPU:2 now
where the time goes in v1:
time: 127 us; the launch traced here: 126 us
  Pallas kernels  49 us (39%)
  starting transfers between devices  41.3 us (33%)
  waiting for transfers between devices  22.1 us (17%)
  local copies, waits for them, and re-layouts  9.87 us (8%)
  between operations  3.41 us (3%)
    pallas_call x5, Pallas kernels, call(): pl.pallas_call(kernel, out_shape=[jax.ShapeDtypeStruct(s, jnp.float32) fo...  49 us
    ppermute x6, starting transfers between devices, per_device(): first = [lax.ppermute(m, 'nest', link) for m, link in zip(msgs, links)]  18.3 us
    ppermute x6, starting transfers between devices, per_device(): second = [lax.ppermute(pack, 'nest', link) for link in links]  12.8 us
    ppermute x6, waiting for transfers between devices, per_device(): second = [lax.ppermute(pack, 'nest', link) for link in links]  7.2 us
    unnamed x19, local copies, waits for them, and re-layouts  6.52 us
    ppermute x6, waiting for transfers between devices, per_device(): first = [lax.ppermute(m, 'nest', link) for m, link in zip(msgs, links)]  6.38 us
    ppermute x3, waiting for transfers between devices, per_device(): got = [lax.ppermute(coarse, 'nest', links[i]) for i in range(3)]  4.46 us
    ppermute x3, starting transfers between devices, per_device(): arrived = lax.ppermute(means, 'nest', links[i])  4.45 us
  transfers between devices with their start and end apart: 22, of which 10 were waited for; matrix products, arithmetic and copies ran while one was open for 4% of the time, Pallas kernels for 1%

profile of v1, /device:TPU:2, one launch (start us, length us, event | category | flops | bytes accessed | tf_op | source)
XLA Modules:
  0.0 126.3 jit_solution(3698899585723197486)
XLA Ops:
  1.4 1.6 %copy-done = f32[4,64,16,128]{3,2,1,0:T(8,128)S(1)} copy-done((f32[4,64,16,128]{3,2,1,0:T(8,128)S(1)}, f32[4,64,16,128]{3,2,1,0:T(8,128)}, u32[]{:S(2)}) %copy-start) | copy-done | bytes 2097176
  3.0 1.8 %shard_map.95 = (f32[1024,128]{1,0:T(8,128)}, f32[1024,128]{1,0:T(8,128)}) custom-call(s32[13]{0:T(128)S(1)} %stack.71.sc, f32[4096,128]{1,0:T(8,128)S(1)} %bitcast.27), custom_call_target="tpu_custom_call" | custom-call | tf_op jit(solution)/shard_map/pallas_call | solution.py:402
  4.9 1.7 %collective-permute-start.1 = (f32[1024,128]{1,0:T(8,128)}, f32[1024,128]{1,0:T(8,128)S(1)}, u32[]{:S(2)}, u32[]{:S(2)}) collective-permute-start(f32[1024,128]{1,0:T(8,128)} %get-tuple-element.21), channel_id=1, source_target_pairs={{0,3},{1,2},{2,1},{3,0},{4,7},{5,6},{6,5},{7,4},{8,11},{9,10},{10,... | collective-permute-start | bytes 1572872 | tf_op jit(solution)/shard_map/ppermute | solution.py:462
  7.2 2.3 %collective-permute-start.3 = (f32[256,128]{1,0:T(8,128)}, f32[256,128]{1,0:T(8,128)S(1)}, u32[]{:S(2)}, u32[]{:S(2)}) collective-permute-start(f32[256,128]{1,0:T(8,128)} %bitcast.30), channel_id=1, source_target_pairs={{0,8},{4,12},{8,0},{12,4},{16,24},{20,28},{24,16},{28,20},{32,40},... | collective-permute-start | bytes 393224 | tf_op jit(solution)/shard_map/ppermute | solution.py:463
  11.6 1.4 %copy.12.face = s32[16,2]{1,0:T(8,128)} copy(s32[16,2]{0,1:T(2,128)} %param.11) | data formatting | bytes 256 | tf_op args[3]
  12.9 3.1 %collective-permute-done.3.got2 = f32[256,128]{1,0:T(8,128)S(1)} collective-permute-done((f32[256,128]{1,0:T(8,128)}, f32[256,128]{1,0:T(8,128)S(1)}, u32[]{:S(2)}, u32[]{:S(2)}) %collective-permute-start.3) | collective-permute-done | bytes 131104 | tf_op jit(solution)/shard_map/ppermute | solution.py:463
  16.0 1.4 %collective-permute-done.4.got3 = f32[256,128]{1,0:T(8,128)S(1)} collective-permute-done((f32[256,128]{1,0:T(8,128)}, f32[256,128]{1,0:T(8,128)S(1)}, u32[]{:S(2)}, u32[]{:S(2)}) %collective-permute-start.4) | collective-permute-done | bytes 131104 | tf_op jit(solution)/shard_map/ppermute | solution.py:463
  21.0 1.6 %shard_map.96 = (f32[128,128]{1,0:T(8,128)S(1)}, f32[16,128]{1,0:T(8,128)S(1)}, f32[44,128]{1,0:T(8,128)S(1)}, f32[44,128]{1,0:T(8,128)S(1)}) custom-call(s32[13]{0:T(128)S(1)} %copy-done.8, f32[256,128]{1,0:T(8,128)S(1)} %bitcast.32, f32[256,128]{1,0:T(8,128)S(1)} %collective-permute-done.2.got1, f32[256,128]{1,0:T(8,128)S(1)} %collective-permute-done.3.got2, ...), custom_call_target="tpu_custom_call" | custom-call | tf_op jit(solution)/shard_map/pallas_call | solution.py:402
  23.7 2.1 %collective-permute-done.6.edge2 = f32[44,128]{1,0:T(8,128)S(1)} collective-permute-done((f32[44,128]{1,0:T(8,128)S(1)}, f32[44,128]{1,0:T(8,128)S(1)}, u32[]{:S(2)}, u32[]{:S(2)}) %collective-permute-start.6) | collective-permute-done | bytes 22560 | tf_op jit(solution)/shard_map/ppermute | solution.py:470
  25.9 5.4 %shard_map.97 = (f32[6160,128]{1,0:T(8,128)S(1)}, f32[192,128]{1,0:T(8,128)S(1)}, f32[192,128]{1,0:T(8,128)S(1)}, f32[72,128]{1,0:T(8,128)S(1)}, f32[216,128]{1,...) custom-call(s32[13]{0:T(128)S(1)} %copy-done.8, f32[4096,128]{1,0:T(8,128)S(1)} %bitcast.28, ...), custom_call_target="tpu_custom_call" | custom-call | tf_op jit(solution)/shard_map/pallas_call | solution.py:402
  31.3 8.2 %collective-permute-start.10 = (f32[216,128]{1,0:T(8,128)S(1)}, f32[216,128]{1,0:T(8,128)S(1)}, u32[]{:S(2)}, u32[]{:S(2)}) collective-permute-start(f32[216,128]{1,0:T(8,128)S(1)} %get-tuple-element.32), channel_id=1, source_target_pairs={{12,16},{16,12},{8,20},{20,8},{28,32},{32,28},{24,36},{36,24},{44,... | collective-permute-start | bytes 331784 | tf_op jit(solution)/shard_map/ppermute | solution.py:478
  39.5 1.6 %collective-permute-start.11 = (f32[216,128]{1,0:T(8,128)S(1)}, f32[216,128]{1,0:T(8,128)S(1)}, u32[]{:S(2)}, u32[]{:S(2)}) collective-permute-start(f32[216,128]{1,0:T(8,128)S(1)} %get-tuple-element.32), channel_id=1, source_target_pairs={{12,20},{20,12},{8,16},{16,8},{28,36},{36,28},{24,32},{32,24},{44,... | collective-permute-start | bytes 331784 | tf_op jit(solution)/shard_map/ppermute | solution.py:478
  41.1 6.9 %collective-permute-start.7 = (f32[216,128]{1,0:T(8,128)S(1)}, f32[216,128]{1,0:T(8,128)S(1)}, u32[]{:S(2)}, u32[]{:S(2)}) collective-permute-start(f32[216,128]{1,0:T(8,128)S(1)} %get-tuple-element.30), channel_id=1, source_target_pairs={{0,4},{4,0},{8,12},{12,8},{16,20},{20,16},{24,28},{28,24},{32,36},... | collective-permute-start | bytes 331784 | tf_op jit(solution)/shard_map/ppermute | solution.py:478
  48.1 1.5 %collective-permute-start.8 = (f32[216,128]{1,0:T(8,128)S(1)}, f32[216,128]{1,0:T(8,128)S(1)}, u32[]{:S(2)}, u32[]{:S(2)}) collective-permute-start(f32[216,128]{1,0:T(8,128)S(1)} %get-tuple-element.31), channel_id=1, source_target_pairs={{0,8},{4,12},{8,0},{12,4},{16,24},{20,28},{24,16},{28,20},{32,40},... | collective-permute-start | bytes 331784 | tf_op jit(solution)/shard_map/ppermute | solution.py:478
  49.6 2.0 %collective-permute-done.11.r4 = f32[216,128]{1,0:T(8,128)S(1)} collective-permute-done((f32[216,128]{1,0:T(8,128)S(1)}, f32[216,128]{1,0:T(8,128)S(1)}, u32[]{:S(2)}, u32[]{:S(2)}) %collective-permute-start.11) | collective-permute-done | bytes 110624 | tf_op jit(solution)/shard_map/ppermute | solution.py:478
  51.6 3.1 %collective-permute-done.8.r1 = f32[216,128]{1,0:T(8,128)S(1)} collective-permute-done((f32[216,128]{1,0:T(8,128)S(1)}, f32[216,128]{1,0:T(8,128)S(1)}, u32[]{:S(2)}, u32[]{:S(2)}) %collective-permute-start.8) | collective-permute-done | bytes 110624 | tf_op jit(solution)/shard_map/ppermute | solution.py:478
  56.0 22.6 %shard_map.98 = (f32[6160,128]{1,0:T(8,128)S(1)}, f32[192,128]{1,0:T(8,128)S(1)}) custom-call(s32[13]{0:T(128)S(1)} %copy-done.8, f32[6160,128]{1,0:T(8,128)S(1)} %get-tuple-element.26.ext, f32[192,128]{1,0:T(8,128)S(1)} %get-tuple-element.27.own, f32[192,128]{1,0:T(8,128)S(1)} %get-tuple-element.28.og_ext, f32[72,128]{1,0:T(8,128)S(1)} %get-tuple-element.29.stat, ...), custom_call_target="tpu_custom_call" | custom-call | tf_op jit(solution)/shard_map/pallas_call | solution.py:402
  78.6 1.5 %collective-permute-start.13 = (f32[192,128]{1,0:T(8,128)S(1)}, f32[192,128]{1,0:T(8,128)S(1)}, u32[]{:S(2)}, u32[]{:S(2)}) collective-permute-start(f32[192,128]{1,0:T(8,128)S(1)} %get-tuple-element.35.own), channel_id=1, source_target_pairs={{0,4},{4,0},{8,12},{12,8},{16,20},{20,16},{24,28},{28,24},{32,36},... | collective-permute-start | bytes 294920 | tf_op jit(solution)/shard_map/ppermute | solution.py:483
  82.1 4.4 %collective-permute-start.16 = (f32[192,128]{1,0:T(8,128)S(1)}, f32[192,128]{1,0:T(8,128)S(1)}, u32[]{:S(2)}, u32[]{:S(2)}) collective-permute-start(f32[192,128]{1,0:T(8,128)S(1)} %get-tuple-element.35.own), channel_id=1, source_target_pairs={{12,16},{16,12},{8,20},{20,8},{28,32},{32,28},{24,36},{36,24},{44,... | collective-permute-start | bytes 294920 | tf_op jit(solution)/shard_map/ppermute | solution.py:483
  86.5 4.8 %collective-permute-start.17 = (f32[192,128]{1,0:T(8,128)S(1)}, f32[192,128]{1,0:T(8,128)S(1)}, u32[]{:S(2)}, u32[]{:S(2)}) collective-permute-start(f32[192,128]{1,0:T(8,128)S(1)} %get-tuple-element.35.own), channel_id=1, source_target_pairs={{12,20},{20,12},{8,16},{16,8},{28,36},{36,28},{24,32},{32,24},{44,... | collective-permute-start | bytes 294920 | tf_op jit(solution)/shard_map/ppermute | solution.py:483
  91.4 6.3 %collective-permute-done.17.s4 = f32[192,128]{1,0:T(8,128)S(1)} collective-permute-done((f32[192,128]{1,0:T(8,128)S(1)}, f32[192,128]{1,0:T(8,128)S(1)}, u32[]{:S(2)}, u32[]{:S(2)}) %collective-permute-start.17) | collective-permute-done | bytes 98336 | tf_op jit(solution)/shard_map/ppermute | solution.py:483
  98.5 17.6 %shard_map.99 = (f32[4096,128]{1,0:T(8,128)}, f32[256,128]{1,0:T(8,128)S(1)}) custom-call(s32[13]{0:T(128)S(1)} %copy-done.8, f32[6160,128]{1,0:T(8,128)S(1)} %get-tuple-element.34.ext, f32[192,128]{1,0:T(8,128)S(1)} %get-tuple-element.35.own, f32[192,128]{1,0:T(8,128)S(1)} %get-tuple-element.28.og_ext, f32[72,128]{1,0:T(8,128)S(1)} %get-tuple-element.29.stat, ...), custom_call_target="tpu_custom_call" | custom-call | tf_op jit(solution)/shard_map/pallas_call | solution.py:402
  116.2 1.4 %collective-permute-start.19 = (f32[256,128]{1,0:T(8,128)S(1)}, f32[256,128]{1,0:T(8,128)S(1)}, u32[]{:S(2)}, u32[]{:S(2)}) collective-permute-start(f32[256,128]{1,0:T(8,128)S(1)} %get-tuple-element.37), channel_id=1, source_target_pairs={{0,12},{4,8},{8,4},{12,0},{16,28},{20,24},{24,20},{28,16},{32,44},... | collective-permute-start | bytes 393224 | tf_op jit(solution)/shard_map/ppermute | solution.py:491
  117.6 3.0 %collective-permute-start.20 = (f32[256,128]{1,0:T(8,128)S(1)}, f32[256,128]{1,0:T(8,128)S(1)}, u32[]{:S(2)}, u32[]{:S(2)}) collective-permute-start(f32[256,128]{1,0:T(8,128)S(1)} %get-tuple-element.37), channel_id=1, source_target_pairs={{0,8},{4,12},{8,0},{12,4},{16,24},{20,28},{24,16},{28,20},{32,40},... | collective-permute-start | bytes 393224 | tf_op jit(solution)/shard_map/ppermute | solution.py:491
  (51 shorter events, 15.5 us)
Async XLA Ops:
  3.0 22.9 %copy-start.1 = (f32[4,64,16,128]{3,2,1,0:T(8,128)S(1)}, f32[4,64,16,128]{3,2,1,0:T(8,128)}, u32[]{:S(2)}) copy-start(f32[4,64,16,128]{3,2,1,0:T(8,128)} %param.8) | copy-start | bytes 6291460
  4.9 21.0 %collective-permute-start = (f32[1024,128]{1,0:T(8,128)}, f32[1024,128]{1,0:T(8,128)S(1)}, u32[]{:S(2)}, u32[]{:S(2)}) collective-permute-start(f32[1024,128]{1,0:T(8,128)} %get-tuple-element.20), channel_id=1, source_target_pairs={{0,1},{1,0},{2,3},{3,2},{4,5},{5,4},{6,7},{7,6},{8,9},{9,8},{10,11... | collective-permute-start | bytes 1572872 | tf_op jit(solution)/shard_map/ppermute | solution.py:461
  4.9 21.0 %collective-permute-start.1 = (f32[1024,128]{1,0:T(8,128)}, f32[1024,128]{1,0:T(8,128)S(1)}, u32[]{:S(2)}, u32[]{:S(2)}) collective-permute-start(f32[1024,128]{1,0:T(8,128)} %get-tuple-element.21), channel_id=1, source_target_pairs={{0,3},{1,2},{2,1},{3,0},{4,7},{5,6},{6,5},{7,4},{8,11},{9,10},{10,... | collective-permute-start | bytes 1572872 | tf_op jit(solution)/shard_map/ppermute | solution.py:462
  6.6 6.4 %collective-permute-start.2 = (f32[256,128]{1,0:T(8,128)}, f32[256,128]{1,0:T(8,128)S(1)}, u32[]{:S(2)}, u32[]{:S(2)}) collective-permute-start(f32[256,128]{1,0:T(8,128)} %bitcast.29), channel_id=1, source_target_pairs={{0,4},{4,0},{8,12},{12,8},{16,20},{20,16},{24,28},{28,24},{32,36},... | collective-permute-start | bytes 393224 | tf_op jit(solution)/shard_map/ppermute | solution.py:463
  7.2 8.8 %collective-permute-start.3 = (f32[256,128]{1,0:T(8,128)}, f32[256,128]{1,0:T(8,128)S(1)}, u32[]{:S(2)}, u32[]{:S(2)}) collective-permute-start(f32[256,128]{1,0:T(8,128)} %bitcast.30), channel_id=1, source_target_pairs={{0,8},{4,12},{8,0},{12,4},{16,24},{20,28},{24,16},{28,20},{32,40},... | collective-permute-start | bytes 393224 | tf_op jit(solution)/shard_map/ppermute | solution.py:463
  9.5 7.9 %collective-permute-start.4 = (f32[256,128]{1,0:T(8,128)}, f32[256,128]{1,0:T(8,128)S(1)}, u32[]{:S(2)}, u32[]{:S(2)}) collective-permute-start(f32[256,128]{1,0:T(8,128)} %bitcast.31), channel_id=1, source_target_pairs={{0,12},{4,8},{8,4},{12,0},{16,28},{20,24},{24,20},{28,16},{32,44},... | collective-permute-start | bytes 393224 | tf_op jit(solution)/shard_map/ppermute | solution.py:463
  22.5 1.2 collective-permute-start.5
  22.6 3.3 %collective-permute-start.6 = (f32[44,128]{1,0:T(8,128)S(1)}, f32[44,128]{1,0:T(8,128)S(1)}, u32[]{:S(2)}, u32[]{:S(2)}) collective-permute-start(f32[44,128]{1,0:T(8,128)S(1)} %get-tuple-element.25), channel_id=1, source_target_pairs={{0,3},{1,2},{2,1},{3,0},{4,7},{5,6},{6,5},{7,4},{8,11},{9,10},{10,... | collective-permute-start | bytes 67592 | tf_op jit(solution)/shard_map/ppermute | solution.py:470
  31.3 18.3 %collective-permute-start.10 = (f32[216,128]{1,0:T(8,128)S(1)}, f32[216,128]{1,0:T(8,128)S(1)}, u32[]{:S(2)}, u32[]{:S(2)}) collective-permute-start(f32[216,128]{1,0:T(8,128)S(1)} %get-tuple-element.32), channel_id=1, source_target_pairs={{12,16},{16,12},{8,20},{20,8},{28,32},{32,28},{24,36},{36,24},{44,... | collective-permute-start | bytes 331784 | tf_op jit(solution)/shard_map/ppermute | solution.py:478
  39.5 12.1 %collective-permute-start.11 = (f32[216,128]{1,0:T(8,128)S(1)}, f32[216,128]{1,0:T(8,128)S(1)}, u32[]{:S(2)}, u32[]{:S(2)}) collective-permute-start(f32[216,128]{1,0:T(8,128)S(1)} %get-tuple-element.32), channel_id=1, source_target_pairs={{12,20},{20,12},{8,16},{16,8},{28,36},{36,28},{24,32},{32,24},{44,... | collective-permute-start | bytes 331784 | tf_op jit(solution)/shard_map/ppermute | solution.py:478
  41.1 10.4 %collective-permute-start.12 = (f32[216,128]{1,0:T(8,128)S(1)}, f32[216,128]{1,0:T(8,128)S(1)}, u32[]{:S(2)}, u32[]{:S(2)}) collective-permute-start(f32[216,128]{1,0:T(8,128)S(1)} %get-tuple-element.33), channel_id=1, source_target_pairs={{12,24},{24,12},{4,16},{16,4},{28,40},{40,28},{20,32},{32,20},{44,... | collective-permute-start | bytes 331784 | tf_op jit(solution)/shard_map/ppermute | solution.py:478
  41.1 10.4 %collective-permute-start.7 = (f32[216,128]{1,0:T(8,128)S(1)}, f32[216,128]{1,0:T(8,128)S(1)}, u32[]{:S(2)}, u32[]{:S(2)}) collective-permute-start(f32[216,128]{1,0:T(8,128)S(1)} %get-tuple-element.30), channel_id=1, source_target_pairs={{0,4},{4,0},{8,12},{12,8},{16,20},{20,16},{24,28},{28,24},{32,36},... | collective-permute-start | bytes 331784 | tf_op jit(solution)/shard_map/ppermute | solution.py:478
  48.1 6.7 %collective-permute-start.8 = (f32[216,128]{1,0:T(8,128)S(1)}, f32[216,128]{1,0:T(8,128)S(1)}, u32[]{:S(2)}, u32[]{:S(2)}) collective-permute-start(f32[216,128]{1,0:T(8,128)S(1)} %get-tuple-element.31), channel_id=1, source_target_pairs={{0,8},{4,12},{8,0},{12,4},{16,24},{20,28},{24,16},{28,20},{32,40},... | collective-permute-start | bytes 331784 | tf_op jit(solution)/shard_map/ppermute | solution.py:478
  49.6 6.4 %collective-permute-start.9 = (f32[216,128]{1,0:T(8,128)S(1)}, f32[216,128]{1,0:T(8,128)S(1)}, u32[]{:S(2)}, u32[]{:S(2)}) collective-permute-start(f32[216,128]{1,0:T(8,128)S(1)} %get-tuple-element.31), channel_id=1, source_target_pairs={{0,12},{4,8},{8,4},{12,0},{16,28},{20,24},{24,20},{28,16},{32,44},... | collective-permute-start | bytes 331784 | tf_op jit(solution)/shard_map/ppermute | solution.py:478
  78.5 47.1 %copy-start.3 = (f32[4,64,1,128]{3,2,1,0:T(1,128)S(1)}, f32[4,64,1,128]{3,2,1,0:T(1,128)}, u32[]{:S(2)}) copy-start(f32[4,64,1,128]{3,2,1,0:T(1,128)} %param.12) | copy-start | bytes 393220
  78.6 12.8 %collective-permute-start.13 = (f32[192,128]{1,0:T(8,128)S(1)}, f32[192,128]{1,0:T(8,128)S(1)}, u32[]{:S(2)}, u32[]{:S(2)}) collective-permute-start(f32[192,128]{1,0:T(8,128)S(1)} %get-tuple-element.35.own), channel_id=1, source_target_pairs={{0,4},{4,0},{8,12},{12,8},{16,20},{20,16},{24,28},{28,24},{32,36},... | collective-permute-start | bytes 294920 | tf_op jit(solution)/shard_map/ppermute | solution.py:483
  80.0 11.3 %collective-permute-start.14 = (f32[192,128]{1,0:T(8,128)S(1)}, f32[192,128]{1,0:T(8,128)S(1)}, u32[]{:S(2)}, u32[]{:S(2)}) collective-permute-start(f32[192,128]{1,0:T(8,128)S(1)} %get-tuple-element.35.own), channel_id=1, source_target_pairs={{0,8},{4,12},{8,0},{12,4},{16,24},{20,28},{24,16},{28,20},{32,40},... | collective-permute-start | bytes 294920 | tf_op jit(solution)/shard_map/ppermute | solution.py:483
  81.2 10.2 %collective-permute-start.15 = (f32[192,128]{1,0:T(8,128)S(1)}, f32[192,128]{1,0:T(8,128)S(1)}, u32[]{:S(2)}, u32[]{:S(2)}) collective-permute-start(f32[192,128]{1,0:T(8,128)S(1)} %get-tuple-element.35.own), channel_id=1, source_target_pairs={{0,12},{4,8},{8,4},{12,0},{16,28},{20,24},{24,20},{28,16},{32,44},... | collective-permute-start | bytes 294920 | tf_op jit(solution)/shard_map/ppermute | solution.py:483
  82.1 9.2 %collective-permute-start.16 = (f32[192,128]{1,0:T(8,128)S(1)}, f32[192,128]{1,0:T(8,128)S(1)}, u32[]{:S(2)}, u32[]{:S(2)}) collective-permute-start(f32[192,128]{1,0:T(8,128)S(1)} %get-tuple-element.35.own), channel_id=1, source_target_pairs={{12,16},{16,12},{8,20},{20,8},{28,32},{32,28},{24,36},{36,24},{44,... | collective-permute-start | bytes 294920 | tf_op jit(solution)/shard_map/ppermute | solution.py:483
  86.5 11.2 %collective-permute-start.17 = (f32[192,128]{1,0:T(8,128)S(1)}, f32[192,128]{1,0:T(8,128)S(1)}, u32[]{:S(2)}, u32[]{:S(2)}) collective-permute-start(f32[192,128]{1,0:T(8,128)S(1)} %get-tuple-element.35.own), channel_id=1, source_target_pairs={{12,20},{20,12},{8,16},{16,8},{28,36},{36,28},{24,32},{32,24},{44,... | collective-permute-start | bytes 294920 | tf_op jit(solution)/shard_map/ppermute | solution.py:483
  91.3 7.2 %collective-permute-start.18 = (f32[192,128]{1,0:T(8,128)S(1)}, f32[192,128]{1,0:T(8,128)S(1)}, u32[]{:S(2)}, u32[]{:S(2)}) collective-permute-start(f32[192,128]{1,0:T(8,128)S(1)} %get-tuple-element.35.own), channel_id=1, source_target_pairs={{12,24},{24,12},{4,16},{16,4},{28,40},{40,28},{20,32},{32,20},{44,... | collective-permute-start | bytes 294920 | tf_op jit(solution)/shard_map/ppermute | solution.py:483
  116.2 8.2 %collective-permute-start.19 = (f32[256,128]{1,0:T(8,128)S(1)}, f32[256,128]{1,0:T(8,128)S(1)}, u32[]{:S(2)}, u32[]{:S(2)}) collective-permute-start(f32[256,128]{1,0:T(8,128)S(1)} %get-tuple-element.37), channel_id=1, source_target_pairs={{0,12},{4,8},{8,4},{12,0},{16,28},{20,24},{24,20},{28,16},{32,44},... | collective-permute-start | bytes 393224 | tf_op jit(solution)/shard_map/ppermute | solution.py:491
  117.6 6.8 %collective-permute-start.20 = (f32[256,128]{1,0:T(8,128)S(1)}, f32[256,128]{1,0:T(8,128)S(1)}, u32[]{:S(2)}, u32[]{:S(2)}) collective-permute-start(f32[256,128]{1,0:T(8,128)S(1)} %get-tuple-element.37), channel_id=1, source_target_pairs={{0,8},{4,12},{8,0},{12,4},{16,24},{20,28},{24,16},{28,20},{32,40},... | collective-permute-start | bytes 393224 | tf_op jit(solution)/shard_map/ppermute | solution.py:491
  120.6 5.0 %collective-permute-start.21 = (f32[256,128]{1,0:T(8,128)S(1)}, f32[256,128]{1,0:T(8,128)S(1)}, u32[]{:S(2)}, u32[]{:S(2)}) collective-permute-start(f32[256,128]{1,0:T(8,128)S(1)} %get-tuple-element.37), channel_id=1, source_target_pairs={{0,4},{4,0},{8,12},{12,8},{16,20},{20,16},{24,28},{28,24},{32,36},... | collective-permute-start | bytes 393224 | tf_op jit(solution)/shard_map/ppermute | solution.py:491
  (7 other events, 8.6 us)

commit v2 on v0

v2 whole, which is shorter than its diff:
```python
import jax
import jax.numpy as jnp
from jax import lax
from jax.experimental import pallas as pl
from jax.experimental.pallas import tpu as pltpu
from jax.sharding import PartitionSpec as P

FIELDS = 4
LEVELS = 64
ROWS = 16
COLS = 128
HALO = 4
EXT = ROWS + 2 * HALO
YB = 3
YC = 8
KB = 4
KA = 16
BLOCKS = YB * FIELDS * KB
PAD = 8
STATE_ROWS = BLOCKS * COLS + 2 * PAD
SIDE_ROWS = 4 * BLOCKS + 16
WIDE_ROWS = FIELDS * LEVELS * HALO
REACH = 3
SLOTS = 2 * REACH + 1
GROUP = 4
VMEM_BYTES = 44 * 1024 * 1024

TIME_STEP = 0.1
TURN = 0.05
FEEDBACK = 0.5
HIGHEST = lax.Precision.HIGHEST

S_EVEN, S_TOP, S_BOTTOM, S_PBX, S_SLOT, S_XEVEN, S_LOW, S_PB, S_ME = 0, 1, 2, 3, 4, 10, 11, 12, 13


def lanes(rows=8):
    return lax.broadcasted_iota(jnp.int32, (rows, COLS), 1)


def sublanes(rows=8):
    return lax.broadcasted_iota(jnp.int32, (rows, COLS), 0)


def wide(row):
    return jnp.broadcast_to(row, (8, COLS))


def unrolled(count, step, body):
    def several(i, carry):
        for j in range(step):
            body(i * step + j)
        return carry

    lax.fori_loop(0, count // step, several, 0)


def rows_kernel(sc, far_nest, mask, mixing, pay1, pay2, nest, wet, mix, sems):
    share = LEVELS * ROWS
    copies = [
        pltpu.make_async_copy(far_nest.at[pl.ds(f * share, share)], nest.at[pl.ds(f * share, share)], sems.at[f])
        for f in range(FIELDS)
    ]
    copies += [
        pltpu.make_async_copy(mask, wet, sems.at[FIELDS]),
        pltpu.make_async_copy(mixing, mix, sems.at[FIELDS + 1]),
    ]
    for copy in copies:
        copy.start()
    even = sc[S_EVEN] == 1
    first = jnp.where(even, ROWS - HALO, 0)
    second = jnp.where(even, 0, ROWS - HALO)
    for f in range(FIELDS):
        copies[f].wait()

        def move(i, f=f):
            at, to = (f * LEVELS + i) * ROWS, (f * LEVELS + i) * HALO
            pay1[pl.ds(to, HALO), :] = nest[pl.ds(at + first, HALO), :]
            pay2[pl.ds(to, HALO), :] = nest[pl.ds(at + second, HALO), :]

        unrolled(LEVELS, 16, move)
    copies[FIELDS].wait()
    copies[FIELDS + 1].wait()
    for i, plane in enumerate((wet[...].astype(jnp.float32), mix[...])):
        low, high = plane[:HALO], plane[ROWS - HALO :]
        pay1[pl.ds(WIDE_ROWS + i * HALO, HALO), :] = jnp.where(even, high, low)
        pay2[pl.ds(WIDE_ROWS + i * HALO, HALO), :] = jnp.where(even, low, high)


def table_kernel(coarse, face, idx, weight, table, offs, kept, spread, near, face_in, idx_in, weight_in, sems):
    pairs = ((coarse, near), (face, face_in), (idx, idx_in), (weight, weight_in))
    copies = [pltpu.make_async_copy(far, here, sems.at[i]) for i, (far, here) in enumerate(pairs)]
    for copy in copies:
        copy.start()
    for copy in copies:
        copy.wait()
    kept[...] = near[...]

    def upright(small):
        spread[pl.ds(0, 8), :] = jnp.zeros((8, COLS), jnp.float32)
        spread[pl.ds(0, small.shape[0]), 0:ROWS] = small.astype(jnp.float32)
        return spread[pl.ds(0, 8), :].T[:ROWS]

    face = upright(face_in[...])
    idx = upright(idx_in[...])
    weight = upright(weight_in[...])
    offs[pl.ds(0, ROWS), :] = jnp.broadcast_to(face[:, 0:1], (ROWS, COLS))
    offs[pl.ds(ROWS, ROWS), :] = jnp.broadcast_to(face[:, 1:2], (ROWS, COLS))
    cell = lanes(ROWS).astype(jnp.float32)
    spread[...] = jnp.zeros_like(spread)
    for side in range(2):
        total = jnp.zeros((ROWS, 1), jnp.float32)
        values = jnp.zeros((ROWS, COLS), jnp.float32)
        for j in range(4):
            c = side * 4 + j
            w = weight[:, c : c + 1]
            total = total + w
            values = values + jnp.where(idx[:, c : c + 1] == cell, w, 0.0)
        spread[pl.ds(side * EXT + HALO, ROWS), :] = values / total
    for side in range(2):
        for yb in range(YB):
            table[pl.ds(side * EXT + yb * YC, YC), :] = spread[pl.ds(side * EXT + yb, YC, stride=YB), :]


def open_kernel(sc, own, got1, got2, got3, table, offs, og, chosen):
    og[pl.ds(2 * BLOCKS, 2 * ROWS), :] = offs[...]
    pbx = sc[S_PBX]
    value = own[...]
    for code, got in ((1, got1), (2, got2), (3, got3)):
        value = jnp.where(pbx == code, got[...], value)
    chosen[...] = value
    rows = []
    for f in range(FIELDS):
        for kb in range(KB):
            for a in range(2):
                rows.append(chosen[pl.ds(f * LEVELS + kb + a * 8 * KB, 8, stride=KB), :])
    weights = jnp.concatenate([table[...], jnp.zeros((COLS - 2 * EXT, COLS), jnp.float32)], axis=0)
    values = lax.dot_general(
        jnp.concatenate(rows, axis=0), weights, (((1,), (1,)), ((), ())),
        precision=HIGHEST, preferred_element_type=jnp.float32,
    )
    shift = (lanes() // KA - sublanes()) % 8
    for half in range(2):
        upright = values[half * COLS : (half + 1) * COLS].T
        for i in range(2 * YB):
            part = upright[i * YC : (i + 1) * YC]
            value = part
            for d in range(1, 8):
                value = jnp.where(shift == d, pltpu.roll(pltpu.roll(part, KA * d, 1), 8 - d, 0), value)
            og[pl.ds(i * 16 + half * 8, 8), :] = value


def columns_of(state, edges):
    for c, x in enumerate((COLS - 1, 0, COLS - 2, 1)):
        for i in range(BLOCKS // 8):
            edges[pl.ds(c * BLOCKS + 8 * i, 8), :] = state[pl.ds(PAD + 8 * i * COLS + x, 8, stride=COLS), :]


def halos(sc, one, two):
    even = sc[S_EVEN] == 1
    top = jnp.where(sc[S_TOP] == 1, jnp.where(even, two, one), 0.0)
    bottom = jnp.where(sc[S_BOTTOM] == 1, jnp.where(even, one, two), 0.0)
    return top, bottom


def turn_kernel(sc, nest, wide1, wide2, far_mask, far_mixing, state, coef, edges, ext, mask, mixing, sems):
    copies = [
        pltpu.make_async_copy(far_mask, mask, sems.at[0]),
        pltpu.make_async_copy(far_mixing, mixing, sems.at[1]),
    ]
    for copy in copies:
        copy.start()
    pad = jnp.zeros((PAD, COLS), jnp.float32)
    state[pl.ds(0, PAD), :] = pad
    state[pl.ds(STATE_ROWS - PAD, PAD), :] = pad
    even = sc[S_EVEN] == 1
    top_in, bottom_in = sc[S_TOP] == 1, sc[S_BOTTOM] == 1
    for yb in range(YB):

        def tile(i, yb=yb):
            base = (i // KB) * LEVELS + i % KB
            rows = []
            for yc in range(YC):
                r = YB * yc + yb
                for a in range(2):
                    level = base + a * 8 * KB
                    if HALO <= r < HALO + ROWS:
                        rows.append(nest[pl.ds(level * ROWS + r - HALO, 8, stride=KB * ROWS), :])
                    else:
                        at = pl.ds(level * HALO + r % ROWS % HALO, 8, stride=KB * HALO)
                        one, two = wide1[at, :], wide2[at, :]
                        if r < HALO:
                            rows.append(jnp.where(top_in, jnp.where(even, two, one), 0.0))
                        else:
                            rows.append(jnp.where(bottom_in, jnp.where(even, one, two), 0.0))
            at = pl.multiple_of(PAD + (yb * 16 + i) * COLS, 8)
            state[pl.ds(at, COLS), :] = jnp.concatenate(rows, axis=0).T

        unrolled(16, TILES, tile)
    for copy in copies:
        copy.wait()
    for i, plane in enumerate((mask[...].astype(jnp.float32), mixing[...])):
        at = pl.ds(WIDE_ROWS + i * HALO, HALO)
        top, bottom = halos(sc, wide1[at, :], wide2[at, :])
        ext[pl.ds(i * EXT, HALO), :] = top
        ext[pl.ds(i * EXT + HALO, ROWS), :] = plane
        ext[pl.ds(i * EXT + HALO + ROWS, HALO), :] = bottom
    for yb in range(YB):
        for i in range(2):
            rows = [
                jnp.broadcast_to(ext[pl.ds(i * EXT + YB * yc + yb, 1), :], (KA, COLS)) for yc in range(YC)
            ]
            coef[pl.ds((i * YB + yb) * COLS, COLS), :] = jnp.concatenate(rows, axis=0).T
    columns_of(state, edges)


def message_kernel(sc, edges, og, edge1, edge2, coef, ogx, offv, msg_e, msg_o, msg_lo, msg_hi, left, right, ext):
    mine = sublanes() == lanes() // KA
    even = sc[S_EVEN] == 1
    for i in range(2):
        at = 2 * BLOCKS + i * ROWS
        one_low, one_high = edge1[pl.ds(at, HALO), :], edge1[pl.ds(at + ROWS - HALO, HALO), :]
        two_low, two_high = edge2[pl.ds(at, HALO), :], edge2[pl.ds(at + ROWS - HALO, HALO), :]
        ext[pl.ds(i * EXT, HALO), :] = jnp.where(even, two_high, one_high)
        ext[pl.ds(i * EXT + HALO, ROWS), :] = og[pl.ds(at, ROWS), :]
        ext[pl.ds(i * EXT + HALO + ROWS, HALO), :] = jnp.where(even, one_low, two_low)
        for yb in range(YB):
            away = ext[pl.ds(i * EXT + yb, YC, stride=YB), :]
            offv[pl.ds(i * YB + yb, 1), :] = jnp.sum(jnp.where(mine, away, 0.0), axis=0, keepdims=True)
    lane16 = lanes(16) // KA
    for side in range(2):
        tops, bottoms = [], []
        for yb in range(YB):
            rows = pl.ds((side * YB + yb) * 16, 16)
            top, bottom = halos(sc, edge1[rows, :], edge2[rows, :])
            tops.append(top)
            bottoms.append(bottom)
        for yb in range(YB):
            rows = pl.ds((side * YB + yb) * 16, 16)
            row = YB * lane16 + yb
            up = pltpu.roll(tops[(yb + 1) % YB], COLS - KA * (6 if yb == 2 else 5), 1)
            down = pltpu.roll(bottoms[(yb + 2) % YB], KA * (6 if yb == 0 else 5), 1)
            ogx[rows, :] = jnp.where(row < HALO, up, jnp.where(row >= HALO + ROWS, down, og[rows, :]))
    number = sc[S_PB].astype(jnp.float32)
    for ref, third, opened, x, off in ((right, 2, 1, COLS - 1, 1), (left, 3, 0, 0, 0)):
        ref[pl.ds(0, 2 * BLOCKS), :] = edges[pl.ds(0, 2 * BLOCKS), :]
        ref[pl.ds(2 * BLOCKS, BLOCKS), :] = edges[pl.ds(third * BLOCKS, BLOCKS), :]
        ref[pl.ds(3 * BLOCKS, BLOCKS), :] = ogx[pl.ds(opened * BLOCKS, BLOCKS), :]
        ref[pl.ds(4 * BLOCKS, 16), :] = jnp.zeros((16, COLS), jnp.float32) + number
        for i in range(2 * YB):
            ref[pl.ds(4 * BLOCKS + i, 1), :] = coef[pl.ds(i * COLS + x, 1), :]
        ref[pl.ds(4 * BLOCKS + 2 * YB, YB), :] = offv[pl.ds(off * YB, YB), :]
    x_even, low = sc[S_XEVEN] == 1, sc[S_LOW] == 1
    msg_e[...] = jnp.where(x_even, right[...], left[...])
    msg_o[...] = jnp.where(x_even, left[...], right[...])
    msg_lo[...] = jnp.where(low, right[...], left[...])
    msg_hi[...] = jnp.where(low, left[...], right[...])


def coefficients(wet, mix):
    kmix = wet * mix
    return kmix, wet - 4.0 * TIME_STEP * wet - 2.0 * kmix, TIME_STEP * wet, TURN * wet


def advance_edge(q, east, west, wet, mix):
    sub, lane = sublanes(), lanes() % KA
    new = []
    for yb in range(YB):
        kmix, centre, base, turn = coefficients(wide(wet[yb]), wide(mix[yb]))
        flow = q[yb][1]
        swapped = pltpu.roll(flow, 4, 0)
        cu = turn * jnp.where(sub < 4, flow, swapped)
        cv = turn * jnp.where(sub < 4, swapped, flow)
        pair = []
        for half in range(2):
            c = q[yb][half]
            above = jnp.where(
                sub % KB >= 1, pltpu.roll(c, 1, 0),
                jnp.where(lane == 0, c, pltpu.roll(pltpu.roll(c, 5, 0), 1, 1)),
            )
            below = jnp.where(
                sub % KB < KB - 1, pltpu.roll(c, 7, 0),
                jnp.where(lane == KA - 1, c, pltpu.roll(pltpu.roll(c, 3, 0), COLS - 1, 1)),
            )
            south = q[yb - 1][half] if yb > 0 else pltpu.roll(q[YB - 1][half], KA, 1)
            north = q[yb + 1][half] if yb < YB - 1 else pltpu.roll(q[0][half], COLS - KA, 1)
            value = (centre * c + (base - cu) * east[yb][half]) + ((base + cu) * west[yb][half] + (base - cv) * north)
            value = value + ((base + cv) * south + kmix * (above + below))
            if half == 1:
                value = value + jnp.where(sub < 4, cv, -cu)
            pair.append(value)
        new.append(pair)
    return new


def ghosts(side, ogx, offv, west0, east0, west1, east1):
    def column(slot, c):
        return [
            [side[pl.ds(slot * SIDE_ROWS + c * BLOCKS + yb * 16 + half * 8, 8), :] for half in range(2)]
            for yb in range(YB)
        ]

    def fact(slot, i):
        return [side[pl.ds(slot * SIDE_ROWS + 4 * BLOCKS + i * YB + yb, 1), :] for yb in range(YB)]

    def pick(away, choices, value):
        for e, choice in choices:
            value = [
                [jnp.where(wide(away[yb]) == e, choice[yb][half], value[yb][half]) for half in range(2)]
                for yb in range(YB)
            ]
        return value

    def put(ref, value):
        for yb in range(YB):
            for half in range(2):
                ref[pl.ds(yb * 16 + half * 8, 8), :] = value[yb][half]

    for sign, first, second in ((-1, west0, west1), (1, east0, east1)):
        which = 0 if sign < 0 else 1
        away = [offv[pl.ds(which * YB + yb, 1), :] for yb in range(YB)]
        opened = [
            [ogx[pl.ds(which * BLOCKS + yb * 16 + half * 8, 8), :] for half in range(2)] for yb in range(YB)
        ]
        reach = range(1, REACH + 1)
        put(first, pick(away, [(d, column(REACH + sign * d, which)) for d in reach], opened))
        later = opened
        for d in reach:
            slot = REACH + sign * d
            outer = pick(
                fact(slot, 2), [(e, column(slot - sign * e, 1 - which)) for e in reach], column(slot, 3)
            )
            inner = column(slot, 2)
            east, west = (outer, inner) if sign < 0 else (inner, outer)
            new = advance_edge(column(slot, which), east, west, fact(slot, 0), fact(slot, 1))
            later = pick(away, [(d, new)], later)
        put(second, later)


def substep(src, dst, west_ghost, east_ghost, coef):
    sub, ka = sublanes(), lanes() % KA

    def block(yb, f, kb):
        return (yb * FIELDS + f) * KB + kb

    for yb in range(YB):

        def group(xg, first, last, yb=yb):
            x = xg * 8

            def load(yb, f, kb, shift=0):
                return src[pl.ds(PAD + block(yb, f, kb) * COLS + x + shift, 8), :]

            kmix, centre, base, turn = coefficients(
                coef[pl.ds(yb * COLS + x, 8), :], coef[pl.ds((YB + yb) * COLS + x, 8), :]
            )
            q = [[load(yb, f, kb) for kb in range(KB)] for f in range(FIELDS)]
            for kb in range(KB):
                cu, cv = turn * q[2][kb], turn * q[3][kb]
                ke, kw, kn, ks = base - cu, base + cu, base - cv, base + cv
                for f in range(FIELDS):
                    c = q[f][kb]
                    b = block(yb, f, kb)
                    west, east = load(yb, f, kb, -1), load(yb, f, kb, 1)
                    if first:
                        west = jnp.where(sub == 0, wide(west_ghost[pl.ds(b, 1), :]), west)
                    if last:
                        east = jnp.where(sub == 7, wide(east_ghost[pl.ds(b, 1), :]), east)
                    south = load(yb - 1, f, kb) if yb > 0 else pltpu.roll(load(YB - 1, f, kb), KA, 1)
                    north = load(yb + 1, f, kb) if yb < YB - 1 else pltpu.roll(load(0, f, kb), COLS - KA, 1)
                    above = q[f][kb - 1] if kb > 0 else jnp.where(ka == 0, c, pltpu.roll(q[f][KB - 1], 1, 1))
                    below = q[f][kb + 1] if kb < KB - 1 else jnp.where(ka == KA - 1, c, pltpu.roll(q[f][0], COLS - 1, 1))
                    new = (centre * c + ke * east) + (kw * west + kn * north)
                    new = new + (ks * south + kmix * (above + below))
                    if f == 2:
                        new = new + cv
                    if f == 3:
                        new = new - cu
                    dst[pl.ds(PAD + b * COLS + x, 8), :] = new

        group(0, True, False)

        def body(i, carry, group=group):
            for j in range(UNROLL):
                group(1 + i * UNROLL + j, False, False)
            return carry

        lax.fori_loop(0, (COLS // 8 - 2) // UNROLL, body, 0)
        group(COLS // 8 - 1, False, True)


UNROLL = 2
TILES = 4


def clear_pads(*refs):
    for ref in refs:
        ref[pl.ds(0, PAD), :] = jnp.zeros((PAD, COLS), jnp.float32)
        ref[pl.ds(STATE_ROWS - PAD, PAD), :] = jnp.zeros((PAD, COLS), jnp.float32)


def first_kernel(
    sc, state, own, ogx, coef, offv, r0, r1, r2, r3, r4, r5, out, edges, side, mid, west0, east0, west1, east1
):
    clear_pads(mid, out)
    side[pl.ds(REACH * SIDE_ROWS, 2 * BLOCKS), :] = own[pl.ds(0, 2 * BLOCKS), :]
    for j, r in enumerate((r0, r1, r2, r3, r4, r5)):
        side[pl.ds(pl.multiple_of(sc[S_SLOT + j] * SIDE_ROWS, 8), SIDE_ROWS), :] = r[...]
    ghosts(side, ogx, offv, west0, east0, west1, east1)
    substep(state, mid, west0, east0, coef)
    substep(mid, out, west1, east1, coef)
    columns_of(out, edges)


def second_kernel(
    sc, state, own, ogx, coef, offv, r0, r1, r2, r3, r4, r5, s0, s1, s2, s3, s4, s5,
    out, means, blocks, side, mid, west0, east0, west1, east1, end, nat, sems,
):
    clear_pads(mid)
    side[pl.ds(REACH * SIDE_ROWS, 2 * BLOCKS), :] = own[pl.ds(0, 2 * BLOCKS), :]
    for j, (r, s) in enumerate(zip((r0, r1, r2, r3, r4, r5), (s0, s1, s2, s3, s4, s5))):
        slot = sc[S_SLOT + j]
        at = slot * SIDE_ROWS
        third = pl.multiple_of(jnp.where(slot > REACH, 3 * BLOCKS, 2 * BLOCKS), 8)
        side[pl.ds(pl.multiple_of(at, 8), 2 * BLOCKS), :] = s[pl.ds(0, 2 * BLOCKS), :]
        side[pl.ds(pl.multiple_of(at + 2 * BLOCKS, 8), BLOCKS), :] = s[pl.ds(third, BLOCKS), :]
        side[pl.ds(pl.multiple_of(at + 3 * BLOCKS, 8), BLOCKS + 16), :] = r[pl.ds(3 * BLOCKS, BLOCKS + 16), :]
    ghosts(side, ogx, offv, west0, east0, west1, east1)
    substep(state, mid, west0, east0, coef)
    substep(mid, end, west1, east1, coef)
    for j in range(3):
        blocks[pl.ds(j * 8, 8), :] = wide((r0, r1, r2)[j][pl.ds(SIDE_ROWS - 1, 1), :])
    share = LEVELS * ROWS
    copies = [
        pltpu.make_async_copy(nat.at[pl.ds(f * share, share)], out.at[pl.ds(f * share, share)], sems.at[f])
        for f in range(FIELDS)
    ]
    for f in range(FIELDS):
        for yb in range(YB):

            def tile(kb, yb=yb, f=f):
                base = f * LEVELS + kb
                block = (yb * FIELDS + f) * KB + kb
                rows = end[pl.ds(pl.multiple_of(PAD + block * COLS, 8), COLS), :].T
                for yc in range(YC):
                    r = YB * yc + yb - HALO
                    if 0 <= r < ROWS:
                        for a in range(2):
                            at = pl.ds((base + a * 8 * KB) * ROWS + r, 8, stride=KB * ROWS)
                            nat[at, :] = rows[yc * KA + 8 * a : yc * KA + 8 * a + 8]

            unrolled(KB, TILES, tile)
        copies[f].start()

    target = lanes(COLS)
    block = 64
    for b in range(FIELDS * LEVELS // block):
        total = jnp.zeros((block, COLS), jnp.float32)
        for a in range(4):
            rows = []
            for c in range(block // 8):
                at = (b * block + c * 8) * ROWS + 4 * a
                part = [nat[pl.ds(at + i, 8, stride=ROWS), :] for i in range(4)]
                rows.append((part[0] + part[1]) + (part[2] + part[3]))
            gather = jnp.where(a * 32 + sublanes(COLS) // 4 == target, 1.0 / 16.0, 0.0).astype(jnp.float32)
            total = total + lax.dot_general(
                jnp.concatenate(rows, axis=0), gather, (((1,), (0,)), ((), ())),
                precision=HIGHEST, preferred_element_type=jnp.float32,
            )
        means[pl.ds(b * block, block), :] = total
    for copy in copies:
        copy.wait()


def feedback_kernel(sc, coarse, means, got1, got2, got3, blocks, out):
    me = sc[S_ME].astype(jnp.float32)
    for i in range(FIELDS * LEVELS // 8):
        rows = pl.ds(i * 8, 8)
        value = means[rows, :]
        for j, got in enumerate((got1, got2, got3)):
            value = jnp.where(blocks[pl.ds(j * 8, 8), :] == me, got[rows, :], value)
        old = coarse[rows, :]
        out[rows, :] = old + FEEDBACK * (value - old)


def call(kernel, outs, scratch, *args, far=(), far_out=()):
    def spec(i, places, arg=None):
        if i in places:
            return pl.BlockSpec(memory_space=pltpu.HBM)
        small = arg is not None and arg.ndim == 1
        return pl.BlockSpec(memory_space=pltpu.SMEM if small else pltpu.VMEM)

    return pl.pallas_call(
        kernel,
        out_shape=[jax.ShapeDtypeStruct(s, jnp.float32) for s in outs],
        in_specs=[spec(i, far, a) for i, a in enumerate(args)],
        out_specs=[spec(i, far_out) for i in range(len(outs))],
        scratch_shapes=[pltpu.VMEM(s, jnp.float32) if isinstance(s, tuple) else s for s in scratch],
        compiler_params=pltpu.CompilerParams(vmem_limit_bytes=VMEM_BYTES),
    )(*args)


def per_device(nest_state, mixing, land_mask, face_off, parent_state, parent_block, interp_idx, interp_w):
    tiles = lax.axis_size("nest")
    blocks = lax.axis_size("parent")
    n = lax.axis_index("nest")
    p = lax.axis_index("parent")
    x = n % GROUP
    own_block = parent_block[0, 0]

    def inside(code):
        return [(s, s ^ code) for s in range(tiles)]

    def across(pairs):
        links = []
        for g in range(tiles // GROUP):
            for a, b in pairs:
                i, j = GROUP * g + a, (GROUP * (g + 1) + b) % tiles
                links += [(i, j), (j, i)]
        return links

    rows_1 = [(s, s ^ 1) for s in range(blocks)]
    rows_2 = [(s, ((s + 1) ^ 1) - 1) if 0 < s < blocks - 1 else (s, blocks - 1 - s) for s in range(blocks)]
    links = [
        inside(1), inside(2), inside(3),
        across([(3, 0), (2, 1)]), across([(3, 1), (2, 0)]), across([(3, 2), (1, 0)]),
    ]
    x_even, low = x % 2 == 0, x < 2
    rel = [
        jnp.where(x_even, 1, -1),
        jnp.where(low, 2, -2),
        3 - 2 * x,
        jnp.where(low, -1 - 2 * x, 7 - 2 * x),
        jnp.where(low, -2, 2),
        jnp.where(x_even, -3, 3),
    ]
    sc = jnp.stack(
        [
            (p % 2 == 0).astype(jnp.int32),
            (p > 0).astype(jnp.int32),
            (p < blocks - 1).astype(jnp.int32),
            own_block ^ n,
        ]
        + [REACH + r for r in rel]
        + [x_even.astype(jnp.int32), low.astype(jnp.int32), own_block, n]
    ).astype(jnp.int32)

    nest2 = nest_state.reshape(FIELDS * LEVELS * ROWS, COLS)
    coarse = parent_state.reshape(FIELDS * LEVELS, COLS)
    natural = (FIELDS * LEVELS * ROWS, COLS)
    rows, narrow = (WIDE_ROWS + 2 * HALO, COLS), (ROWS, COLS)
    pay1, pay2 = call(
        rows_kernel, [rows, rows],
        [natural, pltpu.VMEM(narrow, jnp.int32), pltpu.VMEM(narrow, jnp.float32), pltpu.SemaphoreType.DMA((6,))],
        sc, nest2, land_mask, mixing, far=(1, 2, 3),
    )
    wide1 = lax.ppermute(pay1, "parent", rows_1)
    wide2 = lax.ppermute(pay2, "parent", rows_2[1:-1])
    got = [lax.ppermute(coarse, "nest", links[i]) for i in range(3)]
    face, idx, weight, pay1 = lax.optimization_barrier(
        (face_off.T, interp_idx.transpose(1, 2, 0).reshape(8, ROWS), interp_w.transpose(1, 2, 0).reshape(8, ROWS), pay1)
    )
    coarse_rows = (FIELDS * LEVELS, COLS)
    table, offs, kept = call(
        table_kernel, [(2 * EXT, COLS), (2 * ROWS, COLS), coarse_rows],
        [(2 * EXT, COLS), coarse_rows, pltpu.VMEM((2, ROWS), jnp.int32), pltpu.VMEM((8, ROWS), jnp.int32),
         pltpu.VMEM((8, ROWS), jnp.float32), pltpu.SemaphoreType.DMA((4,))],
        coarse, face, idx, weight, far=(0, 1, 2, 3),
    )
    block, state_rows = (BLOCKS, COLS), (STATE_ROWS, COLS)
    (og,) = call(
        open_kernel, [(2 * BLOCKS + 2 * ROWS, COLS)], [coarse_rows], sc, kept, *got, table, offs
    )
    edge1 = lax.ppermute(og, "parent", rows_1)
    edge2 = lax.ppermute(og, "parent", rows_2)
    state, coef, edges = call(
        turn_kernel, [state_rows, (2 * YB * COLS, COLS), (4 * BLOCKS, COLS)],
        [(2 * EXT, COLS), pltpu.VMEM(narrow, jnp.int32), pltpu.VMEM(narrow, jnp.float32), pltpu.SemaphoreType.DMA((2,))],
        sc, nest2, wide1, wide2, land_mask, mixing, far=(4, 5),
    )
    side = (SIDE_ROWS, COLS)
    ogx, offv, msg_e, msg_o, msg_lo, msg_hi = call(
        message_kernel, [(2 * BLOCKS, COLS), (8, COLS)] + [side] * 4, [side, side, (2 * EXT, COLS)],
        sc, edges, og, edge1, edge2, coef,
    )
    msgs = [msg_e, msg_lo, msg_lo, msg_hi, msg_hi, msg_o]
    first = [lax.ppermute(m, "nest", link) for m, link in zip(msgs, links)]
    work = [(SLOTS * SIDE_ROWS, COLS), state_rows] + [block] * 4
    state, edges = call(
        first_kernel, [state_rows, (4 * BLOCKS, COLS)], work, sc, state, edges, ogx, coef, offv, *first
    )
    second = [lax.ppermute(edges, "nest", link) for link in links]
    new2, means, blocks = call(
        second_kernel, [natural, coarse_rows, (24, COLS)],
        work + [state_rows, natural, pltpu.SemaphoreType.DMA((FIELDS,))],
        sc, state, edges, ogx, coef, offv, *first, *second, far_out=(0,),
    )
    arrived = [lax.ppermute(means, "nest", links[i]) for i in range(3)]
    (parent_new,) = call(feedback_kernel, [coarse_rows], [], sc, kept, means, *arrived, blocks)
    return new2.reshape(nest_state.shape), parent_new.reshape(parent_state.shape)


def solution(mesh):
    return jax.shard_map(
        per_device,
        mesh=mesh,
        in_specs=(
            P(None, None, "parent", "nest"),
            P("parent", "nest"),
            P("parent", "nest"),
            P("parent", "nest"),
            P(None, None, "parent", "nest"),
            P("parent", "nest"),
            P("parent", "nest", None),
            P("parent", "nest", None),
        ),
        out_specs=(P(None, None, "parent", "nest"), P(None, None, "parent", "nest")),
        check_vma=False,
    )
```

time: 423 us -> 95.1 us (0.22)
  the two profiles are of different devices: /device:TPU:122 before, /device:TPU:2 now
where the time goes in v2:
time: 95.1 us; the launch traced here: 94.7 us
  starting transfers between devices  47.2 us (50%)
  Pallas kernels  24.2 us (25%)
  waiting for transfers between devices  15.8 us (17%)
  local copies, waits for them, and re-layouts  6.06 us (6%)
  between operations  1.48 us (2%)
    pallas_call x8, Pallas kernels, call(): pl.pallas_call(kernel, out_shape=[jax.ShapeDtypeStruct(s, jnp.float32) fo...  24.2 us
    ppermute x6, starting transfers between devices, per_device(): first = [lax.ppermute(m, 'nest', link) for m, link in zip(msgs, links)]  20 us
    ppermute x6, starting transfers between devices, per_device(): second = [lax.ppermute(edges, 'nest', link) for link in links]  14.8 us
    unnamed x16, local copies, waits for them, and re-layouts  5.97 us
    ppermute x6, waiting for transfers between devices, per_device(): second = [lax.ppermute(edges, 'nest', link) for link in links]  4.61 us
    ppermute x3, waiting for transfers between devices, per_device(): arrived = [lax.ppermute(means, 'nest', links[i]) for i in range(3)]  4.34 us
    ppermute x3, starting transfers between devices, per_device(): arrived = [lax.ppermute(means, 'nest', links[i]) for i in range(3)]  4.17 us
    ppermute x3, starting transfers between devices, per_device(): got = [lax.ppermute(coarse, 'nest', links[i]) for i in range(3)]  4.09 us
  transfers between devices with their start and end apart: 22, of which 10 were waited for; matrix products, arithmetic and copies ran while one was open for 0% of the time, Pallas kernels for 5%

profile of v2, /device:TPU:2, one launch (start us, length us, event | category | flops | bytes accessed | tf_op | source)
XLA Modules:
  0.0 94.7 jit_solution(9163181864235028754)
XLA Ops:
  1.4 1.6 %copy-done = f32[4,64,16,128]{3,2,1,0:T(8,128)S(1)} copy-done((f32[4,64,16,128]{3,2,1,0:T(8,128)S(1)}, f32[4,64,16,128]{3,2,1,0:T(8,128)}, u32[]{:S(2)}) %copy-start) | copy-done | bytes 2097176
  6.2 3.0 %collective-permute-start = (f32[1032,128]{1,0:T(8,128)S(1)}, f32[1032,128]{1,0:T(8,128)S(1)}, u32[]{:S(2)}, u32[]{:S(2)}) collective-permute-start(f32[1032,128]{1,0:T(8,128)S(1)} %get-tuple-element.24), channel_id=1, source_target_pairs={{0,1},{1,0},{2,3},{3,2},{4,5},{5,4},{6,7},{7,6},{8,9},{9,8},{10,11... | collective-permute-start | bytes 1585160 | tf_op jit(solution)/shard_map/ppermute | solution.py:556
  9.2 1.5 %collective-permute-start.4 = (f32[256,128]{1,0:T(8,128)}, f32[256,128]{1,0:T(8,128)S(1)}, u32[]{:S(2)}, u32[]{:S(2)}) collective-permute-start(f32[256,128]{1,0:T(8,128)} %bitcast.32), channel_id=1, source_target_pairs={{0,12},{4,8},{8,4},{12,0},{16,28},{20,24},{24,20},{28,16},{32,44},... | collective-permute-start | bytes 393224 | tf_op jit(solution)/shard_map/ppermute | solution.py:558
  11.8 1.5 %collective-permute-start.2 = (f32[256,128]{1,0:T(8,128)}, f32[256,128]{1,0:T(8,128)S(1)}, u32[]{:S(2)}, u32[]{:S(2)}) collective-permute-start(f32[256,128]{1,0:T(8,128)} %bitcast.34), channel_id=1, source_target_pairs={{0,4},{4,0},{8,12},{12,8},{16,20},{20,16},{24,28},{28,24},{32,36},... | collective-permute-start | bytes 393224 | tf_op jit(solution)/shard_map/ppermute | solution.py:558
  16.7 2.0 %collective-permute-done.3.got2 = f32[256,128]{1,0:T(8,128)S(1)} collective-permute-done((f32[256,128]{1,0:T(8,128)}, f32[256,128]{1,0:T(8,128)S(1)}, u32[]{:S(2)}, u32[]{:S(2)}) %collective-permute-start.3) | collective-permute-done | bytes 131104 | tf_op jit(solution)/shard_map/ppermute | solution.py:558
  21.1 3.5 %shard_map.96 = (f32[6160,128]{1,0:T(8,128)S(1)}, f32[768,128]{1,0:T(8,128)S(1)}, f32[192,128]{1,0:T(8,128)S(1)}) custom-call(s32[14]{0:T(128)S(1)} %stack.75.sc, f32[4096,128]{1,0:T(8,128)S(1)} %bitcast.31, f32[1032,128]{1,0:T(8,128)S(1)} %collective-permute-done.wide1, f32[1032,128]{1,0:T(8,128)S(1)} %collective-permute-done.1.wide2, ...), custom_call_target="tpu_custom_call" | custom-call | tf_op jit(solution)/shard_map/pallas_call | solution.py:492
  26.1 1.9 %collective-permute-start.9 = (f32[208,128]{1,0:T(8,128)S(1)}, f32[208,128]{1,0:T(8,128)S(1)}, u32[]{:S(2)}, u32[]{:S(2)}) collective-permute-start(f32[208,128]{1,0:T(8,128)S(1)} %get-tuple-element.38), channel_id=1, source_target_pairs={{0,12},{4,8},{8,4},{12,0},{16,28},{20,24},{24,20},{28,16},{32,44},... | collective-permute-start | bytes 319496 | tf_op jit(solution)/shard_map/ppermute | solution.py:586
  28.0 1.4 %collective-permute-start.8 = (f32[208,128]{1,0:T(8,128)S(1)}, f32[208,128]{1,0:T(8,128)S(1)}, u32[]{:S(2)}, u32[]{:S(2)}) collective-permute-start(f32[208,128]{1,0:T(8,128)S(1)} %get-tuple-element.38), channel_id=1, source_target_pairs={{0,8},{4,12},{8,0},{12,4},{16,24},{20,28},{24,16},{28,20},{32,40},... | collective-permute-start | bytes 319496 | tf_op jit(solution)/shard_map/ppermute | solution.py:586
  29.5 3.2 %collective-permute-start.12 = (f32[208,128]{1,0:T(8,128)S(1)}, f32[208,128]{1,0:T(8,128)S(1)}, u32[]{:S(2)}, u32[]{:S(2)}) collective-permute-start(f32[208,128]{1,0:T(8,128)S(1)} %get-tuple-element.40), channel_id=1, source_target_pairs={{12,24},{24,12},{4,16},{16,4},{28,40},{40,28},{20,32},{32,20},{44,... | collective-permute-start | bytes 319496 | tf_op jit(solution)/shard_map/ppermute | solution.py:586
  32.7 6.7 %collective-permute-start.11 = (f32[208,128]{1,0:T(8,128)S(1)}, f32[208,128]{1,0:T(8,128)S(1)}, u32[]{:S(2)}, u32[]{:S(2)}) collective-permute-start(f32[208,128]{1,0:T(8,128)S(1)} %get-tuple-element.39), channel_id=1, source_target_pairs={{12,20},{20,12},{8,16},{16,8},{28,36},{36,28},{24,32},{32,24},{44,... | collective-permute-start | bytes 319496 | tf_op jit(solution)/shard_map/ppermute | solution.py:586
  39.4 5.9 %collective-permute-start.10 = (f32[208,128]{1,0:T(8,128)S(1)}, f32[208,128]{1,0:T(8,128)S(1)}, u32[]{:S(2)}, u32[]{:S(2)}) collective-permute-start(f32[208,128]{1,0:T(8,128)S(1)} %get-tuple-element.39), channel_id=1, source_target_pairs={{12,16},{16,12},{8,20},{20,8},{28,32},{32,28},{24,36},{36,24},{44,... | collective-permute-start | bytes 319496 | tf_op jit(solution)/shard_map/ppermute | solution.py:586
  45.3 4.0 %collective-permute-done.10.r3 = f32[208,128]{1,0:T(8,128)S(1)} collective-permute-done((f32[208,128]{1,0:T(8,128)S(1)}, f32[208,128]{1,0:T(8,128)S(1)}, u32[]{:S(2)}, u32[]{:S(2)}) %collective-permute-start.10) | collective-permute-done | bytes 106528 | tf_op jit(solution)/shard_map/ppermute | solution.py:586
  49.3 6.6 %shard_map.100 = (f32[6160,128]{1,0:T(8,128)S(1)}, f32[192,128]{1,0:T(8,128)S(1)}) custom-call(s32[14]{0:T(128)S(1)} %stack.75.sc, f32[6160,128]{1,0:T(8,128)S(1)} %get-tuple-element.26.state, f32[192,128]{1,0:T(8,128)S(1)} %get-tuple-element.27.edges.own, f32[96,128]{1,0:T(8,128)S(1)} %get-tuple-element.35.ogx, f32[768,128]{1,0:T(8,128)S(1)} %get-tuple-element.34.coef, ...), custom_call_target="tpu_custom_call" | custom-call | tf_op jit(solution)/shard_map/pallas_call | solution.py:492
  56.0 3.5 %collective-permute-start.18 = (f32[192,128]{1,0:T(8,128)S(1)}, f32[192,128]{1,0:T(8,128)S(1)}, u32[]{:S(2)}, u32[]{:S(2)}) collective-permute-start(f32[192,128]{1,0:T(8,128)S(1)} %get-tuple-element.42.own), channel_id=1, source_target_pairs={{12,24},{24,12},{4,16},{16,4},{28,40},{40,28},{20,32},{32,20},{44,... | collective-permute-start | bytes 294920 | tf_op jit(solution)/shard_map/ppermute | solution.py:591
  59.5 2.0 %collective-permute-start.17 = (f32[192,128]{1,0:T(8,128)S(1)}, f32[192,128]{1,0:T(8,128)S(1)}, u32[]{:S(2)}, u32[]{:S(2)}) collective-permute-start(f32[192,128]{1,0:T(8,128)S(1)} %get-tuple-element.42.own), channel_id=1, source_target_pairs={{12,20},{20,12},{8,16},{16,8},{28,36},{36,28},{24,32},{32,24},{44,... | collective-permute-start | bytes 294920 | tf_op jit(solution)/shard_map/ppermute | solution.py:591
  61.5 3.8 %collective-permute-start.16 = (f32[192,128]{1,0:T(8,128)S(1)}, f32[192,128]{1,0:T(8,128)S(1)}, u32[]{:S(2)}, u32[]{:S(2)}) collective-permute-start(f32[192,128]{1,0:T(8,128)S(1)} %get-tuple-element.42.own), channel_id=1, source_target_pairs={{12,16},{16,12},{8,20},{20,8},{28,32},{32,28},{24,36},{36,24},{44,... | collective-permute-start | bytes 294920 | tf_op jit(solution)/shard_map/ppermute | solution.py:591
  65.2 5.5 %collective-permute-start.14 = (f32[192,128]{1,0:T(8,128)S(1)}, f32[192,128]{1,0:T(8,128)S(1)}, u32[]{:S(2)}, u32[]{:S(2)}) collective-permute-start(f32[192,128]{1,0:T(8,128)S(1)} %get-tuple-element.42.own), channel_id=1, source_target_pairs={{0,8},{4,12},{8,0},{12,4},{16,24},{20,28},{24,16},{28,20},{32,40},... | collective-permute-start | bytes 294920 | tf_op jit(solution)/shard_map/ppermute | solution.py:591
  71.6 1.7 %collective-permute-done.14.s1 = f32[192,128]{1,0:T(8,128)S(1)} collective-permute-done((f32[192,128]{1,0:T(8,128)S(1)}, f32[192,128]{1,0:T(8,128)S(1)}, u32[]{:S(2)}, u32[]{:S(2)}) %collective-permute-start.14) | collective-permute-done | bytes 98336 | tf_op jit(solution)/shard_map/ppermute | solution.py:591
  73.3 2.0 %collective-permute-done.13.s0 = f32[192,128]{1,0:T(8,128)S(1)} collective-permute-done((f32[192,128]{1,0:T(8,128)S(1)}, f32[192,128]{1,0:T(8,128)S(1)}, u32[]{:S(2)}, u32[]{:S(2)}) %collective-permute-start.13) | collective-permute-done | bytes 98336 | tf_op jit(solution)/shard_map/ppermute | solution.py:591
  75.4 9.6 %shard_map.101 = (f32[4096,128]{1,0:T(8,128)}, f32[256,128]{1,0:T(8,128)S(1)}, f32[24,128]{1,0:T(8,128)S(1)}) custom-call(s32[14]{0:T(128)S(1)} %stack.75.sc, f32[6160,128]{1,0:T(8,128)S(1)} %get-tuple-element.41.state, f32[192,128]{1,0:T(8,128)S(1)} %get-tuple-element.42.own, f32[96,128]{1,0:T(8,128)S(1)} %get-tuple-element.35.ogx, ...), custom_call_target="tpu_custom_call" | custom-call | tf_op jit(solution)/shard_map/pallas_call | solution.py:492
  85.0 3.1 %collective-permute-start.20 = (f32[256,128]{1,0:T(8,128)S(1)}, f32[256,128]{1,0:T(8,128)S(1)}, u32[]{:S(2)}, u32[]{:S(2)}) collective-permute-start(f32[256,128]{1,0:T(8,128)S(1)} %get-tuple-element.44.means), channel_id=1, source_target_pairs={{0,8},{4,12},{8,0},{12,4},{16,24},{20,28},{24,16},{28,20},{32,40},... | collective-permute-start | bytes 393224 | tf_op jit(solution)/shard_map/ppermute | solution.py:597
  90.0 1.6 %collective-permute-done.20.got2 = f32[256,128]{1,0:T(8,128)S(1)} collective-permute-done((f32[256,128]{1,0:T(8,128)S(1)}, f32[256,128]{1,0:T(8,128)S(1)}, u32[]{:S(2)}, u32[]{:S(2)}) %collective-permute-start.20) | collective-permute-done | bytes 131104 | tf_op jit(solution)/shard_map/ppermute | solution.py:597
  91.6 1.9 %collective-permute-done.19.got1 = f32[256,128]{1,0:T(8,128)S(1)} collective-permute-done((f32[256,128]{1,0:T(8,128)S(1)}, f32[256,128]{1,0:T(8,128)S(1)}, u32[]{:S(2)}, u32[]{:S(2)}) %collective-permute-start.19) | collective-permute-done | bytes 131104 | tf_op jit(solution)/shard_map/ppermute | solution.py:597
  93.5 1.2 %shard_map.102 = f32[256,128]{1,0:T(8,128)} custom-call(s32[14]{0:T(128)S(1)} %stack.75.sc, f32[256,128]{1,0:T(8,128)S(1)} %get-tuple-element.31.own.coarse, f32[256,128]{1,0:T(8,128)S(1)} %get-tuple-element.44.means, f32[256,128]{1,0:T(8,128)S(1)} %collective-permute-done.19.got1, f32[256,128]{1,0:T(8,128)S(1)} %collective-permute-done.20.got2, ...), custom_call_target="tpu_custom_call" | custom-call | tf_op jit(solution)/shard_map/pallas_call | solution.py:492
  (45 shorter events, 14.4 us)
Async XLA Ops:
  1.4 1.6 %copy-start = (f32[4,64,16,128]{3,2,1,0:T(8,128)S(1)}, f32[4,64,16,128]{3,2,1,0:T(8,128)}, u32[]{:S(2)}) copy-start(f32[4,64,16,128]{3,2,1,0:T(8,128)} %param.8) | copy-start | bytes 6291460
  4.4 16.7 %copy-start.1 = (f32[4,64,16,128]{3,2,1,0:T(8,128)S(1)}, f32[4,64,16,128]{3,2,1,0:T(8,128)}, u32[]{:S(2)}) copy-start(f32[4,64,16,128]{3,2,1,0:T(8,128)} %param.8) | copy-start | bytes 6291460
  5.5 15.6 %collective-permute-start.1 = (f32[1032,128]{1,0:T(8,128)S(1)}, f32[1032,128]{1,0:T(8,128)S(1)}, u32[]{:S(2)}, u32[]{:S(2)}) collective-permute-start(f32[1032,128]{1,0:T(8,128)S(1)} %get-tuple-element.25), channel_id=1, source_target_pairs={{1,2},{2,1},{5,6},{6,5},{9,10},{10,9},{13,14},{14,13},{17,18},{18,... | collective-permute-start | bytes 1585160 | tf_op jit(solution)/shard_map/ppermute | solution.py:557
  6.2 14.9 %collective-permute-start = (f32[1032,128]{1,0:T(8,128)S(1)}, f32[1032,128]{1,0:T(8,128)S(1)}, u32[]{:S(2)}, u32[]{:S(2)}) collective-permute-start(f32[1032,128]{1,0:T(8,128)S(1)} %get-tuple-element.24), channel_id=1, source_target_pairs={{0,1},{1,0},{2,3},{3,2},{4,5},{5,4},{6,7},{7,6},{8,9},{9,8},{10,11... | collective-permute-start | bytes 1585160 | tf_op jit(solution)/shard_map/ppermute | solution.py:556
  9.2 7.5 %collective-permute-start.4 = (f32[256,128]{1,0:T(8,128)}, f32[256,128]{1,0:T(8,128)S(1)}, u32[]{:S(2)}, u32[]{:S(2)}) collective-permute-start(f32[256,128]{1,0:T(8,128)} %bitcast.32), channel_id=1, source_target_pairs={{0,12},{4,8},{8,4},{12,0},{16,28},{20,24},{24,20},{28,16},{32,44},... | collective-permute-start | bytes 393224 | tf_op jit(solution)/shard_map/ppermute | solution.py:558
  10.7 8.1 %collective-permute-start.3 = (f32[256,128]{1,0:T(8,128)}, f32[256,128]{1,0:T(8,128)S(1)}, u32[]{:S(2)}, u32[]{:S(2)}) collective-permute-start(f32[256,128]{1,0:T(8,128)} %bitcast.33), channel_id=1, source_target_pairs={{0,8},{4,12},{8,0},{12,4},{16,24},{20,28},{24,16},{28,20},{32,40},... | collective-permute-start | bytes 393224 | tf_op jit(solution)/shard_map/ppermute | solution.py:558
  11.8 7.8 %collective-permute-start.2 = (f32[256,128]{1,0:T(8,128)}, f32[256,128]{1,0:T(8,128)S(1)}, u32[]{:S(2)}, u32[]{:S(2)}) collective-permute-start(f32[256,128]{1,0:T(8,128)} %bitcast.34), channel_id=1, source_target_pairs={{0,4},{4,0},{8,12},{12,8},{16,20},{20,16},{24,28},{28,24},{32,36},... | collective-permute-start | bytes 393224 | tf_op jit(solution)/shard_map/ppermute | solution.py:558
  20.6 4.1 %collective-permute-start.6 = (f32[128,128]{1,0:T(8,128)S(1)}, f32[128,128]{1,0:T(8,128)S(1)}, u32[]{:S(2)}, u32[]{:S(2)}) collective-permute-start(f32[128,128]{1,0:T(8,128)S(1)} %shard_map.98.og), channel_id=1, source_target_pairs={{0,3},{1,2},{2,1},{3,0},{4,7},{5,6},{6,5},{7,4},{8,11},{9,10},{10,... | collective-permute-start | bytes 196616 | tf_op jit(solution)/shard_map/ppermute | solution.py:574
  20.7 4.0 %collective-permute-start.5 = (f32[128,128]{1,0:T(8,128)S(1)}, f32[128,128]{1,0:T(8,128)S(1)}, u32[]{:S(2)}, u32[]{:S(2)}) collective-permute-start(f32[128,128]{1,0:T(8,128)S(1)} %shard_map.98.og), channel_id=1, source_target_pairs={{0,1},{1,0},{2,3},{3,2},{4,5},{5,4},{6,7},{7,6},{8,9},{9,8},{10,11... | collective-permute-start | bytes 196616 | tf_op jit(solution)/shard_map/ppermute | solution.py:573
  25.3 14.1 %collective-permute-start.7 = (f32[208,128]{1,0:T(8,128)S(1)}, f32[208,128]{1,0:T(8,128)S(1)}, u32[]{:S(2)}, u32[]{:S(2)}) collective-permute-start(f32[208,128]{1,0:T(8,128)S(1)} %get-tuple-element.37), channel_id=1, source_target_pairs={{0,4},{4,0},{8,12},{12,8},{16,20},{20,16},{24,28},{28,24},{32,36},... | collective-permute-start | bytes 319496 | tf_op jit(solution)/shard_map/ppermute | solution.py:586
  26.1 19.2 %collective-permute-start.9 = (f32[208,128]{1,0:T(8,128)S(1)}, f32[208,128]{1,0:T(8,128)S(1)}, u32[]{:S(2)}, u32[]{:S(2)}) collective-permute-start(f32[208,128]{1,0:T(8,128)S(1)} %get-tuple-element.38), channel_id=1, source_target_pairs={{0,12},{4,8},{8,4},{12,0},{16,28},{20,24},{24,20},{28,16},{32,44},... | collective-permute-start | bytes 319496 | tf_op jit(solution)/shard_map/ppermute | solution.py:586
  28.0 17.3 %collective-permute-start.8 = (f32[208,128]{1,0:T(8,128)S(1)}, f32[208,128]{1,0:T(8,128)S(1)}, u32[]{:S(2)}, u32[]{:S(2)}) collective-permute-start(f32[208,128]{1,0:T(8,128)S(1)} %get-tuple-element.38), channel_id=1, source_target_pairs={{0,8},{4,12},{8,0},{12,4},{16,24},{20,28},{24,16},{28,20},{32,40},... | collective-permute-start | bytes 319496 | tf_op jit(solution)/shard_map/ppermute | solution.py:586
  29.5 15.8 %collective-permute-start.12 = (f32[208,128]{1,0:T(8,128)S(1)}, f32[208,128]{1,0:T(8,128)S(1)}, u32[]{:S(2)}, u32[]{:S(2)}) collective-permute-start(f32[208,128]{1,0:T(8,128)S(1)} %get-tuple-element.40), channel_id=1, source_target_pairs={{12,24},{24,12},{4,16},{16,4},{28,40},{40,28},{20,32},{32,20},{44,... | collective-permute-start | bytes 319496 | tf_op jit(solution)/shard_map/ppermute | solution.py:586
  32.7 12.6 %collective-permute-start.11 = (f32[208,128]{1,0:T(8,128)S(1)}, f32[208,128]{1,0:T(8,128)S(1)}, u32[]{:S(2)}, u32[]{:S(2)}) collective-permute-start(f32[208,128]{1,0:T(8,128)S(1)} %get-tuple-element.39), channel_id=1, source_target_pairs={{12,20},{20,12},{8,16},{16,8},{28,36},{36,28},{24,32},{32,24},{44,... | collective-permute-start | bytes 319496 | tf_op jit(solution)/shard_map/ppermute | solution.py:586
  39.4 9.9 %collective-permute-start.10 = (f32[208,128]{1,0:T(8,128)S(1)}, f32[208,128]{1,0:T(8,128)S(1)}, u32[]{:S(2)}, u32[]{:S(2)}) collective-permute-start(f32[208,128]{1,0:T(8,128)S(1)} %get-tuple-element.39), channel_id=1, source_target_pairs={{12,16},{16,12},{8,20},{20,8},{28,32},{32,28},{24,36},{36,24},{44,... | collective-permute-start | bytes 319496 | tf_op jit(solution)/shard_map/ppermute | solution.py:586
  56.0 14.8 %collective-permute-start.18 = (f32[192,128]{1,0:T(8,128)S(1)}, f32[192,128]{1,0:T(8,128)S(1)}, u32[]{:S(2)}, u32[]{:S(2)}) collective-permute-start(f32[192,128]{1,0:T(8,128)S(1)} %get-tuple-element.42.own), channel_id=1, source_target_pairs={{12,24},{24,12},{4,16},{16,4},{28,40},{40,28},{20,32},{32,20},{44,... | collective-permute-start | bytes 294920 | tf_op jit(solution)/shard_map/ppermute | solution.py:591
  59.5 11.5 %collective-permute-start.17 = (f32[192,128]{1,0:T(8,128)S(1)}, f32[192,128]{1,0:T(8,128)S(1)}, u32[]{:S(2)}, u32[]{:S(2)}) collective-permute-start(f32[192,128]{1,0:T(8,128)S(1)} %get-tuple-element.42.own), channel_id=1, source_target_pairs={{12,20},{20,12},{8,16},{16,8},{28,36},{36,28},{24,32},{32,24},{44,... | collective-permute-start | bytes 294920 | tf_op jit(solution)/shard_map/ppermute | solution.py:591
  61.5 10.2 %collective-permute-start.16 = (f32[192,128]{1,0:T(8,128)S(1)}, f32[192,128]{1,0:T(8,128)S(1)}, u32[]{:S(2)}, u32[]{:S(2)}) collective-permute-start(f32[192,128]{1,0:T(8,128)S(1)} %get-tuple-element.42.own), channel_id=1, source_target_pairs={{12,16},{16,12},{8,20},{20,8},{28,32},{32,28},{24,36},{36,24},{44,... | collective-permute-start | bytes 294920 | tf_op jit(solution)/shard_map/ppermute | solution.py:591
  65.2 6.4 %collective-permute-start.15 = (f32[192,128]{1,0:T(8,128)S(1)}, f32[192,128]{1,0:T(8,128)S(1)}, u32[]{:S(2)}, u32[]{:S(2)}) collective-permute-start(f32[192,128]{1,0:T(8,128)S(1)} %get-tuple-element.42.own), channel_id=1, source_target_pairs={{0,12},{4,8},{8,4},{12,0},{16,28},{20,24},{24,20},{28,16},{32,44},... | collective-permute-start | bytes 294920 | tf_op jit(solution)/shard_map/ppermute | solution.py:591
  65.2 8.1 %collective-permute-start.14 = (f32[192,128]{1,0:T(8,128)S(1)}, f32[192,128]{1,0:T(8,128)S(1)}, u32[]{:S(2)}, u32[]{:S(2)}) collective-permute-start(f32[192,128]{1,0:T(8,128)S(1)} %get-tuple-element.42.own), channel_id=1, source_target_pairs={{0,8},{4,12},{8,0},{12,4},{16,24},{20,28},{24,16},{28,20},{32,40},... | collective-permute-start | bytes 294920 | tf_op jit(solution)/shard_map/ppermute | solution.py:591
  70.8 4.6 %collective-permute-start.13 = (f32[192,128]{1,0:T(8,128)S(1)}, f32[192,128]{1,0:T(8,128)S(1)}, u32[]{:S(2)}, u32[]{:S(2)}) collective-permute-start(f32[192,128]{1,0:T(8,128)S(1)} %get-tuple-element.42.own), channel_id=1, source_target_pairs={{0,4},{4,0},{8,12},{12,8},{16,20},{20,16},{24,28},{28,24},{32,36},... | collective-permute-start | bytes 294920 | tf_op jit(solution)/shard_map/ppermute | solution.py:591
  84.9 5.1 %collective-permute-start.21 = (f32[256,128]{1,0:T(8,128)S(1)}, f32[256,128]{1,0:T(8,128)S(1)}, u32[]{:S(2)}, u32[]{:S(2)}) collective-permute-start(f32[256,128]{1,0:T(8,128)S(1)} %get-tuple-element.44.means), channel_id=1, source_target_pairs={{0,12},{4,8},{8,4},{12,0},{16,28},{20,24},{24,20},{28,16},{32,44},... | collective-permute-start | bytes 393224 | tf_op jit(solution)/shard_map/ppermute | solution.py:597
  85.0 6.6 %collective-permute-start.20 = (f32[256,128]{1,0:T(8,128)S(1)}, f32[256,128]{1,0:T(8,128)S(1)}, u32[]{:S(2)}, u32[]{:S(2)}) collective-permute-start(f32[256,128]{1,0:T(8,128)S(1)} %get-tuple-element.44.means), channel_id=1, source_target_pairs={{0,8},{4,12},{8,0},{12,4},{16,24},{20,28},{24,16},{28,20},{32,40},... | collective-permute-start | bytes 393224 | tf_op jit(solution)/shard_map/ppermute | solution.py:597
  88.2 5.3 %collective-permute-start.19 = (f32[256,128]{1,0:T(8,128)S(1)}, f32[256,128]{1,0:T(8,128)S(1)}, u32[]{:S(2)}, u32[]{:S(2)}) collective-permute-start(f32[256,128]{1,0:T(8,128)S(1)} %get-tuple-element.44.means), channel_id=1, source_target_pairs={{0,4},{4,0},{8,12},{12,8},{16,20},{20,16},{24,28},{28,24},{32,36},... | collective-permute-start | bytes 393224 | tf_op jit(solution)/shard_map/ppermute | solution.py:597
  (6 other events, 4.4 us)

commit v3 on v2

--- a/solution.py
+++ b/solution.py
@@ -19,8 +19,11 @@
 PAD = 8
 STATE_ROWS = BLOCKS * COLS + 2 * PAD
 SIDE_ROWS = 4 * BLOCKS + 16
+SHARE = 6 * 16 + 8
+SWAP_ROWS = SHARE + 4 * ROWS
 WIDE_ROWS = FIELDS * LEVELS * HALO
 REACH = 3
+SMALL = 1000
 SLOTS = 2 * REACH + 1
 GROUP = 4
 VMEM_BYTES = 44 * 1024 * 1024
@@ -54,36 +57,49 @@
     lax.fori_loop(0, count // step, several, 0)
 
 
-def rows_kernel(sc, far_nest, mask, mixing, pay1, pay2, nest, wet, mix, sems):
-    share = LEVELS * ROWS
-    copies = [
-        pltpu.make_async_copy(far_nest.at[pl.ds(f * share, share)], nest.at[pl.ds(f * share, share)], sems.at[f])
-        for f in range(FIELDS)
-    ]
-    copies += [
-        pltpu.make_async_copy(mask, wet, sems.at[FIELDS]),
-        pltpu.make_async_copy(mixing, mix, sems.at[FIELDS + 1]),
-    ]
-    for copy in copies:
-        copy.start()
+def rows_kernel(sc, nest, pay1, pay2):
     even = sc[S_EVEN] == 1
     first = jnp.where(even, ROWS - HALO, 0)
     second = jnp.where(even, 0, ROWS - HALO)
-    for f in range(FIELDS):
-        copies[f].wait()
-
-        def move(i, f=f):
-            at, to = (f * LEVELS + i) * ROWS, (f * LEVELS + i) * HALO
-            pay1[pl.ds(to, HALO), :] = nest[pl.ds(at + first, HALO), :]
-            pay2[pl.ds(to, HALO), :] = nest[pl.ds(at + second, HALO), :]
-
-        unrolled(LEVELS, 16, move)
-    copies[FIELDS].wait()
-    copies[FIELDS + 1].wait()
-    for i, plane in enumerate((wet[...].astype(jnp.float32), mix[...])):
-        low, high = plane[:HALO], plane[ROWS - HALO :]
-        pay1[pl.ds(WIDE_ROWS + i * HALO, HALO), :] = jnp.where(even, high, low)
-        pay2[pl.ds(WIDE_ROWS + i * HALO, HALO), :] = jnp.where(even, low, high)
+
+    def move(i):
+        at, to = i * ROWS, i * HALO
+        pay1[pl.ds(to, HALO), :] = nest[pl.ds(at + first, HALO), :]
+        pay2[pl.ds(to, HALO), :] = nest[pl.ds(at + second, HALO), :]
+
+    unrolled(FIELDS * LEVELS, 16, move)
+
+
+def ends_kernel(nest, mask, mixing, ends, ext):
+    nothing = jnp.zeros((8, COLS), jnp.float32)
+    ext[...] = jnp.zeros_like(ext)
+    planes = (mask[...].astype(jnp.float32), mixing[...])
+    for i, plane in enumerate(planes):
+        ext[pl.ds(i * EXT + HALO, ROWS), :] = plane
+        ends[pl.ds(YB * SHARE + i * ROWS, ROWS), :] = plane
+    for yb in range(YB):
+        ends[pl.ds(yb * SHARE + 96, 8), :] = nothing
+        for i in range(2):
+            rows = [jnp.broadcast_to(ext[pl.ds(i * EXT + YB * yc + yb, 1), :], (KA, COLS)) for yc in range(YC)]
+            tile = jnp.concatenate(rows, axis=0).T
+            ends[pl.ds(yb * SHARE + 96 + i, 1), :] = tile[COLS - 1 : COLS]
+            ends[pl.ds(yb * SHARE + 98 + i, 1), :] = tile[0:1]
+
+        def take(i, yb=yb):
+            base = (i // KB) * LEVELS + i % KB
+            rows = []
+            for yc in range(YC):
+                r = YB * yc + yb - HALO
+                for a in range(2):
+                    if 0 <= r < ROWS:
+                        rows.append(nest[pl.ds((base + a * 8 * KB) * ROWS + r, 8, stride=KB * ROWS), :])
+                    else:
+                        rows.append(nothing)
+            tile = jnp.concatenate(rows, axis=0).T
+            for c, x in enumerate((COLS - 1, 0, COLS - 2, 1)):
+                ends[pl.ds(yb * SHARE + c * 16 + i, 1), :] = tile[x : x + 1]
+
+        unrolled(16, TILES, take)
 
 
 def table_kernel(coarse, face, idx, weight, table, offs, kept, spread, near, face_in, idx_in, weight_in, sems):
@@ -121,8 +137,12 @@
             table[pl.ds(side * EXT + yb * YC, YC), :] = spread[pl.ds(side * EXT + yb, YC, stride=YB), :]
 
 
-def open_kernel(sc, own, got1, got2, got3, table, offs, og, chosen):
-    og[pl.ds(2 * BLOCKS, 2 * ROWS), :] = offs[...]
+def open_kernel(sc, own, got1, got2, got3, table, offs, ends, og, swap, chosen):
+    swap[pl.ds(SHARE, 2 * ROWS), :] = offs[...]
+    swap[pl.ds(SHARE + 2 * ROWS, 2 * ROWS), :] = ends[pl.ds(YB * SHARE, 2 * ROWS), :]
+    for yb in range(YB):
+        og[pl.ds(yb * SHARE, 64), :] = ends[pl.ds(yb * SHARE, 64), :]
+        og[pl.ds(yb * SHARE + 96, 8), :] = ends[pl.ds(yb * SHARE + 96, 8), :]
     pbx = sc[S_PBX]
     value = own[...]
     for code, got in ((1, got1), (2, got2), (3, got3)):
@@ -146,7 +166,13 @@
             value = part
             for d in range(1, 8):
                 value = jnp.where(shift == d, pltpu.roll(pltpu.roll(part, KA * d, 1), 8 - d, 0), value)
-            og[pl.ds(i * 16 + half * 8, 8), :] = value
+            og[pl.ds((i % YB) * SHARE + 64 + (i // YB) * 16 + half * 8, 8), :] = value
+    chunk = lanes(SHARE) // KA
+    planes = [og[pl.ds(yb * SHARE, SHARE), :] for yb in range(YB)]
+    swap[pl.ds(0, SHARE), :] = jnp.where(
+        chunk % 4 == 3, pltpu.roll(planes[0], KA, 1),
+        jnp.where(chunk % 4 == 0, pltpu.roll(planes[2], COLS - KA, 1), planes[1]),
+    )
 
 
 def columns_of(state, edges):
@@ -162,7 +188,7 @@
     return top, bottom
 
 
-def turn_kernel(sc, nest, wide1, wide2, far_mask, far_mixing, state, coef, edges, ext, mask, mixing, sems):
+def turn_kernel(sc, nest, wide1, wide2, edge1, edge2, far_mask, far_mixing, state, coef, ext, mask, mixing, sems):
     copies = [
         pltpu.make_async_copy(far_mask, mask, sems.at[0]),
         pltpu.make_async_copy(far_mixing, mixing, sems.at[1]),
@@ -199,8 +225,10 @@
     for copy in copies:
         copy.wait()
     for i, plane in enumerate((mask[...].astype(jnp.float32), mixing[...])):
-        at = pl.ds(WIDE_ROWS + i * HALO, HALO)
-        top, bottom = halos(sc, wide1[at, :], wide2[at, :])
+        at = SHARE + (2 + i) * ROWS
+        low, high = pl.ds(at, HALO), pl.ds(at + ROWS - HALO, HALO)
+        top = halos(sc, edge1[high, :], edge2[high, :])[0]
+        bottom = halos(sc, edge1[low, :], edge2[low, :])[1]
         ext[pl.ds(i * EXT, HALO), :] = top
         ext[pl.ds(i * EXT + HALO, ROWS), :] = plane
         ext[pl.ds(i * EXT + HALO + ROWS, HALO), :] = bottom
@@ -210,44 +238,42 @@
                 jnp.broadcast_to(ext[pl.ds(i * EXT + YB * yc + yb, 1), :], (KA, COLS)) for yc in range(YC)
             ]
             coef[pl.ds((i * YB + yb) * COLS, COLS), :] = jnp.concatenate(rows, axis=0).T
-    columns_of(state, edges)
-
-
-def message_kernel(sc, edges, og, edge1, edge2, coef, ogx, offv, msg_e, msg_o, msg_lo, msg_hi, left, right, ext):
+
+
+def message_kernel(sc, og, offs, edge1, edge2, ogx, offv, edges, msg_e, msg_o, msg_lo, msg_hi, left, right, ext, joint):
     mine = sublanes() == lanes() // KA
     even = sc[S_EVEN] == 1
     for i in range(2):
-        at = 2 * BLOCKS + i * ROWS
+        at = SHARE + i * ROWS
         one_low, one_high = edge1[pl.ds(at, HALO), :], edge1[pl.ds(at + ROWS - HALO, HALO), :]
         two_low, two_high = edge2[pl.ds(at, HALO), :], edge2[pl.ds(at + ROWS - HALO, HALO), :]
         ext[pl.ds(i * EXT, HALO), :] = jnp.where(even, two_high, one_high)
-        ext[pl.ds(i * EXT + HALO, ROWS), :] = og[pl.ds(at, ROWS), :]
+        ext[pl.ds(i * EXT + HALO, ROWS), :] = offs[pl.ds(i * ROWS, ROWS), :]
         ext[pl.ds(i * EXT + HALO + ROWS, HALO), :] = jnp.where(even, one_low, two_low)
         for yb in range(YB):
             away = ext[pl.ds(i * EXT + yb, YC, stride=YB), :]
             offv[pl.ds(i * YB + yb, 1), :] = jnp.sum(jnp.where(mine, away, 0.0), axis=0, keepdims=True)
-    lane16 = lanes(16) // KA
-    for side in range(2):
-        tops, bottoms = [], []
-        for yb in range(YB):
-            rows = pl.ds((side * YB + yb) * 16, 16)
-            top, bottom = halos(sc, edge1[rows, :], edge2[rows, :])
-            tops.append(top)
-            bottoms.append(bottom)
-        for yb in range(YB):
-            rows = pl.ds((side * YB + yb) * 16, 16)
-            row = YB * lane16 + yb
-            up = pltpu.roll(tops[(yb + 1) % YB], COLS - KA * (6 if yb == 2 else 5), 1)
-            down = pltpu.roll(bottoms[(yb + 2) % YB], KA * (6 if yb == 0 else 5), 1)
-            ogx[rows, :] = jnp.where(row < HALO, up, jnp.where(row >= HALO + ROWS, down, og[rows, :]))
+    chunk = lanes(SHARE) // KA
+    top, bottom = halos(sc, edge1[pl.ds(0, SHARE), :], edge2[pl.ds(0, SHARE), :])
+    for yb in range(YB):
+        rows = pl.ds(yb * SHARE, SHARE)
+        row = YB * chunk + yb
+        up = pltpu.roll(top, KA * (3, 4, 1)[yb], 1)
+        down = pltpu.roll(bottom, KA * (7, 4, 5)[yb], 1)
+        joint[rows, :] = jnp.where(row < HALO, up, jnp.where(row >= HALO + ROWS, down, og[rows, :]))
+        for c in range(4):
+            edges[pl.ds(c * BLOCKS + yb * 16, 16), :] = joint[pl.ds(yb * SHARE + c * 16, 16), :]
+        for side in range(2):
+            ogx[pl.ds(side * BLOCKS + yb * 16, 16), :] = joint[pl.ds(yb * SHARE + 64 + side * 16, 16), :]
     number = sc[S_PB].astype(jnp.float32)
-    for ref, third, opened, x, off in ((right, 2, 1, COLS - 1, 1), (left, 3, 0, 0, 0)):
+    for ref, third, opened, fact, off in ((right, 2, 1, 0, 1), (left, 3, 0, 2, 0)):
         ref[pl.ds(0, 2 * BLOCKS), :] = edges[pl.ds(0, 2 * BLOCKS), :]
         ref[pl.ds(2 * BLOCKS, BLOCKS), :] = edges[pl.ds(third * BLOCKS, BLOCKS), :]
         ref[pl.ds(3 * BLOCKS, BLOCKS), :] = ogx[pl.ds(opened * BLOCKS, BLOCKS), :]
         ref[pl.ds(4 * BLOCKS, 16), :] = jnp.zeros((16, COLS), jnp.float32) + number
-        for i in range(2 * YB):
-            ref[pl.ds(4 * BLOCKS + i, 1), :] = coef[pl.ds(i * COLS + x, 1), :]
+        for yb in range(YB):
+            for i in range(2):
+                ref[pl.ds(4 * BLOCKS + i * YB + yb, 1), :] = joint[pl.ds(yb * SHARE + 96 + fact + i, 1), :]
         ref[pl.ds(4 * BLOCKS + 2 * YB, YB), :] = offv[pl.ds(off * YB, YB), :]
     x_even, low = sc[S_XEVEN] == 1, sc[S_LOW] == 1
     msg_e[...] = jnp.where(x_even, right[...], left[...])
@@ -482,7 +508,7 @@
         out[rows, :] = old + FEEDBACK * (value - old)
 
 
-def call(kernel, outs, scratch, *args, far=(), far_out=()):
+def call(kernel, outs, scratch, *args, far=(), far_out=(), cost=None):
     def spec(i, places, arg=None):
         if i in places:
             return pl.BlockSpec(memory_space=pltpu.HBM)
@@ -495,6 +521,7 @@
         in_specs=[spec(i, far, a) for i, a in enumerate(args)],
         out_specs=[spec(i, far_out) for i in range(len(outs))],
         scratch_shapes=[pltpu.VMEM(s, jnp.float32) if isinstance(s, tuple) else s for s in scratch],
+        cost_estimate=None if cost is None else pl.CostEstimate(flops=cost, bytes_accessed=cost, transcendentals=0),
         compiler_params=pltpu.CompilerParams(vmem_limit_bytes=VMEM_BYTES),
     )(*args)
 
@@ -547,40 +574,40 @@
     nest2 = nest_state.reshape(FIELDS * LEVELS * ROWS, COLS)
     coarse = parent_state.reshape(FIELDS * LEVELS, COLS)
     natural = (FIELDS * LEVELS * ROWS, COLS)
-    rows, narrow = (WIDE_ROWS + 2 * HALO, COLS), (ROWS, COLS)
-    pay1, pay2 = call(
-        rows_kernel, [rows, rows],
-        [natural, pltpu.VMEM(narrow, jnp.int32), pltpu.VMEM(narrow, jnp.float32), pltpu.SemaphoreType.DMA((6,))],
-        sc, nest2, land_mask, mixing, far=(1, 2, 3),
+    rows, narrow = (WIDE_ROWS, COLS), (ROWS, COLS)
+    got = [lax.ppermute(coarse, "nest", links[i]) for i in range(3)]
+    pay1, pay2 = call(rows_kernel, [rows, rows], [], sc, nest2)
+    (ends,) = call(
+        ends_kernel, [(YB * SHARE + 2 * ROWS, COLS)], [(2 * EXT, COLS)], nest2, land_mask, mixing, cost=SMALL
     )
     wide1 = lax.ppermute(pay1, "parent", rows_1)
-    wide2 = lax.ppermute(pay2, "parent", rows_2[1:-1])
-    got = [lax.ppermute(coarse, "nest", links[i]) for i in range(3)]
-    face, idx, weight, pay1 = lax.optimization_barrier(
-        (face_off.T, interp_idx.transpose(1, 2, 0).reshape(8, ROWS), interp_w.transpose(1, 2, 0).reshape(8, ROWS), pay1)
+    wide2 = lax.ppermute(pay2, "parent", rows_2)
+    face, idx, weight = (
+        face_off.T, interp_idx.transpose(1, 2, 0).reshape(8, ROWS), interp_w.transpose(1, 2, 0).reshape(8, ROWS)
     )
     coarse_rows = (FIELDS * LEVELS, COLS)
     table, offs, kept = call(
         table_kernel, [(2 * EXT, COLS), (2 * ROWS, COLS), coarse_rows],
         [(2 * EXT, COLS), coarse_rows, pltpu.VMEM((2, ROWS), jnp.int32), pltpu.VMEM((8, ROWS), jnp.int32),
          pltpu.VMEM((8, ROWS), jnp.float32), pltpu.SemaphoreType.DMA((4,))],
-        coarse, face, idx, weight, far=(0, 1, 2, 3),
+        coarse, face, idx, weight, far=(0, 1, 2, 3), cost=SMALL,
     )
     block, state_rows = (BLOCKS, COLS), (STATE_ROWS, COLS)
-    (og,) = call(
-        open_kernel, [(2 * BLOCKS + 2 * ROWS, COLS)], [coarse_rows], sc, kept, *got, table, offs
-    )
-    edge1 = lax.ppermute(og, "parent", rows_1)
-    edge2 = lax.ppermute(og, "parent", rows_2)
-    state, coef, edges = call(
-        turn_kernel, [state_rows, (2 * YB * COLS, COLS), (4 * BLOCKS, COLS)],
+    og, swap = call(
+        open_kernel, [(YB * SHARE, COLS), (SWAP_ROWS, COLS)], [coarse_rows], sc, kept, *got, table, offs, ends
+    )
+    edge1 = lax.ppermute(swap, "parent", rows_1)
+    edge2 = lax.ppermute(swap, "parent", rows_2)
+    side = (SIDE_ROWS, COLS)
+    ogx, offv, edges, msg_e, msg_o, msg_lo, msg_hi = call(
+        message_kernel, [(2 * BLOCKS, COLS), (8, COLS), (4 * BLOCKS, COLS)] + [side] * 4,
+        [side, side, (2 * EXT, COLS), (YB * SHARE, COLS)], sc, og, offs, edge1, edge2,
+    )
+    nest_later, offv = lax.optimization_barrier((nest2, offv))
+    state, coef = call(
+        turn_kernel, [state_rows, (2 * YB * COLS, COLS)],
         [(2 * EXT, COLS), pltpu.VMEM(narrow, jnp.int32), pltpu.VMEM(narrow, jnp.float32), pltpu.SemaphoreType.DMA((2,))],
-        sc, nest2, wide1, wide2, land_mask, mixing, far=(4, 5),
-    )
-    side = (SIDE_ROWS, COLS)
-    ogx, offv, msg_e, msg_o, msg_lo, msg_hi = call(
-        message_kernel, [(2 * BLOCKS, COLS), (8, COLS)] + [side] * 4, [side, side, (2 * EXT, COLS)],
-        sc, edges, og, edge1, edge2, coef,
+        sc, nest_later, wide1, wide2, edge1, edge2, land_mask, mixing, far=(6, 7),
     )
     msgs = [msg_e, msg_lo, msg_lo, msg_hi, msg_hi, msg_o]
     first = [lax.ppermute(m, "nest", link) for m, link in zip(msgs, links)]

time: 95.1 us -> 92.3 us (0.971)
  local copies, waits for them, and re-layouts: 6.06 us -> 3.11 us
  Pallas kernels: 24.2 us -> 26.3 us
  starting transfers between devices: 47.2 us -> 45.7 us
    ppermute x3, waiting for transfers between devices: 0.01 us -> 3.42 us  [the longest x1 3.41 us: per_device(): edge2 = lax.ppermute(swap, 'parent', rows_2)]
    unnamed x16 -> x20, local copies, waits for them, and re-layouts: 5.97 us -> 3.02 us
    ppermute x1, starting transfers between devices: 2.99 us -> 0.09 us  [per_device(): wide1 = lax.ppermute(pay1, 'parent', rows_1)]
    ppermute x6, waiting for transfers between devices: 4.01 us -> 1.18 us  [per_device(): first = [lax.ppermute(m, 'nest', link) for m, link in zip(msgs, links)]]
    pallas_call x8 -> x9, Pallas kernels: 24.2 us -> 26.3 us  [call(): pl.pallas_call(kernel, out_shape=[jax.ShapeDtypeStruct(s, jnp.float32) fo...]
    ppermute x3, starting transfers between devices: 1.22 us -> 2.33 us  [the longest x1 1.7 us: per_device(): wide2 = lax.ppermute(pay2, 'parent', rows_2)]
  transfers between devices with their start and end apart: 22 -> 22, of which waited for: 10 -> 12; matrix products, arithmetic and copies ran while one was open for 0% -> 0% of each run, Pallas kernels for 5% -> 9%
where the time goes in v3:
time: 92.3 us; the launch traced here: 92.1 us
  starting transfers between devices  45.7 us (50%)
  Pallas kernels  26.3 us (28%)
  waiting for transfers between devices  15.4 us (17%)
  local copies, waits for them, and re-layouts  3.11 us (3%)
  between operations  1.59 us (2%)
    pallas_call x9, Pallas kernels, call(): pl.pallas_call(kernel, out_shape=[jax.ShapeDtypeStruct(s, jnp.float32) fo...  26.3 us
    ppermute x6, starting transfers between devices, per_device(): first = [lax.ppermute(m, 'nest', link) for m, link in zip(msgs, links)]  19.8 us
    ppermute x6, starting transfers between devices, per_device(): second = [lax.ppermute(edges, 'nest', link) for link in links]  15.2 us
    ppermute x6, waiting for transfers between devices, per_device(): second = [lax.ppermute(edges, 'nest', link) for link in links]  4.61 us
    ppermute x3, waiting for transfers between devices, per_device(): arrived = [lax.ppermute(means, 'nest', links[i]) for i in range(3)]  4.34 us
    ppermute x3, starting transfers between devices, per_device(): arrived = [lax.ppermute(means, 'nest', links[i]) for i in range(3)]  4.17 us
    ppermute x3, starting transfers between devices, per_device(): got = [lax.ppermute(coarse, 'nest', links[i]) for i in range(3)]  4.09 us
    ppermute x1, waiting for transfers between devices, per_device(): edge2 = lax.ppermute(swap, 'parent', rows_2)  3.41 us
  transfers between devices with their start and end apart: 22, of which 12 were waited for; matrix products, arithmetic and copies ran while one was open for 0% of the time, Pallas kernels for 9%

profile of v3, /device:TPU:2, one launch (start us, length us, event | category | flops | bytes accessed | tf_op | source)
XLA Modules:
  0.0 92.1 jit_solution(11748111644493238715)
XLA Ops:
  1.5 1.6 %copy-done = f32[4,64,16,128]{3,2,1,0:T(8,128)S(1)} copy-done((f32[4,64,16,128]{3,2,1,0:T(8,128)S(1)}, f32[4,64,16,128]{3,2,1,0:T(8,128)}, u32[]{:S(2)}) %copy-start) | copy-done | bytes 2097176
  4.0 1.7 %collective-permute-start.6 = (f32[1024,128]{1,0:T(8,128)S(1)}, f32[1024,128]{1,0:T(8,128)S(1)}, u32[]{:S(2)}, u32[]{:S(2)}) collective-permute-start(f32[1024,128]{1,0:T(8,128)S(1)} %get-tuple-element.33), channel_id=1, source_target_pairs={{0,3},{1,2},{2,1},{3,0},{4,7},{5,6},{6,5},{7,4},{8,11},{9,10},{10,... | collective-permute-start | bytes 1572872 | tf_op jit(solution)/shard_map/ppermute | solution.py:584
  5.7 1.5 %collective-permute-start.2 = (f32[256,128]{1,0:T(8,128)}, f32[256,128]{1,0:T(8,128)S(1)}, u32[]{:S(2)}, u32[]{:S(2)}) collective-permute-start(f32[256,128]{1,0:T(8,128)} %bitcast.33), channel_id=1, source_target_pairs={{0,12},{4,8},{8,4},{12,0},{16,28},{20,24},{24,20},{28,16},{32,44},... | collective-permute-start | bytes 393224 | tf_op jit(solution)/shard_map/ppermute | solution.py:578
  7.2 1.3 %collective-permute-start.1 = (f32[256,128]{1,0:T(8,128)}, f32[256,128]{1,0:T(8,128)S(1)}, u32[]{:S(2)}, u32[]{:S(2)}) collective-permute-start(f32[256,128]{1,0:T(8,128)} %bitcast.34), channel_id=1, source_target_pairs={{0,8},{4,12},{8,0},{12,4},{16,24},{20,28},{24,16},{28,20},{32,40},... | collective-permute-start | bytes 393224 | tf_op jit(solution)/shard_map/ppermute | solution.py:578
  8.6 1.3 %collective-permute-start = (f32[256,128]{1,0:T(8,128)}, f32[256,128]{1,0:T(8,128)S(1)}, u32[]{:S(2)}, u32[]{:S(2)}) collective-permute-start(f32[256,128]{1,0:T(8,128)} %bitcast.35), channel_id=1, source_target_pairs={{0,4},{4,0},{8,12},{12,8},{16,20},{20,16},{24,28},{28,24},{32,36},... | collective-permute-start | bytes 393224 | tf_op jit(solution)/shard_map/ppermute | solution.py:578
  11.2 2.4 %shard_map.96.ends = f32[344,128]{1,0:T(8,128)S(1)} custom-call(f32[4096,128]{1,0:T(8,128)S(1)} %bitcast.31, s32[16,128]{1,0:T(8,128)S(1)} %copy-done.3, f32[16,128]{1,0:T(8,128)S(1)} %copy-done.5), custom_call_target="tpu_custom_call" | custom-call | flops 1000 | bytes 1000 | tf_op jit(solution)/shard_map/pallas_call | solution.py:518
  17.8 3.4 %collective-permute-done.4.edge2 = f32[168,128]{1,0:T(8,128)S(1)} collective-permute-done((f32[168,128]{1,0:T(8,128)S(1)}, f32[168,128]{1,0:T(8,128)S(1)}, u32[]{:S(2)}, u32[]{:S(2)}) %collective-permute-start.4) | collective-permute-done | bytes 86048 | tf_op jit(solution)/shard_map/ppermute | solution.py:600
  21.9 1.8 %collective-permute-start.7 = (f32[208,128]{1,0:T(8,128)S(1)}, f32[208,128]{1,0:T(8,128)S(1)}, u32[]{:S(2)}, u32[]{:S(2)}) collective-permute-start(f32[208,128]{1,0:T(8,128)S(1)} %get-tuple-element.39), channel_id=1, source_target_pairs={{0,4},{4,0},{8,12},{12,8},{16,20},{20,16},{24,28},{28,24},{32,36},... | collective-permute-start | bytes 319496 | tf_op jit(solution)/shard_map/ppermute | solution.py:613
  24.7 1.4 %collective-permute-start.8 = (f32[208,128]{1,0:T(8,128)S(1)}, f32[208,128]{1,0:T(8,128)S(1)}, u32[]{:S(2)}, u32[]{:S(2)}) collective-permute-start(f32[208,128]{1,0:T(8,128)S(1)} %get-tuple-element.40), channel_id=1, source_target_pairs={{0,8},{4,12},{8,0},{12,4},{16,24},{20,28},{24,16},{28,20},{32,40},... | collective-permute-start | bytes 319496 | tf_op jit(solution)/shard_map/ppermute | solution.py:613
  27.0 3.5 %collective-permute-start.12 = (f32[208,128]{1,0:T(8,128)S(1)}, f32[208,128]{1,0:T(8,128)S(1)}, u32[]{:S(2)}, u32[]{:S(2)}) collective-permute-start(f32[208,128]{1,0:T(8,128)S(1)} %get-tuple-element.42), channel_id=1, source_target_pairs={{12,24},{24,12},{4,16},{16,4},{28,40},{40,28},{20,32},{32,20},{44,... | collective-permute-start | bytes 319496 | tf_op jit(solution)/shard_map/ppermute | solution.py:613
  30.5 6.4 %collective-permute-start.11 = (f32[208,128]{1,0:T(8,128)S(1)}, f32[208,128]{1,0:T(8,128)S(1)}, u32[]{:S(2)}, u32[]{:S(2)}) collective-permute-start(f32[208,128]{1,0:T(8,128)S(1)} %get-tuple-element.41), channel_id=1, source_target_pairs={{12,20},{20,12},{8,16},{16,8},{28,36},{36,28},{24,32},{32,24},{44,... | collective-permute-start | bytes 319496 | tf_op jit(solution)/shard_map/ppermute | solution.py:613
  36.9 5.7 %collective-permute-start.10 = (f32[208,128]{1,0:T(8,128)S(1)}, f32[208,128]{1,0:T(8,128)S(1)}, u32[]{:S(2)}, u32[]{:S(2)}) collective-permute-start(f32[208,128]{1,0:T(8,128)S(1)} %get-tuple-element.41), channel_id=1, source_target_pairs={{12,16},{16,12},{8,20},{20,8},{28,32},{32,28},{24,36},{36,24},{44,... | collective-permute-start | bytes 319496 | tf_op jit(solution)/shard_map/ppermute | solution.py:613
  42.6 3.5 %shard_map.100 = (f32[6160,128]{1,0:T(8,128)S(1)}, f32[768,128]{1,0:T(8,128)S(1)}) custom-call(s32[14]{0:T(128)S(1)} %stack.75.sc, f32[4096,128]{1,0:T(8,128)S(1)} %bitcast.32, f32[1024,128]{1,0:T(8,128)S(1)} %collective-permute-done.5.wide1, f32[1024,128]{1,0:T(8,128)S(1)} %collective-permute-done.6.wide2, f32[168,128]{1,0:T(8,128)S(1)} %collective-permute-done.3.edge1, ...), custom_call_target="tpu_custom_call" | custom-call | tf_op jit(solution)/shard_map/pallas_call | solution.py:518
  46.4 6.5 %shard_map.101 = (f32[6160,128]{1,0:T(8,128)S(1)}, f32[192,128]{1,0:T(8,128)S(1)}) custom-call(s32[14]{0:T(128)S(1)} %stack.75.sc, f32[6160,128]{1,0:T(8,128)S(1)} %get-tuple-element.34.state, f32[192,128]{1,0:T(8,128)S(1)} %get-tuple-element.35.own, f32[96,128]{1,0:T(8,128)S(1)} %get-tuple-element.36.ogx, f32[768,128]{1,0:T(8,128)S(1)} %get-tuple-element.37.coef, ...), custom_call_target="tpu_custom_call" | custom-call | tf_op jit(solution)/shard_map/pallas_call | solution.py:518
  52.9 3.9 %collective-permute-start.18 = (f32[192,128]{1,0:T(8,128)S(1)}, f32[192,128]{1,0:T(8,128)S(1)}, u32[]{:S(2)}, u32[]{:S(2)}) collective-permute-start(f32[192,128]{1,0:T(8,128)S(1)} %get-tuple-element.44.own), channel_id=1, source_target_pairs={{12,24},{24,12},{4,16},{16,4},{28,40},{40,28},{20,32},{32,20},{44,... | collective-permute-start | bytes 294920 | tf_op jit(solution)/shard_map/ppermute | solution.py:618
  56.9 1.8 %collective-permute-start.17 = (f32[192,128]{1,0:T(8,128)S(1)}, f32[192,128]{1,0:T(8,128)S(1)}, u32[]{:S(2)}, u32[]{:S(2)}) collective-permute-start(f32[192,128]{1,0:T(8,128)S(1)} %get-tuple-element.44.own), channel_id=1, source_target_pairs={{12,20},{20,12},{8,16},{16,8},{28,36},{36,28},{24,32},{32,24},{44,... | collective-permute-start | bytes 294920 | tf_op jit(solution)/shard_map/ppermute | solution.py:618
  58.7 4.1 %collective-permute-start.16 = (f32[192,128]{1,0:T(8,128)S(1)}, f32[192,128]{1,0:T(8,128)S(1)}, u32[]{:S(2)}, u32[]{:S(2)}) collective-permute-start(f32[192,128]{1,0:T(8,128)S(1)} %get-tuple-element.44.own), channel_id=1, source_target_pairs={{12,16},{16,12},{8,20},{20,8},{28,32},{32,28},{24,36},{36,24},{44,... | collective-permute-start | bytes 294920 | tf_op jit(solution)/shard_map/ppermute | solution.py:618
  62.8 5.4 %collective-permute-start.14 = (f32[192,128]{1,0:T(8,128)S(1)}, f32[192,128]{1,0:T(8,128)S(1)}, u32[]{:S(2)}, u32[]{:S(2)}) collective-permute-start(f32[192,128]{1,0:T(8,128)S(1)} %get-tuple-element.44.own), channel_id=1, source_target_pairs={{0,8},{4,12},{8,0},{12,4},{16,24},{20,28},{24,16},{28,20},{32,40},... | collective-permute-start | bytes 294920 | tf_op jit(solution)/shard_map/ppermute | solution.py:618
  68.8 1.9 %collective-permute-done.14.s1 = f32[192,128]{1,0:T(8,128)S(1)} collective-permute-done((f32[192,128]{1,0:T(8,128)S(1)}, f32[192,128]{1,0:T(8,128)S(1)}, u32[]{:S(2)}, u32[]{:S(2)}) %collective-permute-start.14) | collective-permute-done | bytes 98336 | tf_op jit(solution)/shard_map/ppermute | solution.py:618
  70.7 2.0 %collective-permute-done.13.s0 = f32[192,128]{1,0:T(8,128)S(1)} collective-permute-done((f32[192,128]{1,0:T(8,128)S(1)}, f32[192,128]{1,0:T(8,128)S(1)}, u32[]{:S(2)}, u32[]{:S(2)}) %collective-permute-start.13) | collective-permute-done | bytes 98336 | tf_op jit(solution)/shard_map/ppermute | solution.py:618
  72.8 9.5 %shard_map.102 = (f32[4096,128]{1,0:T(8,128)}, f32[256,128]{1,0:T(8,128)S(1)}, f32[24,128]{1,0:T(8,128)S(1)}) custom-call(s32[14]{0:T(128)S(1)} %stack.75.sc, f32[6160,128]{1,0:T(8,128)S(1)} %get-tuple-element.43.state, f32[192,128]{1,0:T(8,128)S(1)} %get-tuple-element.44.own, f32[96,128]{1,0:T(8,128)S(1)} %get-tuple-element.36.ogx, ...), custom_call_target="tpu_custom_call" | custom-call | tf_op jit(solution)/shard_map/pallas_call | solution.py:518
  82.4 3.1 %collective-permute-start.20 = (f32[256,128]{1,0:T(8,128)S(1)}, f32[256,128]{1,0:T(8,128)S(1)}, u32[]{:S(2)}, u32[]{:S(2)}) collective-permute-start(f32[256,128]{1,0:T(8,128)S(1)} %get-tuple-element.46.means), channel_id=1, source_target_pairs={{0,8},{4,12},{8,0},{12,4},{16,24},{20,28},{24,16},{28,20},{32,40},... | collective-permute-start | bytes 393224 | tf_op jit(solution)/shard_map/ppermute | solution.py:624
  87.3 1.6 %collective-permute-done.20.got2 = f32[256,128]{1,0:T(8,128)S(1)} collective-permute-done((f32[256,128]{1,0:T(8,128)S(1)}, f32[256,128]{1,0:T(8,128)S(1)}, u32[]{:S(2)}, u32[]{:S(2)}) %collective-permute-start.20) | collective-permute-done | bytes 131104 | tf_op jit(solution)/shard_map/ppermute | solution.py:624
  88.9 1.9 %collective-permute-done.19.got1 = f32[256,128]{1,0:T(8,128)S(1)} collective-permute-done((f32[256,128]{1,0:T(8,128)S(1)}, f32[256,128]{1,0:T(8,128)S(1)}, u32[]{:S(2)}, u32[]{:S(2)}) %collective-permute-start.19) | collective-permute-done | bytes 131104 | tf_op jit(solution)/shard_map/ppermute | solution.py:624
  (50 shorter events, 13.2 us)
Async XLA Ops:
  0.6 41.9 %copy-start.4 = (s32[16,128]{1,0:T(8,128)S(1)}, s32[16,128]{1,0:T(8,128)}, u32[]{:S(2)}) copy-start(s32[16,128]{1,0:T(8,128)} %far_mask.1) | copy-start | bytes 24580
  0.7 41.9 %copy-start.6 = (f32[16,128]{1,0:T(8,128)S(1)}, f32[16,128]{1,0:T(8,128)}, u32[]{:S(2)}) copy-start(f32[16,128]{1,0:T(8,128)} %far_mixing.1) | copy-start | bytes 24580
  3.9 26.5 %collective-permute-start.5 = (f32[1024,128]{1,0:T(8,128)S(1)}, f32[1024,128]{1,0:T(8,128)S(1)}, u32[]{:S(2)}, u32[]{:S(2)}) collective-permute-start(f32[1024,128]{1,0:T(8,128)S(1)} %get-tuple-element.32), channel_id=1, source_target_pairs={{0,1},{1,0},{2,3},{3,2},{4,5},{5,4},{6,7},{7,6},{8,9},{9,8},{10,11... | collective-permute-start | bytes 1572872 | tf_op jit(solution)/shard_map/ppermute | solution.py:583
  4.0 32.9 %collective-permute-start.6 = (f32[1024,128]{1,0:T(8,128)S(1)}, f32[1024,128]{1,0:T(8,128)S(1)}, u32[]{:S(2)}, u32[]{:S(2)}) collective-permute-start(f32[1024,128]{1,0:T(8,128)S(1)} %get-tuple-element.33), channel_id=1, source_target_pairs={{0,3},{1,2},{2,1},{3,0},{4,7},{5,6},{6,5},{7,4},{8,11},{9,10},{10,... | collective-permute-start | bytes 1572872 | tf_op jit(solution)/shard_map/ppermute | solution.py:584
  5.7 8.5 %collective-permute-start.2 = (f32[256,128]{1,0:T(8,128)}, f32[256,128]{1,0:T(8,128)S(1)}, u32[]{:S(2)}, u32[]{:S(2)}) collective-permute-start(f32[256,128]{1,0:T(8,128)} %bitcast.33), channel_id=1, source_target_pairs={{0,12},{4,8},{8,4},{12,0},{16,28},{20,24},{24,20},{28,16},{32,44},... | collective-permute-start | bytes 393224 | tf_op jit(solution)/shard_map/ppermute | solution.py:578
  7.2 8.1 %collective-permute-start.1 = (f32[256,128]{1,0:T(8,128)}, f32[256,128]{1,0:T(8,128)S(1)}, u32[]{:S(2)}, u32[]{:S(2)}) collective-permute-start(f32[256,128]{1,0:T(8,128)} %bitcast.34), channel_id=1, source_target_pairs={{0,8},{4,12},{8,0},{12,4},{16,24},{20,28},{24,16},{28,20},{32,40},... | collective-permute-start | bytes 393224 | tf_op jit(solution)/shard_map/ppermute | solution.py:578
  8.6 7.5 %collective-permute-start = (f32[256,128]{1,0:T(8,128)}, f32[256,128]{1,0:T(8,128)S(1)}, u32[]{:S(2)}, u32[]{:S(2)}) collective-permute-start(f32[256,128]{1,0:T(8,128)} %bitcast.35), channel_id=1, source_target_pairs={{0,4},{4,0},{8,12},{12,8},{16,20},{20,16},{24,28},{28,24},{32,36},... | collective-permute-start | bytes 393224 | tf_op jit(solution)/shard_map/ppermute | solution.py:578
  17.2 4.1 %collective-permute-start.4 = (f32[168,128]{1,0:T(8,128)S(1)}, f32[168,128]{1,0:T(8,128)S(1)}, u32[]{:S(2)}, u32[]{:S(2)}) collective-permute-start(f32[168,128]{1,0:T(8,128)S(1)} %get-tuple-element.29), channel_id=1, source_target_pairs={{0,3},{1,2},{2,1},{3,0},{4,7},{5,6},{6,5},{7,4},{8,11},{9,10},{10,... | collective-permute-start | bytes 258056 | tf_op jit(solution)/shard_map/ppermute | solution.py:600
  17.2 4.0 %collective-permute-start.3 = (f32[168,128]{1,0:T(8,128)S(1)}, f32[168,128]{1,0:T(8,128)S(1)}, u32[]{:S(2)}, u32[]{:S(2)}) collective-permute-start(f32[168,128]{1,0:T(8,128)S(1)} %get-tuple-element.29), channel_id=1, source_target_pairs={{0,1},{1,0},{2,3},{3,2},{4,5},{5,4},{6,7},{7,6},{8,9},{9,8},{10,11... | collective-permute-start | bytes 258056 | tf_op jit(solution)/shard_map/ppermute | solution.py:599
  21.9 5.0 %collective-permute-start.7 = (f32[208,128]{1,0:T(8,128)S(1)}, f32[208,128]{1,0:T(8,128)S(1)}, u32[]{:S(2)}, u32[]{:S(2)}) collective-permute-start(f32[208,128]{1,0:T(8,128)S(1)} %get-tuple-element.39), channel_id=1, source_target_pairs={{0,4},{4,0},{8,12},{12,8},{16,20},{20,16},{24,28},{28,24},{32,36},... | collective-permute-start | bytes 319496 | tf_op jit(solution)/shard_map/ppermute | solution.py:613
  23.7 22.3 %collective-permute-start.9 = (f32[208,128]{1,0:T(8,128)S(1)}, f32[208,128]{1,0:T(8,128)S(1)}, u32[]{:S(2)}, u32[]{:S(2)}) collective-permute-start(f32[208,128]{1,0:T(8,128)S(1)} %get-tuple-element.40), channel_id=1, source_target_pairs={{0,12},{4,8},{8,4},{12,0},{16,28},{20,24},{24,20},{28,16},{32,44},... | collective-permute-start | bytes 319496 | tf_op jit(solution)/shard_map/ppermute | solution.py:613
  24.7 21.4 %collective-permute-start.8 = (f32[208,128]{1,0:T(8,128)S(1)}, f32[208,128]{1,0:T(8,128)S(1)}, u32[]{:S(2)}, u32[]{:S(2)}) collective-permute-start(f32[208,128]{1,0:T(8,128)S(1)} %get-tuple-element.40), channel_id=1, source_target_pairs={{0,8},{4,12},{8,0},{12,4},{16,24},{20,28},{24,16},{28,20},{32,40},... | collective-permute-start | bytes 319496 | tf_op jit(solution)/shard_map/ppermute | solution.py:613
  27.0 19.1 %collective-permute-start.12 = (f32[208,128]{1,0:T(8,128)S(1)}, f32[208,128]{1,0:T(8,128)S(1)}, u32[]{:S(2)}, u32[]{:S(2)}) collective-permute-start(f32[208,128]{1,0:T(8,128)S(1)} %get-tuple-element.42), channel_id=1, source_target_pairs={{12,24},{24,12},{4,16},{16,4},{28,40},{40,28},{20,32},{32,20},{44,... | collective-permute-start | bytes 319496 | tf_op jit(solution)/shard_map/ppermute | solution.py:613
  30.5 15.6 %collective-permute-start.11 = (f32[208,128]{1,0:T(8,128)S(1)}, f32[208,128]{1,0:T(8,128)S(1)}, u32[]{:S(2)}, u32[]{:S(2)}) collective-permute-start(f32[208,128]{1,0:T(8,128)S(1)} %get-tuple-element.41), channel_id=1, source_target_pairs={{12,20},{20,12},{8,16},{16,8},{28,36},{36,28},{24,32},{32,24},{44,... | collective-permute-start | bytes 319496 | tf_op jit(solution)/shard_map/ppermute | solution.py:613
  36.9 9.5 %collective-permute-start.10 = (f32[208,128]{1,0:T(8,128)S(1)}, f32[208,128]{1,0:T(8,128)S(1)}, u32[]{:S(2)}, u32[]{:S(2)}) collective-permute-start(f32[208,128]{1,0:T(8,128)S(1)} %get-tuple-element.41), channel_id=1, source_target_pairs={{12,16},{16,12},{8,20},{20,8},{28,32},{32,28},{24,36},{36,24},{44,... | collective-permute-start | bytes 319496 | tf_op jit(solution)/shard_map/ppermute | solution.py:613
  52.9 15.2 %collective-permute-start.18 = (f32[192,128]{1,0:T(8,128)S(1)}, f32[192,128]{1,0:T(8,128)S(1)}, u32[]{:S(2)}, u32[]{:S(2)}) collective-permute-start(f32[192,128]{1,0:T(8,128)S(1)} %get-tuple-element.44.own), channel_id=1, source_target_pairs={{12,24},{24,12},{4,16},{16,4},{28,40},{40,28},{20,32},{32,20},{44,... | collective-permute-start | bytes 294920 | tf_op jit(solution)/shard_map/ppermute | solution.py:618
  56.9 11.5 %collective-permute-start.17 = (f32[192,128]{1,0:T(8,128)S(1)}, f32[192,128]{1,0:T(8,128)S(1)}, u32[]{:S(2)}, u32[]{:S(2)}) collective-permute-start(f32[192,128]{1,0:T(8,128)S(1)} %get-tuple-element.44.own), channel_id=1, source_target_pairs={{12,20},{20,12},{8,16},{16,8},{28,36},{36,28},{24,32},{32,24},{44,... | collective-permute-start | bytes 294920 | tf_op jit(solution)/shard_map/ppermute | solution.py:618
  58.7 10.2 %collective-permute-start.16 = (f32[192,128]{1,0:T(8,128)S(1)}, f32[192,128]{1,0:T(8,128)S(1)}, u32[]{:S(2)}, u32[]{:S(2)}) collective-permute-start(f32[192,128]{1,0:T(8,128)S(1)} %get-tuple-element.44.own), channel_id=1, source_target_pairs={{12,16},{16,12},{8,20},{20,8},{28,32},{32,28},{24,36},{36,24},{44,... | collective-permute-start | bytes 294920 | tf_op jit(solution)/shard_map/ppermute | solution.py:618
  62.8 6.1 %collective-permute-start.15 = (f32[192,128]{1,0:T(8,128)S(1)}, f32[192,128]{1,0:T(8,128)S(1)}, u32[]{:S(2)}, u32[]{:S(2)}) collective-permute-start(f32[192,128]{1,0:T(8,128)S(1)} %get-tuple-element.44.own), channel_id=1, source_target_pairs={{0,12},{4,8},{8,4},{12,0},{16,28},{20,24},{24,20},{28,16},{32,44},... | collective-permute-start | bytes 294920 | tf_op jit(solution)/shard_map/ppermute | solution.py:618
  62.8 8.0 %collective-permute-start.14 = (f32[192,128]{1,0:T(8,128)S(1)}, f32[192,128]{1,0:T(8,128)S(1)}, u32[]{:S(2)}, u32[]{:S(2)}) collective-permute-start(f32[192,128]{1,0:T(8,128)S(1)} %get-tuple-element.44.own), channel_id=1, source_target_pairs={{0,8},{4,12},{8,0},{12,4},{16,24},{20,28},{24,16},{28,20},{32,40},... | collective-permute-start | bytes 294920 | tf_op jit(solution)/shard_map/ppermute | solution.py:618
  68.1 4.6 %collective-permute-start.13 = (f32[192,128]{1,0:T(8,128)S(1)}, f32[192,128]{1,0:T(8,128)S(1)}, u32[]{:S(2)}, u32[]{:S(2)}) collective-permute-start(f32[192,128]{1,0:T(8,128)S(1)} %get-tuple-element.44.own), channel_id=1, source_target_pairs={{0,4},{4,0},{8,12},{12,8},{16,20},{20,16},{24,28},{28,24},{32,36},... | collective-permute-start | bytes 294920 | tf_op jit(solution)/shard_map/ppermute | solution.py:618
  82.3 5.1 %collective-permute-start.21 = (f32[256,128]{1,0:T(8,128)S(1)}, f32[256,128]{1,0:T(8,128)S(1)}, u32[]{:S(2)}, u32[]{:S(2)}) collective-permute-start(f32[256,128]{1,0:T(8,128)S(1)} %get-tuple-element.46.means), channel_id=1, source_target_pairs={{0,12},{4,8},{8,4},{12,0},{16,28},{20,24},{24,20},{28,16},{32,44},... | collective-permute-start | bytes 393224 | tf_op jit(solution)/shard_map/ppermute | solution.py:624
  82.4 6.6 %collective-permute-start.20 = (f32[256,128]{1,0:T(8,128)S(1)}, f32[256,128]{1,0:T(8,128)S(1)}, u32[]{:S(2)}, u32[]{:S(2)}) collective-permute-start(f32[256,128]{1,0:T(8,128)S(1)} %get-tuple-element.46.means), channel_id=1, source_target_pairs={{0,8},{4,12},{8,0},{12,4},{16,24},{20,28},{24,16},{28,20},{32,40},... | collective-permute-start | bytes 393224 | tf_op jit(solution)/shard_map/ppermute | solution.py:624
  85.5 5.3 %collective-permute-start.19 = (f32[256,128]{1,0:T(8,128)S(1)}, f32[256,128]{1,0:T(8,128)S(1)}, u32[]{:S(2)}, u32[]{:S(2)}) collective-permute-start(f32[256,128]{1,0:T(8,128)S(1)} %get-tuple-element.46.means), channel_id=1, source_target_pairs={{0,4},{4,0},{8,12},{12,8},{16,20},{20,16},{24,28},{28,24},{32,36},... | collective-permute-start | bytes 393224 | tf_op jit(solution)/shard_map/ppermute | solution.py:624
  (8 other events, 61.8 us)

commit v4 on v3

--- a/solution.py
+++ b/solution.py
@@ -19,6 +19,7 @@
 PAD = 8
 STATE_ROWS = BLOCKS * COLS + 2 * PAD
 SIDE_ROWS = 4 * BLOCKS + 16
+MESSAGE_ROWS = 6 * BLOCKS + 32
 SHARE = 6 * 16 + 8
 SWAP_ROWS = SHARE + 4 * ROWS
 WIDE_ROWS = FIELDS * LEVELS * HALO
@@ -240,7 +241,7 @@
             coef[pl.ds((i * YB + yb) * COLS, COLS), :] = jnp.concatenate(rows, axis=0).T
 
 
-def message_kernel(sc, og, offs, edge1, edge2, ogx, offv, edges, msg_e, msg_o, msg_lo, msg_hi, left, right, ext, joint):
+def message_kernel(sc, og, offs, edge1, edge2, ogx, offv, message, ext, joint):
     mine = sublanes() == lanes() // KA
     even = sc[S_EVEN] == 1
     for i in range(2):
@@ -262,24 +263,18 @@
         down = pltpu.roll(bottom, KA * (7, 4, 5)[yb], 1)
         joint[rows, :] = jnp.where(row < HALO, up, jnp.where(row >= HALO + ROWS, down, og[rows, :]))
         for c in range(4):
-            edges[pl.ds(c * BLOCKS + yb * 16, 16), :] = joint[pl.ds(yb * SHARE + c * 16, 16), :]
+            message[pl.ds(c * BLOCKS + yb * 16, 16), :] = joint[pl.ds(yb * SHARE + c * 16, 16), :]
         for side in range(2):
             ogx[pl.ds(side * BLOCKS + yb * 16, 16), :] = joint[pl.ds(yb * SHARE + 64 + side * 16, 16), :]
     number = sc[S_PB].astype(jnp.float32)
-    for ref, third, opened, fact, off in ((right, 2, 1, 0, 1), (left, 3, 0, 2, 0)):
-        ref[pl.ds(0, 2 * BLOCKS), :] = edges[pl.ds(0, 2 * BLOCKS), :]
-        ref[pl.ds(2 * BLOCKS, BLOCKS), :] = edges[pl.ds(third * BLOCKS, BLOCKS), :]
-        ref[pl.ds(3 * BLOCKS, BLOCKS), :] = ogx[pl.ds(opened * BLOCKS, BLOCKS), :]
-        ref[pl.ds(4 * BLOCKS, 16), :] = jnp.zeros((16, COLS), jnp.float32) + number
+    message[pl.ds(4 * BLOCKS, BLOCKS), :] = ogx[pl.ds(BLOCKS, BLOCKS), :]
+    message[pl.ds(5 * BLOCKS, BLOCKS), :] = ogx[pl.ds(0, BLOCKS), :]
+    message[pl.ds(6 * BLOCKS, 32), :] = jnp.zeros((32, COLS), jnp.float32) + number
+    for at, fact, off in ((6 * BLOCKS, 0, 1), (6 * BLOCKS + 16, 2, 0)):
         for yb in range(YB):
             for i in range(2):
-                ref[pl.ds(4 * BLOCKS + i * YB + yb, 1), :] = joint[pl.ds(yb * SHARE + 96 + fact + i, 1), :]
-        ref[pl.ds(4 * BLOCKS + 2 * YB, YB), :] = offv[pl.ds(off * YB, YB), :]
-    x_even, low = sc[S_XEVEN] == 1, sc[S_LOW] == 1
-    msg_e[...] = jnp.where(x_even, right[...], left[...])
-    msg_o[...] = jnp.where(x_even, left[...], right[...])
-    msg_lo[...] = jnp.where(low, right[...], left[...])
-    msg_hi[...] = jnp.where(low, left[...], right[...])
+                message[pl.ds(at + i * YB + yb, 1), :] = joint[pl.ds(yb * SHARE + 96 + fact + i, 1), :]
+        message[pl.ds(at + 2 * YB, YB), :] = offv[pl.ds(off * YB, YB), :]
 
 
 def coefficients(wet, mix):
@@ -414,7 +409,7 @@
         group(COLS // 8 - 1, False, True)
 
 
-UNROLL = 2
+UNROLL = 7
 TILES = 4
 
 
@@ -424,13 +419,28 @@
         ref[pl.ds(STATE_ROWS - PAD, PAD), :] = jnp.zeros((PAD, COLS), jnp.float32)
 
 
+def fill_sides(sc, side, own, columns, messages):
+    side[pl.ds(REACH * SIDE_ROWS, 2 * BLOCKS), :] = own[pl.ds(0, 2 * BLOCKS), :]
+    for j, (c, m) in enumerate(zip(columns, messages)):
+        slot = sc[S_SLOT + j]
+        east = slot > REACH
+        parts = (
+            (c, 0, 0, 2 * BLOCKS),
+            (c, jnp.where(east, 3 * BLOCKS, 2 * BLOCKS), 2 * BLOCKS, BLOCKS),
+            (m, jnp.where(east, 5 * BLOCKS, 4 * BLOCKS), 3 * BLOCKS, BLOCKS),
+            (m, jnp.where(east, 6 * BLOCKS + 16, 6 * BLOCKS), 4 * BLOCKS, 16),
+        )
+        for ref, start, to, count in parts:
+            at = pl.multiple_of(slot * SIDE_ROWS + to, 8)
+            side[pl.ds(at, count), :] = ref[pl.ds(pl.multiple_of(start, 8), count), :]
+
+
 def first_kernel(
     sc, state, own, ogx, coef, offv, r0, r1, r2, r3, r4, r5, out, edges, side, mid, west0, east0, west1, east1
 ):
     clear_pads(mid, out)
-    side[pl.ds(REACH * SIDE_ROWS, 2 * BLOCKS), :] = own[pl.ds(0, 2 * BLOCKS), :]
-    for j, r in enumerate((r0, r1, r2, r3, r4, r5)):
-        side[pl.ds(pl.multiple_of(sc[S_SLOT + j] * SIDE_ROWS, 8), SIDE_ROWS), :] = r[...]
+    received = (r0, r1, r2, r3, r4, r5)
+    fill_sides(sc, side, own, received, received)
     ghosts(side, ogx, offv, west0, east0, west1, east1)
     substep(state, mid, west0, east0, coef)
     substep(mid, out, west1, east1, coef)
@@ -442,19 +452,12 @@
     out, means, blocks, side, mid, west0, east0, west1, east1, end, nat, sems,
 ):
     clear_pads(mid)
-    side[pl.ds(REACH * SIDE_ROWS, 2 * BLOCKS), :] = own[pl.ds(0, 2 * BLOCKS), :]
-    for j, (r, s) in enumerate(zip((r0, r1, r2, r3, r4, r5), (s0, s1, s2, s3, s4, s5))):
-        slot = sc[S_SLOT + j]
-        at = slot * SIDE_ROWS
-        third = pl.multiple_of(jnp.where(slot > REACH, 3 * BLOCKS, 2 * BLOCKS), 8)
-        side[pl.ds(pl.multiple_of(at, 8), 2 * BLOCKS), :] = s[pl.ds(0, 2 * BLOCKS), :]
-        side[pl.ds(pl.multiple_of(at + 2 * BLOCKS, 8), BLOCKS), :] = s[pl.ds(third, BLOCKS), :]
-        side[pl.ds(pl.multiple_of(at + 3 * BLOCKS, 8), BLOCKS + 16), :] = r[pl.ds(3 * BLOCKS, BLOCKS + 16), :]
+    fill_sides(sc, side, own, (s0, s1, s2, s3, s4, s5), (r0, r1, r2, r3, r4, r5))
     ghosts(side, ogx, offv, west0, east0, west1, east1)
     substep(state, mid, west0, east0, coef)
     substep(mid, end, west1, east1, coef)
     for j in range(3):
-        blocks[pl.ds(j * 8, 8), :] = wide((r0, r1, r2)[j][pl.ds(SIDE_ROWS - 1, 1), :])
+        blocks[pl.ds(j * 8, 8), :] = wide((r0, r1, r2)[j][pl.ds(MESSAGE_ROWS - 1, 1), :])
     share = LEVELS * ROWS
     copies = [
         pltpu.make_async_copy(nat.at[pl.ds(f * share, share)], out.at[pl.ds(f * share, share)], sems.at[f])
@@ -598,10 +601,9 @@
     )
     edge1 = lax.ppermute(swap, "parent", rows_1)
     edge2 = lax.ppermute(swap, "parent", rows_2)
-    side = (SIDE_ROWS, COLS)
-    ogx, offv, edges, msg_e, msg_o, msg_lo, msg_hi = call(
-        message_kernel, [(2 * BLOCKS, COLS), (8, COLS), (4 * BLOCKS, COLS)] + [side] * 4,
-        [side, side, (2 * EXT, COLS), (YB * SHARE, COLS)], sc, og, offs, edge1, edge2,
+    ogx, offv, message = call(
+        message_kernel, [(2 * BLOCKS, COLS), (8, COLS), (MESSAGE_ROWS, COLS)],
+        [(2 * EXT, COLS), (YB * SHARE, COLS)], sc, og, offs, edge1, edge2,
     )
     nest_later, offv = lax.optimization_barrier((nest2, offv))
     state, coef = call(
@@ -609,11 +611,10 @@
         [(2 * EXT, COLS), pltpu.VMEM(narrow, jnp.int32), pltpu.VMEM(narrow, jnp.float32), pltpu.SemaphoreType.DMA((2,))],
         sc, nest_later, wide1, wide2, edge1, edge2, land_mask, mixing, far=(6, 7),
     )
-    msgs = [msg_e, msg_lo, msg_lo, msg_hi, msg_hi, msg_o]
-    first = [lax.ppermute(m, "nest", link) for m, link in zip(msgs, links)]
+    first = [lax.ppermute(message, "nest", link) for link in links]
     work = [(SLOTS * SIDE_ROWS, COLS), state_rows] + [block] * 4
     state, edges = call(
-        first_kernel, [state_rows, (4 * BLOCKS, COLS)], work, sc, state, edges, ogx, coef, offv, *first
+        first_kernel, [state_rows, (4 * BLOCKS, COLS)], work, sc, state, message, ogx, coef, offv, *first
     )
     second = [lax.ppermute(edges, "nest", link) for link in links]
     new2, means, blocks = call(

time: 92.3 us -> 94.4 us (1.023)
  starting transfers between devices: 45.7 us -> 47.8 us
  Pallas kernels: 26.3 us -> 24.8 us
  waiting for transfers between devices: 15.4 us -> 16.8 us
    ppermute x6, starting transfers between devices: 15.2 us -> 17.2 us  [per_device(): second = [lax.ppermute(edges, 'nest', link) for link in links]]
    pallas_call x9, Pallas kernels: 26.3 us -> 24.8 us  [call(): pl.pallas_call(kernel, out_shape=[jax.ShapeDtypeStruct(s, jnp.float32) fo...]
    ppermute x6, waiting for transfers between devices: 1.18 us -> 2.49 us  [per_device(): first = [lax.ppermute(message, 'nest', link) for link in links]]
where the time goes in v4:
time: 94.4 us; the launch traced here: 94.1 us
  starting transfers between devices  47.8 us (51%)
  Pallas kernels  24.8 us (26%)
  waiting for transfers between devices  16.8 us (18%)
  local copies, waits for them, and re-layouts  3.11 us (3%)
  between operations  1.56 us (2%)
    pallas_call x9, Pallas kernels, call(): pl.pallas_call(kernel, out_shape=[jax.ShapeDtypeStruct(s, jnp.float32) fo...  24.8 us
    ppermute x6, starting transfers between devices, per_device(): first = [lax.ppermute(message, 'nest', link) for link in links]  20 us
    ppermute x6, starting transfers between devices, per_device(): second = [lax.ppermute(edges, 'nest', link) for link in links]  17.2 us
    ppermute x6, waiting for transfers between devices, per_device(): second = [lax.ppermute(edges, 'nest', link) for link in links]  4.61 us
    ppermute x3, waiting for transfers between devices, per_device(): arrived = [lax.ppermute(means, 'nest', links[i]) for i in range(3)]  4.44 us
    ppermute x3, starting transfers between devices, per_device(): arrived = [lax.ppermute(means, 'nest', links[i]) for i in range(3)]  4.18 us
    ppermute x3, starting transfers between devices, per_device(): got = [lax.ppermute(coarse, 'nest', links[i]) for i in range(3)]  4.09 us
    ppermute x1, waiting for transfers between devices, per_device(): edge2 = lax.ppermute(swap, 'parent', rows_2)  3.41 us
  transfers between devices with their start and end apart: 22, of which 12 were waited for; matrix products, arithmetic and copies ran while one was open for 0% of the time, Pallas kernels for 9%

profile of v4, /device:TPU:2, one launch (start us, length us, event | category | flops | bytes accessed | tf_op | source)
XLA Modules:
  0.0 94.1 jit_solution(601919294321133598)
XLA Ops:
  1.5 1.6 %copy-done = f32[4,64,16,128]{3,2,1,0:T(8,128)S(1)} copy-done((f32[4,64,16,128]{3,2,1,0:T(8,128)S(1)}, f32[4,64,16,128]{3,2,1,0:T(8,128)}, u32[]{:S(2)}) %copy-start) | copy-done | bytes 2097176
  4.0 1.7 %collective-permute-start.6 = (f32[1024,128]{1,0:T(8,128)S(1)}, f32[1024,128]{1,0:T(8,128)S(1)}, u32[]{:S(2)}, u32[]{:S(2)}) collective-permute-start(f32[1024,128]{1,0:T(8,128)S(1)} %get-tuple-element.29), channel_id=1, source_target_pairs={{0,3},{1,2},{2,1},{3,0},{4,7},{5,6},{6,5},{7,4},{8,11},{9,10},{10,... | collective-permute-start | bytes 1572872 | tf_op jit(solution)/shard_map/ppermute | solution.py:587
  5.7 1.5 %collective-permute-start.2 = (f32[256,128]{1,0:T(8,128)}, f32[256,128]{1,0:T(8,128)S(1)}, u32[]{:S(2)}, u32[]{:S(2)}) collective-permute-start(f32[256,128]{1,0:T(8,128)} %bitcast.33), channel_id=1, source_target_pairs={{0,12},{4,8},{8,4},{12,0},{16,28},{20,24},{24,20},{28,16},{32,44},... | collective-permute-start | bytes 393224 | tf_op jit(solution)/shard_map/ppermute | solution.py:581
  7.2 1.3 %collective-permute-start.1 = (f32[256,128]{1,0:T(8,128)}, f32[256,128]{1,0:T(8,128)S(1)}, u32[]{:S(2)}, u32[]{:S(2)}) collective-permute-start(f32[256,128]{1,0:T(8,128)} %bitcast.34), channel_id=1, source_target_pairs={{0,8},{4,12},{8,0},{12,4},{16,24},{20,28},{24,16},{28,20},{32,40},... | collective-permute-start | bytes 393224 | tf_op jit(solution)/shard_map/ppermute | solution.py:581
  8.6 1.3 %collective-permute-start = (f32[256,128]{1,0:T(8,128)}, f32[256,128]{1,0:T(8,128)S(1)}, u32[]{:S(2)}, u32[]{:S(2)}) collective-permute-start(f32[256,128]{1,0:T(8,128)} %bitcast.35), channel_id=1, source_target_pairs={{0,4},{4,0},{8,12},{12,8},{16,20},{20,16},{24,28},{28,24},{32,36},... | collective-permute-start | bytes 393224 | tf_op jit(solution)/shard_map/ppermute | solution.py:581
  11.2 2.4 %shard_map.96.ends = f32[344,128]{1,0:T(8,128)S(1)} custom-call(f32[4096,128]{1,0:T(8,128)S(1)} %bitcast.31, s32[16,128]{1,0:T(8,128)S(1)} %copy-done.3, f32[16,128]{1,0:T(8,128)S(1)} %copy-done.5), custom_call_target="tpu_custom_call" | custom-call | flops 1000 | bytes 1000 | tf_op jit(solution)/shard_map/pallas_call | solution.py:521
  17.8 3.4 %collective-permute-done.4.edge2 = f32[168,128]{1,0:T(8,128)S(1)} collective-permute-done((f32[168,128]{1,0:T(8,128)S(1)}, f32[168,128]{1,0:T(8,128)S(1)}, u32[]{:S(2)}, u32[]{:S(2)}) %collective-permute-start.4) | collective-permute-done | bytes 86048 | tf_op jit(solution)/shard_map/ppermute | solution.py:603
  21.9 3.6 %collective-permute-start.12 = (f32[320,128]{1,0:T(8,128)S(1)}, f32[320,128]{1,0:T(8,128)S(1)}, u32[]{:S(2)}, u32[]{:S(2)}) collective-permute-start(f32[320,128]{1,0:T(8,128)S(1)} %get-tuple-element.31.own), channel_id=1, source_target_pairs={{12,24},{24,12},{4,16},{16,4},{28,40},{40,28},{20,32},{32,20},{44,... | collective-permute-start | bytes 491528 | tf_op jit(solution)/shard_map/ppermute | solution.py:614
  25.6 6.4 %collective-permute-start.11 = (f32[320,128]{1,0:T(8,128)S(1)}, f32[320,128]{1,0:T(8,128)S(1)}, u32[]{:S(2)}, u32[]{:S(2)}) collective-permute-start(f32[320,128]{1,0:T(8,128)S(1)} %get-tuple-element.31.own), channel_id=1, source_target_pairs={{12,20},{20,12},{8,16},{16,8},{28,36},{36,28},{24,32},{32,24},{44,... | collective-permute-start | bytes 491528 | tf_op jit(solution)/shard_map/ppermute | solution.py:614
  32.0 5.8 %collective-permute-start.10 = (f32[320,128]{1,0:T(8,128)S(1)}, f32[320,128]{1,0:T(8,128)S(1)}, u32[]{:S(2)}, u32[]{:S(2)}) collective-permute-start(f32[320,128]{1,0:T(8,128)S(1)} %get-tuple-element.31.own), channel_id=1, source_target_pairs={{12,16},{16,12},{8,20},{20,8},{28,32},{32,28},{24,36},{36,24},{44,... | collective-permute-start | bytes 491528 | tf_op jit(solution)/shard_map/ppermute | solution.py:614
  39.1 2.8 %collective-permute-start.7 = (f32[320,128]{1,0:T(8,128)S(1)}, f32[320,128]{1,0:T(8,128)S(1)}, u32[]{:S(2)}, u32[]{:S(2)}) collective-permute-start(f32[320,128]{1,0:T(8,128)S(1)} %get-tuple-element.31.own), channel_id=1, source_target_pairs={{0,4},{4,0},{8,12},{12,8},{16,20},{20,16},{24,28},{28,24},{32,36},... | collective-permute-start | bytes 491528 | tf_op jit(solution)/shard_map/ppermute | solution.py:614
  41.9 3.5 %shard_map.100 = (f32[6160,128]{1,0:T(8,128)S(1)}, f32[768,128]{1,0:T(8,128)S(1)}) custom-call(s32[14]{0:T(128)S(1)} %stack.75.sc, f32[4096,128]{1,0:T(8,128)S(1)} %bitcast.32, f32[1024,128]{1,0:T(8,128)S(1)} %collective-permute-done.5.wide1, f32[1024,128]{1,0:T(8,128)S(1)} %collective-permute-done.6.wide2, f32[168,128]{1,0:T(8,128)S(1)} %collective-permute-done.3.edge1, ...), custom_call_target="tpu_custom_call" | custom-call | tf_op jit(solution)/shard_map/pallas_call | solution.py:521
  46.3 1.5 %collective-permute-done.7.r0 = f32[320,128]{1,0:T(8,128)S(1)} collective-permute-done((f32[320,128]{1,0:T(8,128)S(1)}, f32[320,128]{1,0:T(8,128)S(1)}, u32[]{:S(2)}, u32[]{:S(2)}) %collective-permute-start.7) | collective-permute-done | bytes 163872 | tf_op jit(solution)/shard_map/ppermute | solution.py:614
  47.9 5.7 %shard_map.101 = (f32[6160,128]{1,0:T(8,128)S(1)}, f32[192,128]{1,0:T(8,128)S(1)}) custom-call(s32[14]{0:T(128)S(1)} %stack.75.sc, f32[6160,128]{1,0:T(8,128)S(1)} %get-tuple-element.30.state, f32[320,128]{1,0:T(8,128)S(1)} %get-tuple-element.31.own, f32[96,128]{1,0:T(8,128)S(1)} %get-tuple-element.32.ogx, f32[768,128]{1,0:T(8,128)S(1)} %get-tuple-element.33.coef, ...), custom_call_target="tpu_custom_call" | custom-call | tf_op jit(solution)/shard_map/pallas_call | solution.py:521
  53.6 5.9 %collective-permute-start.18 = (f32[192,128]{1,0:T(8,128)S(1)}, f32[192,128]{1,0:T(8,128)S(1)}, u32[]{:S(2)}, u32[]{:S(2)}) collective-permute-start(f32[192,128]{1,0:T(8,128)S(1)} %get-tuple-element.36.own), channel_id=1, source_target_pairs={{12,24},{24,12},{4,16},{16,4},{28,40},{40,28},{20,32},{32,20},{44,... | collective-permute-start | bytes 294920 | tf_op jit(solution)/shard_map/ppermute | solution.py:619
  60.6 5.7 %collective-permute-start.16 = (f32[192,128]{1,0:T(8,128)S(1)}, f32[192,128]{1,0:T(8,128)S(1)}, u32[]{:S(2)}, u32[]{:S(2)}) collective-permute-start(f32[192,128]{1,0:T(8,128)S(1)} %get-tuple-element.36.own), channel_id=1, source_target_pairs={{12,16},{16,12},{8,20},{20,8},{28,32},{32,28},{24,36},{36,24},{44,... | collective-permute-start | bytes 294920 | tf_op jit(solution)/shard_map/ppermute | solution.py:619
  66.3 4.4 %collective-permute-start.14 = (f32[192,128]{1,0:T(8,128)S(1)}, f32[192,128]{1,0:T(8,128)S(1)}, u32[]{:S(2)}, u32[]{:S(2)}) collective-permute-start(f32[192,128]{1,0:T(8,128)S(1)} %get-tuple-element.36.own), channel_id=1, source_target_pairs={{0,8},{4,12},{8,0},{12,4},{16,24},{20,28},{24,16},{28,20},{32,40},... | collective-permute-start | bytes 294920 | tf_op jit(solution)/shard_map/ppermute | solution.py:619
  72.0 1.7 %collective-permute-done.14.s1 = f32[192,128]{1,0:T(8,128)S(1)} collective-permute-done((f32[192,128]{1,0:T(8,128)S(1)}, f32[192,128]{1,0:T(8,128)S(1)}, u32[]{:S(2)}, u32[]{:S(2)}) %collective-permute-start.14) | collective-permute-done | bytes 98336 | tf_op jit(solution)/shard_map/ppermute | solution.py:619
  73.7 1.7 %collective-permute-done.13.s0 = f32[192,128]{1,0:T(8,128)S(1)} collective-permute-done((f32[192,128]{1,0:T(8,128)S(1)}, f32[192,128]{1,0:T(8,128)S(1)}, u32[]{:S(2)}, u32[]{:S(2)}) %collective-permute-start.13) | collective-permute-done | bytes 98336 | tf_op jit(solution)/shard_map/ppermute | solution.py:619
  75.4 8.8 %shard_map.102 = (f32[4096,128]{1,0:T(8,128)}, f32[256,128]{1,0:T(8,128)S(1)}, f32[24,128]{1,0:T(8,128)S(1)}) custom-call(s32[14]{0:T(128)S(1)} %stack.75.sc, f32[6160,128]{1,0:T(8,128)S(1)} %get-tuple-element.35.state, f32[192,128]{1,0:T(8,128)S(1)} %get-tuple-element.36.own, f32[96,128]{1,0:T(8,128)S(1)} %get-tuple-element.32.ogx, ...), custom_call_target="tpu_custom_call" | custom-call | tf_op jit(solution)/shard_map/pallas_call | solution.py:521
  84.4 3.0 %collective-permute-start.20 = (f32[256,128]{1,0:T(8,128)S(1)}, f32[256,128]{1,0:T(8,128)S(1)}, u32[]{:S(2)}, u32[]{:S(2)}) collective-permute-start(f32[256,128]{1,0:T(8,128)S(1)} %get-tuple-element.38.means), channel_id=1, source_target_pairs={{0,8},{4,12},{8,0},{12,4},{16,24},{20,28},{24,16},{28,20},{32,40},... | collective-permute-start | bytes 393224 | tf_op jit(solution)/shard_map/ppermute | solution.py:625
  88.4 1.7 %collective-permute-done.21.got3 = f32[256,128]{1,0:T(8,128)S(1)} collective-permute-done((f32[256,128]{1,0:T(8,128)S(1)}, f32[256,128]{1,0:T(8,128)S(1)}, u32[]{:S(2)}, u32[]{:S(2)}) %collective-permute-start.21) | collective-permute-done | bytes 131104 | tf_op jit(solution)/shard_map/ppermute | solution.py:625
  91.2 1.6 %collective-permute-done.19.got1 = f32[256,128]{1,0:T(8,128)S(1)} collective-permute-done((f32[256,128]{1,0:T(8,128)S(1)}, f32[256,128]{1,0:T(8,128)S(1)}, u32[]{:S(2)}, u32[]{:S(2)}) %collective-permute-start.19) | collective-permute-done | bytes 131104 | tf_op jit(solution)/shard_map/ppermute | solution.py:625
  92.9 1.2 %shard_map.103 = f32[256,128]{1,0:T(8,128)} custom-call(s32[14]{0:T(128)S(1)} %stack.75.sc, f32[256,128]{1,0:T(8,128)S(1)} %get-tuple-element.21.own.coarse, f32[256,128]{1,0:T(8,128)S(1)} %get-tuple-element.38.means, f32[256,128]{1,0:T(8,128)S(1)} %collective-permute-done.19.got1, f32[256,128]{1,0:T(8,128)S(1)} %collective-permute-done.20.got2, ...), custom_call_target="tpu_custom_call" | custom-call | tf_op jit(solution)/shard_map/pallas_call | solution.py:521
  (50 shorter events, 14.0 us)
Async XLA Ops:
  0.6 41.2 %copy-start.4 = (s32[16,128]{1,0:T(8,128)S(1)}, s32[16,128]{1,0:T(8,128)}, u32[]{:S(2)}) copy-start(s32[16,128]{1,0:T(8,128)} %far_mask.1) | copy-start | bytes 24580
  0.7 41.2 %copy-start.6 = (f32[16,128]{1,0:T(8,128)S(1)}, f32[16,128]{1,0:T(8,128)}, u32[]{:S(2)}) copy-start(f32[16,128]{1,0:T(8,128)} %far_mixing.1) | copy-start | bytes 24580
  3.9 34.0 %collective-permute-start.5 = (f32[1024,128]{1,0:T(8,128)S(1)}, f32[1024,128]{1,0:T(8,128)S(1)}, u32[]{:S(2)}, u32[]{:S(2)}) collective-permute-start(f32[1024,128]{1,0:T(8,128)S(1)} %get-tuple-element.28), channel_id=1, source_target_pairs={{0,1},{1,0},{2,3},{3,2},{4,5},{5,4},{6,7},{7,6},{8,9},{9,8},{10,11... | collective-permute-start | bytes 1572872 | tf_op jit(solution)/shard_map/ppermute | solution.py:586
  4.0 35.0 %collective-permute-start.6 = (f32[1024,128]{1,0:T(8,128)S(1)}, f32[1024,128]{1,0:T(8,128)S(1)}, u32[]{:S(2)}, u32[]{:S(2)}) collective-permute-start(f32[1024,128]{1,0:T(8,128)S(1)} %get-tuple-element.29), channel_id=1, source_target_pairs={{0,3},{1,2},{2,1},{3,0},{4,7},{5,6},{6,5},{7,4},{8,11},{9,10},{10,... | collective-permute-start | bytes 1572872 | tf_op jit(solution)/shard_map/ppermute | solution.py:587
  5.7 8.5 %collective-permute-start.2 = (f32[256,128]{1,0:T(8,128)}, f32[256,128]{1,0:T(8,128)S(1)}, u32[]{:S(2)}, u32[]{:S(2)}) collective-permute-start(f32[256,128]{1,0:T(8,128)} %bitcast.33), channel_id=1, source_target_pairs={{0,12},{4,8},{8,4},{12,0},{16,28},{20,24},{24,20},{28,16},{32,44},... | collective-permute-start | bytes 393224 | tf_op jit(solution)/shard_map/ppermute | solution.py:581
  7.2 8.1 %collective-permute-start.1 = (f32[256,128]{1,0:T(8,128)}, f32[256,128]{1,0:T(8,128)S(1)}, u32[]{:S(2)}, u32[]{:S(2)}) collective-permute-start(f32[256,128]{1,0:T(8,128)} %bitcast.34), channel_id=1, source_target_pairs={{0,8},{4,12},{8,0},{12,4},{16,24},{20,28},{24,16},{28,20},{32,40},... | collective-permute-start | bytes 393224 | tf_op jit(solution)/shard_map/ppermute | solution.py:581
  8.6 7.5 %collective-permute-start = (f32[256,128]{1,0:T(8,128)}, f32[256,128]{1,0:T(8,128)S(1)}, u32[]{:S(2)}, u32[]{:S(2)}) collective-permute-start(f32[256,128]{1,0:T(8,128)} %bitcast.35), channel_id=1, source_target_pairs={{0,4},{4,0},{8,12},{12,8},{16,20},{20,16},{24,28},{28,24},{32,36},... | collective-permute-start | bytes 393224 | tf_op jit(solution)/shard_map/ppermute | solution.py:581
  17.1 4.1 %collective-permute-start.4 = (f32[168,128]{1,0:T(8,128)S(1)}, f32[168,128]{1,0:T(8,128)S(1)}, u32[]{:S(2)}, u32[]{:S(2)}) collective-permute-start(f32[168,128]{1,0:T(8,128)S(1)} %get-tuple-element.25), channel_id=1, source_target_pairs={{0,3},{1,2},{2,1},{3,0},{4,7},{5,6},{6,5},{7,4},{8,11},{9,10},{10,... | collective-permute-start | bytes 258056 | tf_op jit(solution)/shard_map/ppermute | solution.py:603
  17.2 4.0 %collective-permute-start.3 = (f32[168,128]{1,0:T(8,128)S(1)}, f32[168,128]{1,0:T(8,128)S(1)}, u32[]{:S(2)}, u32[]{:S(2)}) collective-permute-start(f32[168,128]{1,0:T(8,128)S(1)} %get-tuple-element.25), channel_id=1, source_target_pairs={{0,1},{1,0},{2,3},{3,2},{4,5},{5,4},{6,7},{7,6},{8,9},{9,8},{10,11... | collective-permute-start | bytes 258056 | tf_op jit(solution)/shard_map/ppermute | solution.py:602
  21.9 15.9 %collective-permute-start.12 = (f32[320,128]{1,0:T(8,128)S(1)}, f32[320,128]{1,0:T(8,128)S(1)}, u32[]{:S(2)}, u32[]{:S(2)}) collective-permute-start(f32[320,128]{1,0:T(8,128)S(1)} %get-tuple-element.31.own), channel_id=1, source_target_pairs={{12,24},{24,12},{4,16},{16,4},{28,40},{40,28},{20,32},{32,20},{44,... | collective-permute-start | bytes 491528 | tf_op jit(solution)/shard_map/ppermute | solution.py:614
  25.6 19.8 %collective-permute-start.11 = (f32[320,128]{1,0:T(8,128)S(1)}, f32[320,128]{1,0:T(8,128)S(1)}, u32[]{:S(2)}, u32[]{:S(2)}) collective-permute-start(f32[320,128]{1,0:T(8,128)S(1)} %get-tuple-element.31.own), channel_id=1, source_target_pairs={{12,20},{20,12},{8,16},{16,8},{28,36},{36,28},{24,32},{32,24},{44,... | collective-permute-start | bytes 491528 | tf_op jit(solution)/shard_map/ppermute | solution.py:614
  32.0 14.3 %collective-permute-start.10 = (f32[320,128]{1,0:T(8,128)S(1)}, f32[320,128]{1,0:T(8,128)S(1)}, u32[]{:S(2)}, u32[]{:S(2)}) collective-permute-start(f32[320,128]{1,0:T(8,128)S(1)} %get-tuple-element.31.own), channel_id=1, source_target_pairs={{12,16},{16,12},{8,20},{20,8},{28,32},{32,28},{24,36},{36,24},{44,... | collective-permute-start | bytes 491528 | tf_op jit(solution)/shard_map/ppermute | solution.py:614
  37.8 8.5 %collective-permute-start.9 = (f32[320,128]{1,0:T(8,128)S(1)}, f32[320,128]{1,0:T(8,128)S(1)}, u32[]{:S(2)}, u32[]{:S(2)}) collective-permute-start(f32[320,128]{1,0:T(8,128)S(1)} %get-tuple-element.31.own), channel_id=1, source_target_pairs={{0,12},{4,8},{8,4},{12,0},{16,28},{20,24},{24,20},{28,16},{32,44},... | collective-permute-start | bytes 491528 | tf_op jit(solution)/shard_map/ppermute | solution.py:614
  38.0 8.3 %collective-permute-start.8 = (f32[320,128]{1,0:T(8,128)S(1)}, f32[320,128]{1,0:T(8,128)S(1)}, u32[]{:S(2)}, u32[]{:S(2)}) collective-permute-start(f32[320,128]{1,0:T(8,128)S(1)} %get-tuple-element.31.own), channel_id=1, source_target_pairs={{0,8},{4,12},{8,0},{12,4},{16,24},{20,28},{24,16},{28,20},{32,40},... | collective-permute-start | bytes 491528 | tf_op jit(solution)/shard_map/ppermute | solution.py:614
  39.1 8.8 %collective-permute-start.7 = (f32[320,128]{1,0:T(8,128)S(1)}, f32[320,128]{1,0:T(8,128)S(1)}, u32[]{:S(2)}, u32[]{:S(2)}) collective-permute-start(f32[320,128]{1,0:T(8,128)S(1)} %get-tuple-element.31.own), channel_id=1, source_target_pairs={{0,4},{4,0},{8,12},{12,8},{16,20},{20,16},{24,28},{28,24},{32,36},... | collective-permute-start | bytes 491528 | tf_op jit(solution)/shard_map/ppermute | solution.py:614
  53.6 17.2 %collective-permute-start.18 = (f32[192,128]{1,0:T(8,128)S(1)}, f32[192,128]{1,0:T(8,128)S(1)}, u32[]{:S(2)}, u32[]{:S(2)}) collective-permute-start(f32[192,128]{1,0:T(8,128)S(1)} %get-tuple-element.36.own), channel_id=1, source_target_pairs={{12,24},{24,12},{4,16},{16,4},{28,40},{40,28},{20,32},{32,20},{44,... | collective-permute-start | bytes 294920 | tf_op jit(solution)/shard_map/ppermute | solution.py:619
  59.5 12.0 %collective-permute-start.17 = (f32[192,128]{1,0:T(8,128)S(1)}, f32[192,128]{1,0:T(8,128)S(1)}, u32[]{:S(2)}, u32[]{:S(2)}) collective-permute-start(f32[192,128]{1,0:T(8,128)S(1)} %get-tuple-element.36.own), channel_id=1, source_target_pairs={{12,20},{20,12},{8,16},{16,8},{28,36},{36,28},{24,32},{32,24},{44,... | collective-permute-start | bytes 294920 | tf_op jit(solution)/shard_map/ppermute | solution.py:619
  60.6 10.8 %collective-permute-start.16 = (f32[192,128]{1,0:T(8,128)S(1)}, f32[192,128]{1,0:T(8,128)S(1)}, u32[]{:S(2)}, u32[]{:S(2)}) collective-permute-start(f32[192,128]{1,0:T(8,128)S(1)} %get-tuple-element.36.own), channel_id=1, source_target_pairs={{12,16},{16,12},{8,20},{20,8},{28,32},{32,28},{24,36},{36,24},{44,... | collective-permute-start | bytes 294920 | tf_op jit(solution)/shard_map/ppermute | solution.py:619
  66.3 5.7 %collective-permute-start.15 = (f32[192,128]{1,0:T(8,128)S(1)}, f32[192,128]{1,0:T(8,128)S(1)}, u32[]{:S(2)}, u32[]{:S(2)}) collective-permute-start(f32[192,128]{1,0:T(8,128)S(1)} %get-tuple-element.36.own), channel_id=1, source_target_pairs={{0,12},{4,8},{8,4},{12,0},{16,28},{20,24},{24,20},{28,16},{32,44},... | collective-permute-start | bytes 294920 | tf_op jit(solution)/shard_map/ppermute | solution.py:619
  66.3 7.4 %collective-permute-start.14 = (f32[192,128]{1,0:T(8,128)S(1)}, f32[192,128]{1,0:T(8,128)S(1)}, u32[]{:S(2)}, u32[]{:S(2)}) collective-permute-start(f32[192,128]{1,0:T(8,128)S(1)} %get-tuple-element.36.own), channel_id=1, source_target_pairs={{0,8},{4,12},{8,0},{12,4},{16,24},{20,28},{24,16},{28,20},{32,40},... | collective-permute-start | bytes 294920 | tf_op jit(solution)/shard_map/ppermute | solution.py:619
  70.8 4.6 %collective-permute-start.13 = (f32[192,128]{1,0:T(8,128)S(1)}, f32[192,128]{1,0:T(8,128)S(1)}, u32[]{:S(2)}, u32[]{:S(2)}) collective-permute-start(f32[192,128]{1,0:T(8,128)S(1)} %get-tuple-element.36.own), channel_id=1, source_target_pairs={{0,4},{4,0},{8,12},{12,8},{16,20},{20,16},{24,28},{28,24},{32,36},... | collective-permute-start | bytes 294920 | tf_op jit(solution)/shard_map/ppermute | solution.py:619
  84.2 5.8 %collective-permute-start.21 = (f32[256,128]{1,0:T(8,128)S(1)}, f32[256,128]{1,0:T(8,128)S(1)}, u32[]{:S(2)}, u32[]{:S(2)}) collective-permute-start(f32[256,128]{1,0:T(8,128)S(1)} %get-tuple-element.38.means), channel_id=1, source_target_pairs={{0,12},{4,8},{8,4},{12,0},{16,28},{20,24},{24,20},{28,16},{32,44},... | collective-permute-start | bytes 393224 | tf_op jit(solution)/shard_map/ppermute | solution.py:625
  84.4 6.8 %collective-permute-start.20 = (f32[256,128]{1,0:T(8,128)S(1)}, f32[256,128]{1,0:T(8,128)S(1)}, u32[]{:S(2)}, u32[]{:S(2)}) collective-permute-start(f32[256,128]{1,0:T(8,128)S(1)} %get-tuple-element.38.means), channel_id=1, source_target_pairs={{0,8},{4,12},{8,0},{12,4},{16,24},{20,28},{24,16},{28,20},{32,40},... | collective-permute-start | bytes 393224 | tf_op jit(solution)/shard_map/ppermute | solution.py:625
  87.5 5.4 %collective-permute-start.19 = (f32[256,128]{1,0:T(8,128)S(1)}, f32[256,128]{1,0:T(8,128)S(1)}, u32[]{:S(2)}, u32[]{:S(2)}) collective-permute-start(f32[256,128]{1,0:T(8,128)S(1)} %get-tuple-element.38.means), channel_id=1, source_target_pairs={{0,4},{4,0},{8,12},{12,8},{16,20},{20,16},{24,28},{28,24},{32,36},... | collective-permute-start | bytes 393224 | tf_op jit(solution)/shard_map/ppermute | solution.py:625
  (8 other events, 61.8 us)

commit v5 on v3

--- a/solution.py
+++ b/solution.py
@@ -414,7 +414,7 @@
         group(COLS // 8 - 1, False, True)
 
 
-UNROLL = 2
+UNROLL = 7
 TILES = 4
 
 

time: 92.3 us -> 90.8 us (0.984)
  Pallas kernels: 26.3 us -> 24.8 us
    pallas_call x9, Pallas kernels: 26.3 us -> 24.8 us  [call(): pl.pallas_call(kernel, out_shape=[jax.ShapeDtypeStruct(s, jnp.float32) fo...]
where the time goes in v5:
time: 90.8 us; the launch traced here: 90.6 us
  starting transfers between devices  45.7 us (50%)
  Pallas kernels  24.8 us (27%)
  waiting for transfers between devices  15.4 us (17%)
  local copies, waits for them, and re-layouts  3.11 us (3%)
  between operations  1.59 us (2%)
    pallas_call x9, Pallas kernels, call(): pl.pallas_call(kernel, out_shape=[jax.ShapeDtypeStruct(s, jnp.float32) fo...  24.8 us
    ppermute x6, starting transfers between devices, per_device(): first = [lax.ppermute(m, 'nest', link) for m, link in zip(msgs, links)]  19.8 us
    ppermute x6, starting transfers between devices, per_device(): second = [lax.ppermute(edges, 'nest', link) for link in links]  15.2 us
    ppermute x6, waiting for transfers between devices, per_device(): second = [lax.ppermute(edges, 'nest', link) for link in links]  4.61 us
    ppermute x3, waiting for transfers between devices, per_device(): arrived = [lax.ppermute(means, 'nest', links[i]) for i in range(3)]  4.34 us
    ppermute x3, starting transfers between devices, per_device(): arrived = [lax.ppermute(means, 'nest', links[i]) for i in range(3)]  4.17 us
    ppermute x3, starting transfers between devices, per_device(): got = [lax.ppermute(coarse, 'nest', links[i]) for i in range(3)]  4.09 us
    ppermute x1, waiting for transfers between devices, per_device(): edge2 = lax.ppermute(swap, 'parent', rows_2)  3.41 us
  transfers between devices with their start and end apart: 22, of which 12 were waited for; matrix products, arithmetic and copies ran while one was open for 0% of the time, Pallas kernels for 9%

profile of v5, /device:TPU:2, one launch (start us, length us, event | category | flops | bytes accessed | tf_op | source)
XLA Modules:
  0.0 90.6 jit_solution(4841552390525508192)
XLA Ops:
  1.5 1.6 %copy-done = f32[4,64,16,128]{3,2,1,0:T(8,128)S(1)} copy-done((f32[4,64,16,128]{3,2,1,0:T(8,128)S(1)}, f32[4,64,16,128]{3,2,1,0:T(8,128)}, u32[]{:S(2)}) %copy-start) | copy-done | bytes 2097176
  4.0 1.7 %collective-permute-start.6 = (f32[1024,128]{1,0:T(8,128)S(1)}, f32[1024,128]{1,0:T(8,128)S(1)}, u32[]{:S(2)}, u32[]{:S(2)}) collective-permute-start(f32[1024,128]{1,0:T(8,128)S(1)} %get-tuple-element.33), channel_id=1, source_target_pairs={{0,3},{1,2},{2,1},{3,0},{4,7},{5,6},{6,5},{7,4},{8,11},{9,10},{10,... | collective-permute-start | bytes 1572872 | tf_op jit(solution)/shard_map/ppermute | solution.py:584
  5.7 1.5 %collective-permute-start.2 = (f32[256,128]{1,0:T(8,128)}, f32[256,128]{1,0:T(8,128)S(1)}, u32[]{:S(2)}, u32[]{:S(2)}) collective-permute-start(f32[256,128]{1,0:T(8,128)} %bitcast.33), channel_id=1, source_target_pairs={{0,12},{4,8},{8,4},{12,0},{16,28},{20,24},{24,20},{28,16},{32,44},... | collective-permute-start | bytes 393224 | tf_op jit(solution)/shard_map/ppermute | solution.py:578
  7.2 1.3 %collective-permute-start.1 = (f32[256,128]{1,0:T(8,128)}, f32[256,128]{1,0:T(8,128)S(1)}, u32[]{:S(2)}, u32[]{:S(2)}) collective-permute-start(f32[256,128]{1,0:T(8,128)} %bitcast.34), channel_id=1, source_target_pairs={{0,8},{4,12},{8,0},{12,4},{16,24},{20,28},{24,16},{28,20},{32,40},... | collective-permute-start | bytes 393224 | tf_op jit(solution)/shard_map/ppermute | solution.py:578
  8.6 1.3 %collective-permute-start = (f32[256,128]{1,0:T(8,128)}, f32[256,128]{1,0:T(8,128)S(1)}, u32[]{:S(2)}, u32[]{:S(2)}) collective-permute-start(f32[256,128]{1,0:T(8,128)} %bitcast.35), channel_id=1, source_target_pairs={{0,4},{4,0},{8,12},{12,8},{16,20},{20,16},{24,28},{28,24},{32,36},... | collective-permute-start | bytes 393224 | tf_op jit(solution)/shard_map/ppermute | solution.py:578
  11.2 2.4 %shard_map.96.ends = f32[344,128]{1,0:T(8,128)S(1)} custom-call(f32[4096,128]{1,0:T(8,128)S(1)} %bitcast.31, s32[16,128]{1,0:T(8,128)S(1)} %copy-done.3, f32[16,128]{1,0:T(8,128)S(1)} %copy-done.5), custom_call_target="tpu_custom_call" | custom-call | flops 1000 | bytes 1000 | tf_op jit(solution)/shard_map/pallas_call | solution.py:518
  17.8 3.4 %collective-permute-done.4.edge2 = f32[168,128]{1,0:T(8,128)S(1)} collective-permute-done((f32[168,128]{1,0:T(8,128)S(1)}, f32[168,128]{1,0:T(8,128)S(1)}, u32[]{:S(2)}, u32[]{:S(2)}) %collective-permute-start.4) | collective-permute-done | bytes 86048 | tf_op jit(solution)/shard_map/ppermute | solution.py:600
  21.9 1.8 %collective-permute-start.7 = (f32[208,128]{1,0:T(8,128)S(1)}, f32[208,128]{1,0:T(8,128)S(1)}, u32[]{:S(2)}, u32[]{:S(2)}) collective-permute-start(f32[208,128]{1,0:T(8,128)S(1)} %get-tuple-element.39), channel_id=1, source_target_pairs={{0,4},{4,0},{8,12},{12,8},{16,20},{20,16},{24,28},{28,24},{32,36},... | collective-permute-start | bytes 319496 | tf_op jit(solution)/shard_map/ppermute | solution.py:613
  24.7 1.4 %collective-permute-start.8 = (f32[208,128]{1,0:T(8,128)S(1)}, f32[208,128]{1,0:T(8,128)S(1)}, u32[]{:S(2)}, u32[]{:S(2)}) collective-permute-start(f32[208,128]{1,0:T(8,128)S(1)} %get-tuple-element.40), channel_id=1, source_target_pairs={{0,8},{4,12},{8,0},{12,4},{16,24},{20,28},{24,16},{28,20},{32,40},... | collective-permute-start | bytes 319496 | tf_op jit(solution)/shard_map/ppermute | solution.py:613
  27.0 3.5 %collective-permute-start.12 = (f32[208,128]{1,0:T(8,128)S(1)}, f32[208,128]{1,0:T(8,128)S(1)}, u32[]{:S(2)}, u32[]{:S(2)}) collective-permute-start(f32[208,128]{1,0:T(8,128)S(1)} %get-tuple-element.42), channel_id=1, source_target_pairs={{12,24},{24,12},{4,16},{16,4},{28,40},{40,28},{20,32},{32,20},{44,... | collective-permute-start | bytes 319496 | tf_op jit(solution)/shard_map/ppermute | solution.py:613
  30.5 6.4 %collective-permute-start.11 = (f32[208,128]{1,0:T(8,128)S(1)}, f32[208,128]{1,0:T(8,128)S(1)}, u32[]{:S(2)}, u32[]{:S(2)}) collective-permute-start(f32[208,128]{1,0:T(8,128)S(1)} %get-tuple-element.41), channel_id=1, source_target_pairs={{12,20},{20,12},{8,16},{16,8},{28,36},{36,28},{24,32},{32,24},{44,... | collective-permute-start | bytes 319496 | tf_op jit(solution)/shard_map/ppermute | solution.py:613
  36.9 5.7 %collective-permute-start.10 = (f32[208,128]{1,0:T(8,128)S(1)}, f32[208,128]{1,0:T(8,128)S(1)}, u32[]{:S(2)}, u32[]{:S(2)}) collective-permute-start(f32[208,128]{1,0:T(8,128)S(1)} %get-tuple-element.41), channel_id=1, source_target_pairs={{12,16},{16,12},{8,20},{20,8},{28,32},{32,28},{24,36},{36,24},{44,... | collective-permute-start | bytes 319496 | tf_op jit(solution)/shard_map/ppermute | solution.py:613
  42.6 3.5 %shard_map.100 = (f32[6160,128]{1,0:T(8,128)S(1)}, f32[768,128]{1,0:T(8,128)S(1)}) custom-call(s32[14]{0:T(128)S(1)} %stack.75.sc, f32[4096,128]{1,0:T(8,128)S(1)} %bitcast.32, f32[1024,128]{1,0:T(8,128)S(1)} %collective-permute-done.5.wide1, f32[1024,128]{1,0:T(8,128)S(1)} %collective-permute-done.6.wide2, f32[168,128]{1,0:T(8,128)S(1)} %collective-permute-done.3.edge1, ...), custom_call_target="tpu_custom_call" | custom-call | tf_op jit(solution)/shard_map/pallas_call | solution.py:518
  46.4 5.7 %shard_map.101 = (f32[6160,128]{1,0:T(8,128)S(1)}, f32[192,128]{1,0:T(8,128)S(1)}) custom-call(s32[14]{0:T(128)S(1)} %stack.75.sc, f32[6160,128]{1,0:T(8,128)S(1)} %get-tuple-element.34.state, f32[192,128]{1,0:T(8,128)S(1)} %get-tuple-element.35.own, f32[96,128]{1,0:T(8,128)S(1)} %get-tuple-element.36.ogx, f32[768,128]{1,0:T(8,128)S(1)} %get-tuple-element.37.coef, ...), custom_call_target="tpu_custom_call" | custom-call | tf_op jit(solution)/shard_map/pallas_call | solution.py:518
  52.1 3.9 %collective-permute-start.18 = (f32[192,128]{1,0:T(8,128)S(1)}, f32[192,128]{1,0:T(8,128)S(1)}, u32[]{:S(2)}, u32[]{:S(2)}) collective-permute-start(f32[192,128]{1,0:T(8,128)S(1)} %get-tuple-element.44.own), channel_id=1, source_target_pairs={{12,24},{24,12},{4,16},{16,4},{28,40},{40,28},{20,32},{32,20},{44,... | collective-permute-start | bytes 294920 | tf_op jit(solution)/shard_map/ppermute | solution.py:618
  56.1 1.8 %collective-permute-start.17 = (f32[192,128]{1,0:T(8,128)S(1)}, f32[192,128]{1,0:T(8,128)S(1)}, u32[]{:S(2)}, u32[]{:S(2)}) collective-permute-start(f32[192,128]{1,0:T(8,128)S(1)} %get-tuple-element.44.own), channel_id=1, source_target_pairs={{12,20},{20,12},{8,16},{16,8},{28,36},{36,28},{24,32},{32,24},{44,... | collective-permute-start | bytes 294920 | tf_op jit(solution)/shard_map/ppermute | solution.py:618
  57.9 4.1 %collective-permute-start.16 = (f32[192,128]{1,0:T(8,128)S(1)}, f32[192,128]{1,0:T(8,128)S(1)}, u32[]{:S(2)}, u32[]{:S(2)}) collective-permute-start(f32[192,128]{1,0:T(8,128)S(1)} %get-tuple-element.44.own), channel_id=1, source_target_pairs={{12,16},{16,12},{8,20},{20,8},{28,32},{32,28},{24,36},{36,24},{44,... | collective-permute-start | bytes 294920 | tf_op jit(solution)/shard_map/ppermute | solution.py:618
  62.0 5.4 %collective-permute-start.14 = (f32[192,128]{1,0:T(8,128)S(1)}, f32[192,128]{1,0:T(8,128)S(1)}, u32[]{:S(2)}, u32[]{:S(2)}) collective-permute-start(f32[192,128]{1,0:T(8,128)S(1)} %get-tuple-element.44.own), channel_id=1, source_target_pairs={{0,8},{4,12},{8,0},{12,4},{16,24},{20,28},{24,16},{28,20},{32,40},... | collective-permute-start | bytes 294920 | tf_op jit(solution)/shard_map/ppermute | solution.py:618
  68.0 1.9 %collective-permute-done.14.s1 = f32[192,128]{1,0:T(8,128)S(1)} collective-permute-done((f32[192,128]{1,0:T(8,128)S(1)}, f32[192,128]{1,0:T(8,128)S(1)}, u32[]{:S(2)}, u32[]{:S(2)}) %collective-permute-start.14) | collective-permute-done | bytes 98336 | tf_op jit(solution)/shard_map/ppermute | solution.py:618
  69.9 2.0 %collective-permute-done.13.s0 = f32[192,128]{1,0:T(8,128)S(1)} collective-permute-done((f32[192,128]{1,0:T(8,128)S(1)}, f32[192,128]{1,0:T(8,128)S(1)}, u32[]{:S(2)}, u32[]{:S(2)}) %collective-permute-start.13) | collective-permute-done | bytes 98336 | tf_op jit(solution)/shard_map/ppermute | solution.py:618
  72.0 8.8 %shard_map.102 = (f32[4096,128]{1,0:T(8,128)}, f32[256,128]{1,0:T(8,128)S(1)}, f32[24,128]{1,0:T(8,128)S(1)}) custom-call(s32[14]{0:T(128)S(1)} %stack.75.sc, f32[6160,128]{1,0:T(8,128)S(1)} %get-tuple-element.43.state, f32[192,128]{1,0:T(8,128)S(1)} %get-tuple-element.44.own, f32[96,128]{1,0:T(8,128)S(1)} %get-tuple-element.36.ogx, ...), custom_call_target="tpu_custom_call" | custom-call | tf_op jit(solution)/shard_map/pallas_call | solution.py:518
  80.9 3.1 %collective-permute-start.20 = (f32[256,128]{1,0:T(8,128)S(1)}, f32[256,128]{1,0:T(8,128)S(1)}, u32[]{:S(2)}, u32[]{:S(2)}) collective-permute-start(f32[256,128]{1,0:T(8,128)S(1)} %get-tuple-element.46.means), channel_id=1, source_target_pairs={{0,8},{4,12},{8,0},{12,4},{16,24},{20,28},{24,16},{28,20},{32,40},... | collective-permute-start | bytes 393224 | tf_op jit(solution)/shard_map/ppermute | solution.py:624
  85.9 1.6 %collective-permute-done.20.got2 = f32[256,128]{1,0:T(8,128)S(1)} collective-permute-done((f32[256,128]{1,0:T(8,128)S(1)}, f32[256,128]{1,0:T(8,128)S(1)}, u32[]{:S(2)}, u32[]{:S(2)}) %collective-permute-start.20) | collective-permute-done | bytes 131104 | tf_op jit(solution)/shard_map/ppermute | solution.py:624
  87.5 1.9 %collective-permute-done.19.got1 = f32[256,128]{1,0:T(8,128)S(1)} collective-permute-done((f32[256,128]{1,0:T(8,128)S(1)}, f32[256,128]{1,0:T(8,128)S(1)}, u32[]{:S(2)}, u32[]{:S(2)}) %collective-permute-start.19) | collective-permute-done | bytes 131104 | tf_op jit(solution)/shard_map/ppermute | solution.py:624
  (50 shorter events, 13.2 us)
Async XLA Ops:
  0.6 41.9 %copy-start.4 = (s32[16,128]{1,0:T(8,128)S(1)}, s32[16,128]{1,0:T(8,128)}, u32[]{:S(2)}) copy-start(s32[16,128]{1,0:T(8,128)} %far_mask.1) | copy-start | bytes 24580
  0.7 41.9 %copy-start.6 = (f32[16,128]{1,0:T(8,128)S(1)}, f32[16,128]{1,0:T(8,128)}, u32[]{:S(2)}) copy-start(f32[16,128]{1,0:T(8,128)} %far_mixing.1) | copy-start | bytes 24580
  3.9 26.5 %collective-permute-start.5 = (f32[1024,128]{1,0:T(8,128)S(1)}, f32[1024,128]{1,0:T(8,128)S(1)}, u32[]{:S(2)}, u32[]{:S(2)}) collective-permute-start(f32[1024,128]{1,0:T(8,128)S(1)} %get-tuple-element.32), channel_id=1, source_target_pairs={{0,1},{1,0},{2,3},{3,2},{4,5},{5,4},{6,7},{7,6},{8,9},{9,8},{10,11... | collective-permute-start | bytes 1572872 | tf_op jit(solution)/shard_map/ppermute | solution.py:583
  4.0 32.9 %collective-permute-start.6 = (f32[1024,128]{1,0:T(8,128)S(1)}, f32[1024,128]{1,0:T(8,128)S(1)}, u32[]{:S(2)}, u32[]{:S(2)}) collective-permute-start(f32[1024,128]{1,0:T(8,128)S(1)} %get-tuple-element.33), channel_id=1, source_target_pairs={{0,3},{1,2},{2,1},{3,0},{4,7},{5,6},{6,5},{7,4},{8,11},{9,10},{10,... | collective-permute-start | bytes 1572872 | tf_op jit(solution)/shard_map/ppermute | solution.py:584
  5.7 8.5 %collective-permute-start.2 = (f32[256,128]{1,0:T(8,128)}, f32[256,128]{1,0:T(8,128)S(1)}, u32[]{:S(2)}, u32[]{:S(2)}) collective-permute-start(f32[256,128]{1,0:T(8,128)} %bitcast.33), channel_id=1, source_target_pairs={{0,12},{4,8},{8,4},{12,0},{16,28},{20,24},{24,20},{28,16},{32,44},... | collective-permute-start | bytes 393224 | tf_op jit(solution)/shard_map/ppermute | solution.py:578
  7.2 8.1 %collective-permute-start.1 = (f32[256,128]{1,0:T(8,128)}, f32[256,128]{1,0:T(8,128)S(1)}, u32[]{:S(2)}, u32[]{:S(2)}) collective-permute-start(f32[256,128]{1,0:T(8,128)} %bitcast.34), channel_id=1, source_target_pairs={{0,8},{4,12},{8,0},{12,4},{16,24},{20,28},{24,16},{28,20},{32,40},... | collective-permute-start | bytes 393224 | tf_op jit(solution)/shard_map/ppermute | solution.py:578
  8.6 7.5 %collective-permute-start = (f32[256,128]{1,0:T(8,128)}, f32[256,128]{1,0:T(8,128)S(1)}, u32[]{:S(2)}, u32[]{:S(2)}) collective-permute-start(f32[256,128]{1,0:T(8,128)} %bitcast.35), channel_id=1, source_target_pairs={{0,4},{4,0},{8,12},{12,8},{16,20},{20,16},{24,28},{28,24},{32,36},... | collective-permute-start | bytes 393224 | tf_op jit(solution)/shard_map/ppermute | solution.py:578
  17.2 4.1 %collective-permute-start.4 = (f32[168,128]{1,0:T(8,128)S(1)}, f32[168,128]{1,0:T(8,128)S(1)}, u32[]{:S(2)}, u32[]{:S(2)}) collective-permute-start(f32[168,128]{1,0:T(8,128)S(1)} %get-tuple-element.29), channel_id=1, source_target_pairs={{0,3},{1,2},{2,1},{3,0},{4,7},{5,6},{6,5},{7,4},{8,11},{9,10},{10,... | collective-permute-start | bytes 258056 | tf_op jit(solution)/shard_map/ppermute | solution.py:600
  17.2 4.0 %collective-permute-start.3 = (f32[168,128]{1,0:T(8,128)S(1)}, f32[168,128]{1,0:T(8,128)S(1)}, u32[]{:S(2)}, u32[]{:S(2)}) collective-permute-start(f32[168,128]{1,0:T(8,128)S(1)} %get-tuple-element.29), channel_id=1, source_target_pairs={{0,1},{1,0},{2,3},{3,2},{4,5},{5,4},{6,7},{7,6},{8,9},{9,8},{10,11... | collective-permute-start | bytes 258056 | tf_op jit(solution)/shard_map/ppermute | solution.py:599
  21.9 5.0 %collective-permute-start.7 = (f32[208,128]{1,0:T(8,128)S(1)}, f32[208,128]{1,0:T(8,128)S(1)}, u32[]{:S(2)}, u32[]{:S(2)}) collective-permute-start(f32[208,128]{1,0:T(8,128)S(1)} %get-tuple-element.39), channel_id=1, source_target_pairs={{0,4},{4,0},{8,12},{12,8},{16,20},{20,16},{24,28},{28,24},{32,36},... | collective-permute-start | bytes 319496 | tf_op jit(solution)/shard_map/ppermute | solution.py:613
  23.7 22.3 %collective-permute-start.9 = (f32[208,128]{1,0:T(8,128)S(1)}, f32[208,128]{1,0:T(8,128)S(1)}, u32[]{:S(2)}, u32[]{:S(2)}) collective-permute-start(f32[208,128]{1,0:T(8,128)S(1)} %get-tuple-element.40), channel_id=1, source_target_pairs={{0,12},{4,8},{8,4},{12,0},{16,28},{20,24},{24,20},{28,16},{32,44},... | collective-permute-start | bytes 319496 | tf_op jit(solution)/shard_map/ppermute | solution.py:613
  24.7 21.4 %collective-permute-start.8 = (f32[208,128]{1,0:T(8,128)S(1)}, f32[208,128]{1,0:T(8,128)S(1)}, u32[]{:S(2)}, u32[]{:S(2)}) collective-permute-start(f32[208,128]{1,0:T(8,128)S(1)} %get-tuple-element.40), channel_id=1, source_target_pairs={{0,8},{4,12},{8,0},{12,4},{16,24},{20,28},{24,16},{28,20},{32,40},... | collective-permute-start | bytes 319496 | tf_op jit(solution)/shard_map/ppermute | solution.py:613
  27.0 19.1 %collective-permute-start.12 = (f32[208,128]{1,0:T(8,128)S(1)}, f32[208,128]{1,0:T(8,128)S(1)}, u32[]{:S(2)}, u32[]{:S(2)}) collective-permute-start(f32[208,128]{1,0:T(8,128)S(1)} %get-tuple-element.42), channel_id=1, source_target_pairs={{12,24},{24,12},{4,16},{16,4},{28,40},{40,28},{20,32},{32,20},{44,... | collective-permute-start | bytes 319496 | tf_op jit(solution)/shard_map/ppermute | solution.py:613
  30.5 15.6 %collective-permute-start.11 = (f32[208,128]{1,0:T(8,128)S(1)}, f32[208,128]{1,0:T(8,128)S(1)}, u32[]{:S(2)}, u32[]{:S(2)}) collective-permute-start(f32[208,128]{1,0:T(8,128)S(1)} %get-tuple-element.41), channel_id=1, source_target_pairs={{12,20},{20,12},{8,16},{16,8},{28,36},{36,28},{24,32},{32,24},{44,... | collective-permute-start | bytes 319496 | tf_op jit(solution)/shard_map/ppermute | solution.py:613
  36.9 9.5 %collective-permute-start.10 = (f32[208,128]{1,0:T(8,128)S(1)}, f32[208,128]{1,0:T(8,128)S(1)}, u32[]{:S(2)}, u32[]{:S(2)}) collective-permute-start(f32[208,128]{1,0:T(8,128)S(1)} %get-tuple-element.41), channel_id=1, source_target_pairs={{12,16},{16,12},{8,20},{20,8},{28,32},{32,28},{24,36},{36,24},{44,... | collective-permute-start | bytes 319496 | tf_op jit(solution)/shard_map/ppermute | solution.py:613
  52.1 15.2 %collective-permute-start.18 = (f32[192,128]{1,0:T(8,128)S(1)}, f32[192,128]{1,0:T(8,128)S(1)}, u32[]{:S(2)}, u32[]{:S(2)}) collective-permute-start(f32[192,128]{1,0:T(8,128)S(1)} %get-tuple-element.44.own), channel_id=1, source_target_pairs={{12,24},{24,12},{4,16},{16,4},{28,40},{40,28},{20,32},{32,20},{44,... | collective-permute-start | bytes 294920 | tf_op jit(solution)/shard_map/ppermute | solution.py:618
  56.1 11.5 %collective-permute-start.17 = (f32[192,128]{1,0:T(8,128)S(1)}, f32[192,128]{1,0:T(8,128)S(1)}, u32[]{:S(2)}, u32[]{:S(2)}) collective-permute-start(f32[192,128]{1,0:T(8,128)S(1)} %get-tuple-element.44.own), channel_id=1, source_target_pairs={{12,20},{20,12},{8,16},{16,8},{28,36},{36,28},{24,32},{32,24},{44,... | collective-permute-start | bytes 294920 | tf_op jit(solution)/shard_map/ppermute | solution.py:618
  57.9 10.2 %collective-permute-start.16 = (f32[192,128]{1,0:T(8,128)S(1)}, f32[192,128]{1,0:T(8,128)S(1)}, u32[]{:S(2)}, u32[]{:S(2)}) collective-permute-start(f32[192,128]{1,0:T(8,128)S(1)} %get-tuple-element.44.own), channel_id=1, source_target_pairs={{12,16},{16,12},{8,20},{20,8},{28,32},{32,28},{24,36},{36,24},{44,... | collective-permute-start | bytes 294920 | tf_op jit(solution)/shard_map/ppermute | solution.py:618
  62.0 6.1 %collective-permute-start.15 = (f32[192,128]{1,0:T(8,128)S(1)}, f32[192,128]{1,0:T(8,128)S(1)}, u32[]{:S(2)}, u32[]{:S(2)}) collective-permute-start(f32[192,128]{1,0:T(8,128)S(1)} %get-tuple-element.44.own), channel_id=1, source_target_pairs={{0,12},{4,8},{8,4},{12,0},{16,28},{20,24},{24,20},{28,16},{32,44},... | collective-permute-start | bytes 294920 | tf_op jit(solution)/shard_map/ppermute | solution.py:618
  62.0 8.0 %collective-permute-start.14 = (f32[192,128]{1,0:T(8,128)S(1)}, f32[192,128]{1,0:T(8,128)S(1)}, u32[]{:S(2)}, u32[]{:S(2)}) collective-permute-start(f32[192,128]{1,0:T(8,128)S(1)} %get-tuple-element.44.own), channel_id=1, source_target_pairs={{0,8},{4,12},{8,0},{12,4},{16,24},{20,28},{24,16},{28,20},{32,40},... | collective-permute-start | bytes 294920 | tf_op jit(solution)/shard_map/ppermute | solution.py:618
  67.3 4.6 %collective-permute-start.13 = (f32[192,128]{1,0:T(8,128)S(1)}, f32[192,128]{1,0:T(8,128)S(1)}, u32[]{:S(2)}, u32[]{:S(2)}) collective-permute-start(f32[192,128]{1,0:T(8,128)S(1)} %get-tuple-element.44.own), channel_id=1, source_target_pairs={{0,4},{4,0},{8,12},{12,8},{16,20},{20,16},{24,28},{28,24},{32,36},... | collective-permute-start | bytes 294920 | tf_op jit(solution)/shard_map/ppermute | solution.py:618
  80.8 5.1 %collective-permute-start.21 = (f32[256,128]{1,0:T(8,128)S(1)}, f32[256,128]{1,0:T(8,128)S(1)}, u32[]{:S(2)}, u32[]{:S(2)}) collective-permute-start(f32[256,128]{1,0:T(8,128)S(1)} %get-tuple-element.46.means), channel_id=1, source_target_pairs={{0,12},{4,8},{8,4},{12,0},{16,28},{20,24},{24,20},{28,16},{32,44},... | collective-permute-start | bytes 393224 | tf_op jit(solution)/shard_map/ppermute | solution.py:624
  80.9 6.6 %collective-permute-start.20 = (f32[256,128]{1,0:T(8,128)S(1)}, f32[256,128]{1,0:T(8,128)S(1)}, u32[]{:S(2)}, u32[]{:S(2)}) collective-permute-start(f32[256,128]{1,0:T(8,128)S(1)} %get-tuple-element.46.means), channel_id=1, source_target_pairs={{0,8},{4,12},{8,0},{12,4},{16,24},{20,28},{24,16},{28,20},{32,40},... | collective-permute-start | bytes 393224 | tf_op jit(solution)/shard_map/ppermute | solution.py:624
  84.0 5.3 %collective-permute-start.19 = (f32[256,128]{1,0:T(8,128)S(1)}, f32[256,128]{1,0:T(8,128)S(1)}, u32[]{:S(2)}, u32[]{:S(2)}) collective-permute-start(f32[256,128]{1,0:T(8,128)S(1)} %get-tuple-element.46.means), channel_id=1, source_target_pairs={{0,4},{4,0},{8,12},{12,8},{16,20},{20,16},{24,28},{28,24},{32,36},... | collective-permute-start | bytes 393224 | tf_op jit(solution)/shard_map/ppermute | solution.py:624
  (8 other events, 61.8 us)
